TPU v7x, 256 devices: a whole 4x4x8 slice. The times are simulated.
256 devices in a mesh: grp: 2 (over core), ep: 128 (over x, y, z).
Axes of the slice: x: 4, y: 4, z: 8, core: 2. Of those that a mesh axis runs over, the one named last changes fastest.
Arguments:
- tokens: float32 [4096, 6144], P('ep'), may hold values from -6 to 6
- route_ids: int32 [4096, 12], P('ep'), may hold values from 0 to 767, as said below
- route_weights: float32 [4096, 12], P('ep'), may hold values from 0.05 to 1
- expert_rows: float32 [512, 96, 6144], P(('grp', 'ep')), may hold values from -6 to 6
Outputs:
- combined: float32 [4096, 6144], P('ep', 'grp')
Inputs may be any that keep to these rules, and one draw needn't show every extreme that they name: `route_ids`: each row names 12 different experts. Each routed expert is chosen by at most 96 tokens in all, and by at most 1 of the 32 tokens of one ep index; some routed expert reaches each of these bounds in every draw. Values 512 and above are identity experts.
All inputs are finite; a program needn't handle non-finite values.
Results may differ from a plain program's by a relative error of at most 0.00002.
Values sent between devices are 32-bit elements; how exact they have to be, the bound alone decides.
No kernel may reach another device: no remote copies, remote signals or barrier semaphores. Data moves between devices by JAX's collectives and lax.ppermute only.
A program may use at most 64 MiB of HBM per device.

v0:
```python
import jax
import jax.numpy as jnp
from jax import lax
from jax.sharding import Mesh
from jax.sharding import PartitionSpec as P

EP = ("ep_0", "ep_1", "ep_2")
GRP_EP = ("grp", "ep_0", "ep_1", "ep_2")


def laid_out(parts, dim):
    parts = jnp.moveaxis(parts, 0, dim)
    shape = parts.shape
    return parts.reshape(*shape[:dim], shape[dim] * shape[dim + 1], *shape[dim + 2 :])


def stacked_from(array, axes, turns):
    parts = array[None]
    for k in turns:
        parts = lax.all_gather(parts, axes[k], axis=0, tiled=True)
    carried = [lax.axis_size(axes[k]) for k in reversed(turns)]
    parts = parts.reshape(*carried, *array.shape)
    turned = sorted(range(len(turns)), key=lambda place: turns[len(turns) - 1 - place])
    return parts.transpose(*turned, *range(len(turns), parts.ndim)).reshape(-1, *array.shape)


def whole_of(array, axes, turns, dim):
    return laid_out(stacked_from(array, axes, turns), dim)


def from_everyone(array, axis):
    length = lax.axis_size(axis)
    return lax.all_to_all(
        jnp.broadcast_to(array[None], (length, *array.shape)), axis, 0, 0, tiled=True
    )


def taken_together(array, axis):
    return from_everyone(array, axis).sum(axis=0)


def shards(tokens, route_ids, route_weights, expert_rows):
    groups = lax.axis_size("grp")
    ep_count = lax.axis_size(EP)
    group_index = lax.axis_index("grp")
    ep_index = lax.axis_index(EP)
    exp_dev, capacity, width = expert_rows.shape
    tok_dev, top = route_ids.shape
    experts = exp_dev * groups * ep_count
    per_group = experts // groups
    ident_per_group = experts // 2 // groups
    slots = (capacity + ep_count - 1) // ep_count
    block_width = 128 * max(1, width // 1024)
    block_count = width // block_width
    all_ids = whole_of(route_ids, EP, (0, 1, 2), 0)
    first = (group_index * ep_count + ep_index) * exp_dev
    owned = first + jnp.arange(exp_dev, dtype=jnp.int32)
    hits = (all_ids[:, :, None] == owned[None, None, :]).astype(jnp.int32).sum(1)
    global_rank = jnp.cumsum(hits, axis=0) - hits
    hit_blocks = hits.reshape(ep_count, tok_dev, exp_dev)
    within = jnp.cumsum(hit_blocks, axis=1) - hit_blocks
    rank_blocks = global_rank.reshape(ep_count, tok_dev, exp_dev)
    places = jnp.arange(slots, dtype=jnp.int32)
    selector = hit_blocks[..., None] * (within[..., None] == places).astype(jnp.int32)
    table = jnp.sum(selector * rank_blocks[..., None], axis=1)
    table = jnp.minimum(table, capacity - 1)
    picked = expert_rows[jnp.arange(exp_dev, dtype=jnp.int32)[None, :, None], table]
    outgoing = picked.reshape(ep_count, exp_dev * slots, block_count, block_width)
    real = route_ids < experts
    group = jnp.where(real, route_ids // per_group, (route_ids - experts) // ident_per_group)
    in_group = group == group_index
    same = (route_ids[:, :, None, None] == route_ids[None, None, :, :]).astype(jnp.int32)
    positions = jnp.arange(tok_dev, dtype=jnp.int32)
    earlier = (positions[None, None, :, None] < positions[:, None, None, None]).astype(jnp.int32)
    seen = jnp.sum(same * earlier, axis=(2, 3))
    source = route_ids % per_group // exp_dev
    local = route_ids % exp_dev
    flat_index = source * (exp_dev * slots) + local * slots + seen
    routed_here = real & in_group
    flat_index = jnp.where(routed_here, flat_index, 0)
    routed_weight = jnp.where(routed_here, route_weights, jnp.zeros_like(route_weights))
    piece = lax.all_to_all(outgoing, EP, split_axis=0, concat_axis=0, tiled=True)
    rows = piece.reshape(ep_count * exp_dev * slots, piece.shape[2], piece.shape[3])
    total = jnp.zeros((tok_dev, piece.shape[2], piece.shape[3]), jnp.float32)
    for slot in range(top):
        total = total + routed_weight[:, slot][:, None, None] * rows[flat_index[:, slot]]
    partial_value = total.reshape(tok_dev, width)
    half = width // groups
    everything = taken_together(partial_value, "grp")
    merged = lax.dynamic_slice_in_dim(everything, group_index * half, half, 1)
    ident_weight = jnp.sum(jnp.where(~real, route_weights, jnp.zeros_like(route_weights)), axis=1)
    own_half = lax.dynamic_slice_in_dim(tokens, group_index * half, half, 1)
    merged = merged + ident_weight[:, None] * own_half
    return merged


def solution(mesh):
    torus = Mesh(mesh.devices.reshape(mesh.shape["grp"], 4, 4, 8), ("grp", "ep_0", "ep_1", "ep_2"))
    in_specs = (P(EP, None), P(EP, None), P(EP, None), P(GRP_EP, None, None))
    out_specs = P(EP, "grp")
    return jax.shard_map(
        shards, mesh=torus, in_specs=in_specs, out_specs=out_specs, check_vma=False
    )
```

profile of v0, /device:TPU:32, one launch (start us, length us, event | category | flops | bytes accessed | tf_op | source)
XLA Modules:
  0.0 284.7 jit_solution(13041195878704374268)
XLA Ops:
  0.0 12.5 %all-gather.1 = s32[4,32,12]{1,2,0:T(8,128)S(1)} all-gather(s32[1,32,12]{1,2,0:T(8,128)} %bitcast.141), channel_id=2, replica_groups=mesh['grp'=2,'ep_0'=4,'ep_1'=4,'ep_2'=8] {'ep_0'}, dimensions={0}, use_global_device_ids=true | all-gather | bytes 7680 | tf_op jit(solution)/shard_map/all_gather | solution.py:20
  12.5 12.5 %all_gather.10 = s32[16,32,12]{1,2,0:T(8,128)S(1)} all-gather(s32[4,32,12]{1,2,0:T(8,128)S(1)} %all-gather.1), channel_id=1, replica_groups=mesh['grp'=2,'ep_0'=4,'ep_1'=4,'ep_2'=8] {'ep_1'}, dimensions={0}, use_global_device_ids=true | all-gather | bytes 30720 | tf_op jit(solution)/shard_map/all_gather | solution.py:20
  25.0 28.7 %all_gather.11 = s32[128,32,12]{1,0,2:T(8,128)S(1)} all-gather(s32[16,32,12]{1,0,2:T(8,128)S(1)} %copy.26), channel_id=1, replica_groups=mesh['grp'=2,'ep_0'=4,'ep_1'=4,'ep_2'=8] {'ep_2'}, dimensions={0}, use_global_device_ids=true | all-gather | bytes 221184 | tf_op jit(solution)/shard_map/all_gather | solution.py:20
  53.7 0.2 copy.51
  53.9 0.4 eq.53
  54.3 0.3 fusion.3
  54.6 0.1 reduce_window_sum.28
  54.7 0.6 reduce-window.6
  55.3 0.2 slice_reduce_fusion
  55.5 0.2 reduce-window.9
  55.7 0.1 add_bitcast_fusion
  55.8 0.1 broadcast_in_dim_reshape.2
  55.9 0.1 copy.31
  56.0 0.1 copy.28
  56.2 0.1 copy.32
  56.3 0.1 reshape.279
  56.5 15.8 %gather_fusion = f32[256,6144]{1,0:T(8,128)} fusion(f32[2,96,6144]{2,1,0:T(8,128)} %param.7, s32[256]{0:T(256)S(1)} %reshape.279), kind=kCustom, calls=%fused_computation | custom fusion | bytes 12584960 | tf_op jit(solution)/shard_map/gather | solution.py:67
  72.3 8.0 %copy.35 = f32[32,8,8,768]{3,2,1,0:T(8,128)} copy(f32[32,8,8,768]{3,1,2,0:T(8,128)} %bitcast.113) | data formatting | bytes 12582912
  80.3 0.0 copy-start
  80.3 0.0 copy-start.2
  80.3 11.2 %all-to-all-start = ((f32[128,2,8,768]{3,2,1,0:T(8,128)}), f32[128,2,8,768]{3,2,1,0:T(8,128)}, u32[]{:S(2)}, u32[]{:S(2)}) async-start(f32[128,2,8,768]{3,2,1,0:T(8,128)} %bitcast.112), calls=%async_computation | async-start | bytes 12582912 | tf_op jit(solution)/shard_map/all_to_all | solution.py:82
  91.6 0.0 copy-done
  91.6 0.5 select_reduce_fusion
  92.2 0.0 copy-done.2
  92.3 131.6 %all-to-all-done = f32[128,2,8,768]{3,2,1,0:T(8,128)} async-done(((f32[128,2,8,768]{3,2,1,0:T(8,128)}), f32[128,2,8,768]{3,2,1,0:T(8,128)}, u32[]{:S(2)}, u32[]{:S(2)}) %all-to-all-start) | async-done | bytes 6291488 | tf_op jit(solution)/shard_map/all_to_all | solution.py:82
  223.8 3.4 %gather_fusion.1 = f32[32,8,768]{2,1,0:T(8,128)S(1)} fusion(f32[256,8,768]{2,1,0:T(8,128)} %bitcast.8, s32[1024]{0:T(1024)S(1)} %get-tuple-element.42), kind=kCustom, calls=%fused_computation.1 | custom fusion | bytes 1572992 | tf_op jit(solution)/shard_map/gather | solution.py:86
  227.2 0.2 copy.36
  227.5 3.4 %gather_fusion.2 = f32[32,8,768]{2,1,0:T(8,128)S(1)} fusion(f32[256,8,768]{2,1,0:T(8,128)} %bitcast.8, s32[1024]{0:T(1024)S(1)} %get-tuple-element.41), kind=kCustom, calls=%fused_computation.2 | custom fusion | bytes 1572992 | tf_op jit(solution)/shard_map/gather | solution.py:86
  230.9 0.2 copy.37
  231.1 3.4 %gather_fusion.3 = f32[32,8,768]{2,1,0:T(8,128)S(1)} fusion(f32[256,8,768]{2,1,0:T(8,128)} %bitcast.8, s32[1024]{0:T(1024)S(1)} %get-tuple-element.40), kind=kCustom, calls=%fused_computation.3 | custom fusion | bytes 1572992 | tf_op jit(solution)/shard_map/gather | solution.py:86
  234.5 0.2 copy.38
  234.8 3.4 %gather_fusion.4 = f32[32,8,768]{2,1,0:T(8,128)S(1)} fusion(f32[256,8,768]{2,1,0:T(8,128)} %bitcast.8, s32[1024]{0:T(1024)S(1)} %get-tuple-element.39), kind=kCustom, calls=%fused_computation.4 | custom fusion | bytes 1572992 | tf_op jit(solution)/shard_map/gather | solution.py:86
  238.2 1.1 copy.39
  239.3 3.4 %gather_fusion.5 = f32[32,8,768]{2,1,0:T(8,128)S(1)} fusion(f32[256,8,768]{2,1,0:T(8,128)} %bitcast.8, s32[1024]{0:T(1024)S(1)} %get-tuple-element.38), kind=kCustom, calls=%fused_computation.5 | custom fusion | bytes 1572992 | tf_op jit(solution)/shard_map/gather | solution.py:86
  242.7 1.1 copy.40
  243.8 3.4 %gather_fusion.6 = f32[32,8,768]{2,1,0:T(8,128)S(1)} fusion(f32[256,8,768]{2,1,0:T(8,128)} %bitcast.8, s32[1024]{0:T(1024)S(1)} %get-tuple-element.37), kind=kCustom, calls=%fused_computation.6 | custom fusion | bytes 1572992 | tf_op jit(solution)/shard_map/gather | solution.py:86
  247.2 1.2 copy.41
  248.4 3.4 %gather_fusion.7 = f32[32,8,768]{2,1,0:T(8,128)S(1)} fusion(f32[256,8,768]{2,1,0:T(8,128)} %bitcast.8, s32[1024]{0:T(1024)S(1)} %get-tuple-element.36), kind=kCustom, calls=%fused_computation.7 | custom fusion | bytes 1572992 | tf_op jit(solution)/shard_map/gather | solution.py:86
  251.8 1.1 copy.42
  252.9 3.4 %gather_fusion.8 = f32[32,8,768]{2,1,0:T(8,128)S(1)} fusion(f32[256,8,768]{2,1,0:T(8,128)} %bitcast.8, s32[1024]{0:T(1024)S(1)} %get-tuple-element.35), kind=kCustom, calls=%fused_computation.8 | custom fusion | bytes 1572992 | tf_op jit(solution)/shard_map/gather | solution.py:86
  256.3 1.2 copy.43
  257.5 3.4 %gather_fusion.9 = f32[32,8,768]{2,1,0:T(8,128)S(1)} fusion(f32[256,8,768]{2,1,0:T(8,128)} %bitcast.8, s32[1024]{0:T(1024)S(1)} %get-tuple-element.34), kind=kCustom, calls=%fused_computation.9 | custom fusion | bytes 1572992 | tf_op jit(solution)/shard_map/gather | solution.py:86
  260.9 1.2 copy.44
  262.1 3.4 %gather_fusion.10 = f32[32,8,768]{2,1,0:T(8,128)S(1)} fusion(f32[256,8,768]{2,1,0:T(8,128)} %bitcast.8, s32[1024]{0:T(1024)S(1)} %get-tuple-element.33), kind=kCustom, calls=%fused_computation.10 | custom fusion | bytes 1572992 | tf_op jit(solution)/shard_map/gather | solution.py:86
  265.5 1.1 copy.45
  266.6 3.4 %gather_fusion.11 = f32[32,8,768]{2,1,0:T(8,128)S(1)} fusion(f32[256,8,768]{2,1,0:T(8,128)} %bitcast.8, s32[1024]{0:T(1024)S(1)} %get-tuple-element.32), kind=kCustom, calls=%fused_computation.11 | custom fusion | bytes 1572992 | tf_op jit(solution)/shard_map/gather | solution.py:86
  270.0 1.1 copy.46
  271.1 3.4 %gather_fusion.12 = f32[32,8,768]{2,1,0:T(8,128)S(1)} fusion(f32[256,8,768]{2,1,0:T(8,128)} %bitcast.8, s32[1024]{0:T(1024)S(1)} %get-tuple-element.31), kind=kCustom, calls=%fused_computation.12 | custom fusion | bytes 1572992 | tf_op jit(solution)/shard_map/gather | solution.py:86
  274.5 0.2 copy.47
  274.7 3.7 %multiply_add_fusion = f32[32,6144]{1,0:T(8,128)S(1)} fusion(f32[32,6144]{1,0:T(8,128)S(1)} %bitcast.139, f32[32,6144]{1,0:T(8,128)} %bitcast.138, f32[32,6144]{1,0:T(8,128)} %bitcast.137, f32[32,6144]{1,0:T(8,128)} %bitcast.136, f32[32,6144]{1,0:T(8,128)} %bitcast.135, f32[32,6144]{1,0:T(8,128)} %bitcast.134, f32[32,6144]{1,0:T(8,128)} %bitcast.133, ...), kind=kLoop, calls=%fused_computation.19 | loop fusion | flops 4521984 | bytes 10225152 | tf_op jit(solution)/shard_map/add | solution.py:86
  278.4 0.0 copy-start.1
  278.4 0.1 broadcast_in_dim.9
  278.6 5.1 %all_to_all.10 = f32[2,32,6144]{2,1,0:T(8,128)S(1)} all-to-all(f32[2,32,6144]{2,1,0:T(8,128)S(1)} %broadcast_in_dim.9), channel_id=1, replica_groups=mesh['grp'=2,'ep_0'=4,'ep_1'=4,'ep_2'=8] {'grp'}, dimensions={0} | all-to-all | bytes 3145728 | tf_op jit(solution)/shard_map/all_to_all | solution.py:33
  283.7 0.2 reduce_sum.48
  283.8 0.0 copy-done.1
  283.9 0.9 multiply_add_fusion.1
  (20 shorter events, 0.3 us)
Async XLA Ops:
  80.3 11.2 %copy-start = (s32[32,12]{0,1:T(8,128)S(1)}, s32[32,12]{0,1:T(8,128)}, u32[]{:S(2)}) copy-start(s32[32,12]{0,1:T(8,128)} %param.5) | copy-start | bytes 4612
  80.3 11.9 %copy-start.2 = (f32[32,12]{0,1:T(8,128)S(1)}, f32[32,12]{0,1:T(8,128)}, u32[]{:S(2)}) copy-start(f32[32,12]{0,1:T(8,128)} %param.6) | copy-start | bytes 4612
  80.3 143.5 %all-to-all-start = ((f32[128,2,8,768]{3,2,1,0:T(8,128)}), f32[128,2,8,768]{3,2,1,0:T(8,128)}, u32[]{:S(2)}, u32[]{:S(2)}) async-start(f32[128,2,8,768]{3,2,1,0:T(8,128)} %bitcast.112), calls=%async_computation | async-start | bytes 12582912 | tf_op jit(solution)/shard_map/all_to_all | solution.py:82
  278.4 5.4 %copy-start.1 = (f32[32,6144]{1,0:T(8,128)S(1)}, f32[32,6144]{1,0:T(8,128)}, u32[]{:S(2)}) copy-start(f32[32,6144]{1,0:T(8,128)} %param.4) | copy-start | bytes 2359300
where the time goes:
time: 287 us; the launch traced here: 285 us
  waiting for transfers between devices  132 us (46%)
  local copies, waits for them, and re-layouts  76.2 us (27%)
  blocking collectives  58.7 us (20%)
  starting transfers between devices  11.2 us (4%)
  other arithmetic  6.59 us (2%)
    all_to_all x1, waiting for transfers between devices, shards(): lax.all_to_all(outgoing, EP, split_axis=0, concat_axis=0, tiled=True)  132 us
    all_gather x3, blocking collectives, stacked_from(): parts = lax.all_gather(parts, axes[k], axis=0, tiled=True)  53.6 us
    gather x12, local copies, waits for them, and re-layouts, shards(): rows[flat_index[:, slot]]  40.6 us
    unnamed x20, local copies, waits for them, and re-layouts  18.3 us
    gather x1, local copies, waits for them, and re-layouts, shards(): expert_rows[jnp.arange(exp_dev, dtype=jnp.int32)[None, :, None], table]  15.8 us
    all_to_all x1, starting transfers between devices, shards(): lax.all_to_all(outgoing, EP, split_axis=0, concat_axis=0, tiled=True)  11.2 us
  transfers between devices with their start and end apart: 1, of which 1 were waited for; matrix products, arithmetic and copies ran while one was open for 0% of the time, Pallas kernels for 0%

commit v1 on v0

v1 whole, which is shorter than its diff:
```python
import jax
import jax.numpy as jnp
from jax import lax
from jax.sharding import Mesh
from jax.sharding import PartitionSpec as P

EP = ("x", "y", "zh", "zl")
NEAR = ("x", "y", "zl")
EXACT = lax.Precision.HIGHEST


def shards(tokens, route_ids, route_weights, expert_rows):
    group = lax.axis_index("grp")
    ep_count = lax.axis_size(EP)
    far = lax.axis_size("zh")
    low = lax.axis_size("zl")
    near = ep_count // far
    tok_dev, top = route_ids.shape
    exp_dev, capacity, width = expert_rows.shape
    half = width // 2
    held = 2 * exp_dev
    per_group = exp_dev * ep_count
    experts = 2 * per_group

    own = lax.dynamic_slice_in_dim(expert_rows, group * half, half, 2)
    given = lax.dynamic_slice_in_dim(expert_rows, (1 - group) * half, half, 2)
    taken = lax.ppermute(given, "grp", [(0, 1), (1, 0)])
    table = jnp.concatenate([own, taken], axis=0).reshape(held * capacity, half)

    real = route_ids < experts
    ids_t = route_ids.T
    chip = jnp.where(ids_t < experts, ids_t % per_group // exp_dev, -1)
    place = (ids_t // per_group != group) * exp_dev + ids_t % exp_dev
    lanes = jnp.arange(128, dtype=jnp.int32)
    chip_hot = (chip[:, :, None] == jnp.arange(ep_count, dtype=jnp.int32)).astype(jnp.bfloat16)
    place_hot = (place[:, :, None] == lanes).astype(jnp.bfloat16)
    flags = lax.dot_general(
        chip_hot.reshape(top * tok_dev, ep_count), place_hot.reshape(top * tok_dev, 128),
        (((0,), (0,)), ((), ())), preferred_element_type=jnp.float32,
    )
    chosen = lax.all_to_all(flags[:, None, :], EP, 0, 0, tiled=True).reshape(ep_count, 128)
    chosen = chosen.astype(jnp.bfloat16)

    row = jnp.arange(ep_count * held, dtype=jnp.int32)[:, None]
    r_exp = row % held
    r_far = row // held % far
    r_near = row // (held * far)
    home = (r_near // low * far + r_far) * low + r_near % low
    homes = jnp.arange(ep_count, dtype=jnp.int32)[None, :]
    before = jnp.dot((homes < home).astype(jnp.bfloat16), chosen, preferred_element_type=jnp.float32)
    here = jnp.dot((homes == home).astype(jnp.bfloat16), chosen, preferred_element_type=jnp.float32)
    mine = lanes[None, :] == r_exp
    rank = jnp.sum(jnp.where(mine, before, 0.0), axis=1, keepdims=True)
    hit = jnp.sum(jnp.where(mine, here, 0.0), axis=1, keepdims=True)
    code = jnp.where(hit > 0, rank.astype(jnp.int32) + capacity * r_exp, -1)
    select = (code == jnp.arange(held * capacity, dtype=jnp.int32)[None, :]).astype(jnp.float32)
    outgoing = jnp.dot(select, table, precision=EXACT).reshape(near, far * held, half)

    rows = lax.all_to_all(outgoing, NEAR, 0, 0, tiled=True).reshape(ep_count * held, half)

    pair = jnp.concatenate([route_ids.astype(jnp.float32), route_weights], axis=1)
    pairs = lax.all_gather(pair, "zh", axis=0, tiled=True)
    col = jnp.arange(ep_count * held, dtype=jnp.int32)[None, :]
    c_exp = col % held
    c_far = col // held % far
    c_near = col // (held * far)
    c_chip = (c_near // low * far + lax.axis_index("zh")) * low + c_near % low
    c_group = jnp.where(c_exp < exp_dev, group, 1 - group)
    c_id = (c_group * per_group + c_chip * exp_dev + c_exp % exp_dev).astype(jnp.float32)
    mix = jnp.zeros((far * tok_dev, ep_count * held), jnp.float32)
    for k in range(top):
        mix = mix + jnp.where(pairs[:, k : k + 1] == c_id, pairs[:, top + k : top + k + 1], 0.0)
    line = jnp.arange(far * tok_dev, dtype=jnp.int32)[:, None]
    mix = jnp.where(line // tok_dev == c_far, mix, 0.0)
    partial = jnp.dot(mix, rows, precision=EXACT).reshape(far, tok_dev, half)
    total = lax.psum_scatter(partial, "zh", scatter_dimension=0, tiled=True).reshape(tok_dev, half)

    ident = jnp.sum(jnp.where(real, 0.0, route_weights), axis=1, keepdims=True)
    return total + ident * lax.dynamic_slice_in_dim(tokens, group * half, half, 1)


def solution(mesh):
    torus = Mesh(mesh.devices.reshape(mesh.shape["grp"], 4, 4, 4, 2), ("grp",) + EP)
    in_specs = (P(EP, None), P(EP, None), P(EP, None), P(("grp",) + EP, None, None))
    return jax.shard_map(
        shards, mesh=torus, in_specs=in_specs, out_specs=P(EP, "grp"), check_vma=False
    )
```

time: 287 us -> 219 us (0.76)
  the two profiles are of different devices: /device:TPU:32 before, /device:TPU:1 now
where the time goes in v1:
time: 219 us
  blocking collectives  80.8 us (37%)
  waiting for transfers between devices  75.4 us (34%)
  starting transfers between devices  22.1 us (10%)
  matrix products  16.6 us (8%)
  between operations  13.5 us (6%)
  local copies, waits for them, and re-layouts  6.55 us (3%)
  other arithmetic  3.94 us (2%)
    all_gather x1, blocking collectives, shards(): pairs = lax.all_gather(pair, 'zh', axis=0, tiled=True)  80.8 us
    reduce_scatter x1, waiting for transfers between devices, shards(): lax.psum_scatter(partial, 'zh', scatter_dimension=0, tiled=True)  47.8 us
    all_to_all x1, waiting for transfers between devices, shards(): lax.all_to_all(outgoing, NEAR, 0, 0, tiled=True)  17.1 us
    all_to_all x1, starting transfers between devices, shards(): lax.all_to_all(flags[:, None, :], EP, 0, 0, tiled=True)  13.8 us
    all_to_all x1, waiting for transfers between devices, shards(): lax.all_to_all(flags[:, None, :], EP, 0, 0, tiled=True)  10.5 us
    dot_general x1, matrix products, shards(): partial = jnp.dot(mix, rows, precision=EXACT).reshape(far, tok_dev, half)  7.8 us
    dot_general x1, matrix products, shards(): jnp.dot(select, table, precision=EXACT).reshape(near, far * held, half)  7.15 us
    all_to_all x1, starting transfers between devices, shards(): lax.all_to_all(outgoing, NEAR, 0, 0, tiled=True)  5.03 us
  transfers between devices with their start and end apart: 4, of which 3 were waited for; matrix products, arithmetic and copies ran while one was open for 2% of the time, Pallas kernels for 0%

profile of v1, /device:TPU:1, one launch (start us, length us, event | category | flops | bytes accessed | tf_op | source)
XLA Modules:
  0.0 218.9 jit_solution(3141260422082935296)
XLA Ops:
  6.5 0.0 copy-start.1
  6.5 4.2 %constant_dynamic-slice_fusion.1 = (f32[2,96,3072]{2,1,0:T(8,128)S(1)}, f32[2,96,3072]{2,1,0:T(8,128)}) fusion(f32[2,96,6144]{2,1,0:T(8,128)} %param.7, s32[]{:T(128)S(6)} %select_n.346, s32[]{:T(128)S(6)} %select_n.347), kind=kLoop, calls=%fused_computation.168 | loop fusion | bytes 9437192 | tf_op jit(solution)/shard_map/dynamic_slice | solution.py:25
  10.8 3.2 %collective-permute-start = (f32[2,96,3072]{2,1,0:T(8,128)}, f32[2,96,3072]{2,1,0:T(8,128)}, u32[]{:S(2)}, u32[]{:S(2)}) collective-permute-start(f32[2,96,3072]{2,1,0:T(8,128)} %get-tuple-element.30), channel_id=1, source_target_pairs={{0,128},{128,0},{1,129},{129,1},{2,130},{130,2},{3,131},{131,3},{4... | collective-permute-start | bytes 7077896 | tf_op jit(solution)/shard_map/ppermute | solution.py:27
  14.0 0.0 copy-done.1
  14.0 1.0 fusion.44
  15.1 13.8 %all-to-all-start = ((f32[128,1,128]{2,1,0:T(1,128)}), f32[128,1,128]{2,1,0:T(1,128)S(1)}, u32[]{:S(2)}, u32[]{:S(2)}) async-start(f32[128,1,128]{2,1,0:T(1,128)} %bitcast.4), calls=%async_computation | async-start | bytes 131072 | tf_op jit(solution)/shard_map/all_to_all | solution.py:41
  28.9 10.5 %all-to-all-done = f32[128,1,128]{2,1,0:T(1,128)S(1)} async-done(((f32[128,1,128]{2,1,0:T(1,128)}), f32[128,1,128]{2,1,0:T(1,128)S(1)}, u32[]{:S(2)}, u32[]{:S(2)}) %all-to-all-start) | async-done | bytes 65568 | tf_op jit(solution)/shard_map/all_to_all | solution.py:41
  39.4 0.3 fusion.1
  39.7 0.1 convert_element_type.39
  39.8 0.3 fusion
  40.1 0.1 gt.16
  40.2 0.0 collective-permute-done
  40.2 2.0 pad_maximum_fusion
  42.2 7.1 %fusion.3 = f32[32,16,3072]{2,1,0:T(8,128)} fusion(f32[384,3072,1]{1,0,2:T(8,128)S(1)} %bitcast.60, s32[32,16]{1,0:T(8,128)S(1)} %fusion.81), kind=kOutput, calls=%fused_computation.7 | convolution fusion | flops 7247953920 | bytes 11012096 | tf_op jit(solution)/shard_map/dot_general | solution.py:57
  49.4 0.0 copy-start.2
  49.4 5.0 %all-to-all-start.1 = ((f32[32,16,3072]{2,1,0:T(8,128)}), f32[32,16,3072]{2,1,0:T(8,128)}, u32[]{:S(2)}, u32[]{:S(2)}) async-start(f32[32,16,3072]{2,1,0:T(8,128)} %fusion.3), calls=%async_computation.1 | async-start | bytes 12582912 | tf_op jit(solution)/shard_map/all_to_all | solution.py:59
  54.4 0.0 reduce-scatter.2.cloned.1.call-start
  54.5 0.0 copy-done.2
  54.5 80.8 %all-gather = f32[4,32,24]{1,2,0:T(8,128)S(1)} all-gather(f32[1,32,24]{1,2,0:T(8,128)S(1)} %maximum_bitcast_fusion), channel_id=1, replica_groups=mesh['grp'=2,'x'=4,'y'=4,'zh'=4,'zl'=2] {'zh'}, dimensions={0}, use_global_device_ids=true | all-gather | bytes 15360 | tf_op jit(solution)/shard_map/all_gather | solution.py:62
  135.3 0.1 reshape.705
  135.5 0.1 broadcast_in_dim.150
  135.6 0.1 broadcast_in_dim.152
  135.6 0.1 broadcast_in_dim.154
  135.7 0.1 broadcast_in_dim.156
  135.8 0.1 broadcast_in_dim.158
  135.9 0.1 broadcast_in_dim.160
  136.0 0.1 broadcast_in_dim.162
  136.1 0.1 broadcast_in_dim.164
  136.1 0.1 broadcast_in_dim.166
  136.2 0.1 eq.342
  136.3 0.1 eq.355
  136.4 0.1 eq.358
  136.5 0.1 eq.361
  136.5 0.1 eq.364
  136.6 0.1 eq.367
  136.7 0.1 eq.370
  136.8 0.1 eq.373
  136.9 0.1 eq.376
  137.0 0.1 broadcast_in_dim.143
  137.1 0.1 broadcast_in_dim.146
  137.2 0.1 broadcast_in_dim.148
  137.3 0.1 eq.346
  137.3 0.1 eq.349
  137.4 0.1 eq.352
  137.5 17.1 %all-to-all-done.1 = f32[32,16,3072]{2,1,0:T(8,128)} async-done(((f32[32,16,3072]{2,1,0:T(8,128)}), f32[32,16,3072]{2,1,0:T(8,128)}, u32[]{:S(2)}, u32[]{:S(2)}) %all-to-all-start.1) | async-done | bytes 6291488 | tf_op jit(solution)/shard_map/all_to_all | solution.py:59
  154.6 0.0 copy-start
  154.6 7.8 %fusion.6 = f32[4,32,3072]{2,1,0:T(8,128)} fusion(f32[512,3072,1]{1,0,2:T(8,128)} %bitcast.11, f32[4,32]{1,0:T(4,128)S(1)} %broadcast_in_dim.166, f32[4,32]{1,0:T(4,128)S(1)} %eq.376, f32[4,32]{1,0:T(4,128)S(1)} %broadcast_in_dim.164, f32[4,32]{1,0:T(4,128)S(1)} %eq.373, f32[4,32]{1,0:T(4,128)S(1)} %broadcast_in_dim.162, f32[4,32]{1,0:T(4,128)S(1)} %eq.370, ...), kind=kOutput, calls=%fused_computation.13 | convolution fusion | flops 2418343936 | bytes 7881216 | tf_op jit(solution)/shard_map/dot_general | solution.py:75
  162.4 0.0 reduce-scatter.2.cloned.1.call-update
  162.5 47.8 %reduce-scatter.2.cloned.1.call-done = f32[1,32,3072]{2,1,0:T(8,128)} async-done(((f32[4,32,3072]{2,1,0:T(8,128)}), f32[1,32,3072]{2,1,0:T(8,128)}) %reduce-scatter.2.cloned.1.call-update) | async-done | bytes 393232 | tf_op jit(solution)/shard_map/reduce_scatter | solution.py:76
  210.2 0.0 copy-done
  210.3 1.8 bitcast_add_fusion
  (13 shorter events, 0.2 us)
Async XLA Ops:
  6.5 7.5 %copy-start.1 = (s32[32,12]{0,1:T(8,128)S(1)}, s32[32,12]{0,1:T(8,128)}, u32[]{:S(2)}) copy-start(s32[32,12]{0,1:T(8,128)} %param.5) | copy-start | bytes 4612
  10.8 29.5 %collective-permute-start = (f32[2,96,3072]{2,1,0:T(8,128)}, f32[2,96,3072]{2,1,0:T(8,128)}, u32[]{:S(2)}, u32[]{:S(2)}) collective-permute-start(f32[2,96,3072]{2,1,0:T(8,128)} %get-tuple-element.30), channel_id=1, source_target_pairs={{0,128},{128,0},{1,129},{129,1},{2,130},{130,2},{3,131},{131,3},{4... | collective-permute-start | bytes 7077896 | tf_op jit(solution)/shard_map/ppermute | solution.py:27
  15.1 24.3 %all-to-all-start = ((f32[128,1,128]{2,1,0:T(1,128)}), f32[128,1,128]{2,1,0:T(1,128)S(1)}, u32[]{:S(2)}, u32[]{:S(2)}) async-start(f32[128,1,128]{2,1,0:T(1,128)} %bitcast.4), calls=%async_computation | async-start | bytes 131072 | tf_op jit(solution)/shard_map/all_to_all | solution.py:41
  49.4 5.1 %copy-start.2 = (f32[32,12]{0,1:T(8,128)S(1)}, f32[32,12]{0,1:T(8,128)}, u32[]{:S(2)}) copy-start(f32[32,12]{0,1:T(8,128)} %param.6) | copy-start | bytes 4612
  49.4 105.2 %all-to-all-start.1 = ((f32[32,16,3072]{2,1,0:T(8,128)}), f32[32,16,3072]{2,1,0:T(8,128)}, u32[]{:S(2)}, u32[]{:S(2)}) async-start(f32[32,16,3072]{2,1,0:T(8,128)} %fusion.3), calls=%async_computation.1 | async-start | bytes 12582912 | tf_op jit(solution)/shard_map/all_to_all | solution.py:59
  54.4 155.8 %reduce-scatter.2.cloned.1.call-start = ((), (), s32[]{:S(2)}) async-start(), calls=%async_computation.3 | async-start | bytes 1966080 | tf_op jit(solution)/shard_map/reduce_scatter | solution.py:76
  154.6 55.6 %copy-start = (f32[32,6144]{1,0:T(8,128)S(1)}, f32[32,6144]{1,0:T(8,128)}, u32[]{:S(2)}) copy-start(f32[32,6144]{1,0:T(8,128)} %param.4) | copy-start | bytes 2359300
Sparse Core Ops, SparseCore 0:
  162.6 47.6 reduce-scatter.1

commit v2 on v1

--- a/solution.py
+++ b/solution.py
@@ -7,6 +7,10 @@
 EP = ("x", "y", "zh", "zl")
 NEAR = ("x", "y", "zl")
 EXACT = lax.Precision.HIGHEST
+
+
+def shift(count, by):
+    return [(i, (i + by) % count) for i in range(count)]
 
 
 def shards(tokens, route_ids, route_weights, expert_rows):
@@ -45,7 +49,8 @@
     r_exp = row % held
     r_far = row // held % far
     r_near = row // (held * far)
-    home = (r_near // low * far + r_far) * low + r_near % low
+    r_home = (lax.axis_index("zh") + r_far) % far
+    home = (r_near // low * far + r_home) * low + r_near % low
     homes = jnp.arange(ep_count, dtype=jnp.int32)[None, :]
     before = jnp.dot((homes < home).astype(jnp.bfloat16), chosen, preferred_element_type=jnp.float32)
     here = jnp.dot((homes == home).astype(jnp.bfloat16), chosen, preferred_element_type=jnp.float32)
@@ -59,7 +64,9 @@
     rows = lax.all_to_all(outgoing, NEAR, 0, 0, tiled=True).reshape(ep_count * held, half)
 
     pair = jnp.concatenate([route_ids.astype(jnp.float32), route_weights], axis=1)
-    pairs = lax.all_gather(pair, "zh", axis=0, tiled=True)
+    pairs = jnp.concatenate(
+        [pair] + [lax.ppermute(pair, "zh", shift(far, -o)) for o in range(1, far)], axis=0
+    )
     col = jnp.arange(ep_count * held, dtype=jnp.int32)[None, :]
     c_exp = col % held
     c_far = col // held % far
@@ -73,7 +80,15 @@
     line = jnp.arange(far * tok_dev, dtype=jnp.int32)[:, None]
     mix = jnp.where(line // tok_dev == c_far, mix, 0.0)
     partial = jnp.dot(mix, rows, precision=EXACT).reshape(far, tok_dev, half)
-    total = lax.psum_scatter(partial, "zh", scatter_dimension=0, tiled=True).reshape(tok_dev, half)
+    cut = half // 2
+    up, down = shift(far, 1), shift(far, -1)
+    far_up = lax.ppermute(partial[2, :, :cut], "zh", up)
+    far_down = lax.ppermute(partial[2, :, cut:], "zh", down)
+    next_right = lax.ppermute(partial[1, :, cut:], "zh", up)
+    prev_left = lax.ppermute(partial[3, :, :cut], "zh", down)
+    next_left = lax.ppermute(partial[1, :, :cut] + far_up, "zh", up)
+    prev_right = lax.ppermute(partial[3, :, cut:] + far_down, "zh", down)
+    total = partial[0] + jnp.concatenate([next_left + prev_left, next_right + prev_right], axis=1)
 
     ident = jnp.sum(jnp.where(real, 0.0, route_weights), axis=1, keepdims=True)
     return total + ident * lax.dynamic_slice_in_dim(tokens, group * half, half, 1)

time: 219 us -> 185 us (0.84)
  the two profiles are of different devices: /device:TPU:1 before, /device:TPU:58 now
where the time goes in v2:
time: 185 us
  waiting for transfers between devices  117 us (63%)
  starting transfers between devices  45.2 us (24%)
  matrix products  15.5 us (8%)
  local copies, waits for them, and re-layouts  4.5 us (2%)
  other arithmetic  3.13 us (2%)
    ppermute x3, waiting for transfers between devices, shards(): lax.ppermute(pair, 'zh', shift(far, -o))  101 us
    all_to_all x1, starting transfers between devices, shards(): lax.all_to_all(flags[:, None, :], EP, 0, 0, tiled=True)  14.9 us
    all_to_all x1, waiting for transfers between devices, shards(): lax.all_to_all(flags[:, None, :], EP, 0, 0, tiled=True)  8.61 us
    all_to_all x1, starting transfers between devices, shards(): lax.all_to_all(outgoing, NEAR, 0, 0, tiled=True)  8.34 us
    dot_general x1, matrix products, shards(): jnp.dot(select, table, precision=EXACT).reshape(near, far * held, half)  7.16 us
    dot_general x1, matrix products, shards(): partial = jnp.dot(mix, rows, precision=EXACT).reshape(far, tok_dev, half)  6.66 us
    ppermute x1, starting transfers between devices, shards(): next_left = lax.ppermute(partial[1, :, :cut] + far_up, 'zh', up)  6.06 us
    ppermute x1, starting transfers between devices, shards(): far_down = lax.ppermute(partial[2, :, cut:], 'zh', down)  4.65 us
  transfers between devices with their start and end apart: 12, of which 6 were waited for; matrix products, arithmetic and copies ran while one was open for 1% of the time, Pallas kernels for 0%

profile of v2, /device:TPU:58, one launch (start us, length us, event | category | flops | bytes accessed | tf_op | source)
XLA Modules:
  0.0 185.1 jit_solution(15604761103046751000)
XLA Ops:
  0.0 0.0 copy-start.1
  0.0 4.2 %constant_dynamic-slice_fusion.1 = (f32[2,96,3072]{2,1,0:T(8,128)S(1)}, f32[2,96,3072]{2,1,0:T(8,128)}) fusion(f32[2,96,6144]{2,1,0:T(8,128)} %param.7, s32[]{:T(128)S(6)} %select_n.283, s32[]{:T(128)S(6)} %select_n.284), kind=kLoop, calls=%fused_computation.183 | loop fusion | bytes 9437192 | tf_op jit(solution)/shard_map/dynamic_slice | solution.py:29
  4.3 0.0 collective-permute-start.3
  4.3 0.0 copy-done.1
  4.3 1.0 fusion.47
  5.3 14.9 %all-to-all-start = ((f32[128,1,128]{2,1,0:T(1,128)}), f32[128,1,128]{2,1,0:T(1,128)S(1)}, u32[]{:S(2)}, u32[]{:S(2)}) async-start(f32[128,1,128]{2,1,0:T(1,128)} %bitcast.27), calls=%async_computation | async-start | bytes 131072 | tf_op jit(solution)/shard_map/all_to_all | solution.py:45
  20.3 8.6 %all-to-all-done = f32[128,1,128]{2,1,0:T(1,128)S(1)} async-done(((f32[128,1,128]{2,1,0:T(1,128)}), f32[128,1,128]{2,1,0:T(1,128)S(1)}, u32[]{:S(2)}, u32[]{:S(2)}) %all-to-all-start) | async-done | bytes 65568 | tf_op jit(solution)/shard_map/all_to_all | solution.py:45
  28.9 0.3 fusion.1
  29.2 0.1 convert_element_type.39
  29.3 0.3 fusion
  29.6 0.1 gt.16
  29.7 0.0 collective-permute-done.3
  29.7 2.0 %pad_maximum_fusion = f32[4,96,3072]{2,1,0:T(8,128)S(1)} fusion(f32[2,96,3072]{2,1,0:T(8,128)} %collective-permute-done.3, f32[2,96,3072]{2,1,0:T(8,128)S(1)} %get-tuple-element.5), kind=kLoop, calls=%fused_computation | loop fusion | flops 1179648 | bytes 9437184 | tf_op jit(solution)/shard_map/concatenate | solution.py:32
  31.7 7.2 %fusion.3 = f32[32,16,3072]{2,1,0:T(8,128)} fusion(f32[384,3072,1]{1,0,2:T(8,128)S(1)} %bitcast.117, s32[32,16]{1,0:T(8,128)S(1)} %fusion.84), kind=kOutput, calls=%fused_computation.7 | convolution fusion | flops 7247953920 | bytes 11012096 | tf_op jit(solution)/shard_map/dot_general | solution.py:62
  38.9 0.0 copy-start.2
  38.9 8.3 %all-to-all-start.1 = ((f32[32,16,3072]{2,1,0:T(8,128)}), f32[32,16,3072]{2,1,0:T(8,128)}, u32[]{:S(2)}, u32[]{:S(2)}) async-start(f32[32,16,3072]{2,1,0:T(8,128)} %fusion.3), calls=%async_computation.1 | async-start | bytes 12582912 | tf_op jit(solution)/shard_map/all_to_all | solution.py:64
  47.2 0.0 copy-done.2
  47.3 0.7 collective-permute-start
  48.0 3.5 %collective-permute-start.1 = (f32[32,24]{0,1:T(8,128)S(1)}, f32[32,24]{0,1:T(8,128)S(1)}, u32[]{:S(2)}, u32[]{:S(2)}) collective-permute-start(f32[32,24]{0,1:T(8,128)S(1)} %pad_maximum_fusion.1), channel_id=1, source_target_pairs={{0,4},{2,6},{4,0},{6,2},{1,5},{3,7},{5,1},{7,3},{8,12},{10,14},{12... | collective-permute-start | bytes 9224 | tf_op jit(solution)/shard_map/ppermute | solution.py:68
  51.5 0.0 collective-permute-start.2
  51.5 101.0 %collective-permute-done = f32[32,24]{0,1:T(8,128)S(1)} collective-permute-done((f32[32,24]{0,1:T(8,128)S(1)}, f32[32,24]{0,1:T(8,128)S(1)}, u32[]{:S(2)}, u32[]{:S(2)}) %collective-permute-start) | collective-permute-done | bytes 3104 | tf_op jit(solution)/shard_map/ppermute | solution.py:68
  152.6 0.1 collective-permute-done.1
  152.7 0.0 collective-permute-done.2
  152.7 0.1 pad_maximum_fusion.2
  152.8 0.0 all-to-all-done.1
  152.8 0.0 copy-start
  152.8 6.7 %fusion.7 = f32[128,3072]{1,0:T(8,128)S(1)} fusion(f32[512,3072]{1,0:T(8,128)} %bitcast.33, f32[128]{0:T(128)S(1)} %get-tuple-element.14, f32[128]{0:T(128)S(1)} %get-tuple-element.16, f32[128]{0:T(128)S(1)} %get-tuple-element.18, f32[128]{0:T(128)S(1)} %get-tuple-element.20, f32[128]{0:T(128)S(1)} %get-tuple-element.22, f32[128]{0:T(128)S(1)} %get-tuple-element.24, ...), kind=kOutput, calls=%fused_computation.14 | convolution fusion | flops 2418343936 | bytes 7881216 | tf_op jit(solution)/shard_map/dot_general | solution.py:82
  159.5 0.1 slice_bitcast_fusion.3
  159.5 0.1 collective-permute-start.4
  159.6 4.6 %collective-permute-start.8 = (f32[32,1536]{1,0:T(8,128)S(1)}, f32[32,1536]{1,0:T(8,128)S(1)}, u32[]{:S(2)}, u32[]{:S(2)}) collective-permute-start(f32[32,1536]{1,0:T(8,128)S(1)} %get-tuple-element.8), channel_id=1, source_target_pairs={{0,6},{2,0},{4,2},{6,4},{1,7},{3,1},{5,3},{7,5},{8,14},{10,8},{12,... | collective-permute-start | bytes 589832 | tf_op jit(solution)/shard_map/ppermute | solution.py:86
  164.3 2.8 %collective-permute-start.6 = (f32[32,1536]{1,0:T(8,128)S(1)}, f32[32,1536]{1,0:T(8,128)S(1)}, u32[]{:S(2)}, u32[]{:S(2)}) collective-permute-start(f32[32,1536]{1,0:T(8,128)S(1)} %get-tuple-element.7), channel_id=1, source_target_pairs={{0,6},{2,0},{4,2},{6,4},{1,7},{3,1},{5,3},{7,5},{8,14},{10,8},{12,... | collective-permute-start | bytes 589832 | tf_op jit(solution)/shard_map/ppermute | solution.py:88
  167.1 2.6 %collective-permute-done.4 = f32[32,1536]{1,0:T(8,128)S(1)} collective-permute-done((f32[32,1536]{1,0:T(8,128)S(1)}, f32[32,1536]{1,0:T(8,128)S(1)}, u32[]{:S(2)}, u32[]{:S(2)}) %collective-permute-start.4) | collective-permute-done | bytes 196640 | tf_op jit(solution)/shard_map/ppermute | solution.py:85
  169.7 0.6 collective-permute-done.8
  170.3 0.1 fusion.46
  170.4 6.1 %collective-permute-start.5 = (f32[32,1536]{1,0:T(8,128)S(1)}, f32[32,1536]{1,0:T(8,128)S(1)}, u32[]{:S(2)}, u32[]{:S(2)}) collective-permute-start(f32[32,1536]{1,0:T(8,128)S(1)} %get-tuple-element.11), channel_id=1, source_target_pairs={{0,2},{2,4},{4,6},{6,0},{1,3},{3,5},{5,7},{7,1},{8,10},{10,12},{12... | collective-permute-start | bytes 589832 | tf_op jit(solution)/shard_map/ppermute | solution.py:89
  176.4 0.1 collective-permute-start.7
  176.5 4.0 %collective-permute-start.9 = (f32[32,1536]{1,0:T(8,128)S(1)}, f32[32,1536]{1,0:T(8,128)S(1)}, u32[]{:S(2)}, u32[]{:S(2)}) collective-permute-start(f32[32,1536]{1,0:T(8,128)S(1)} %get-tuple-element.12), channel_id=1, source_target_pairs={{0,6},{2,0},{4,2},{6,4},{1,7},{3,1},{5,3},{7,5},{8,14},{10,8},{12,... | collective-permute-start | bytes 589832 | tf_op jit(solution)/shard_map/ppermute | solution.py:90
  180.6 0.0 collective-permute-done.6
  180.6 0.0 collective-permute-done.5
  180.6 3.6 %collective-permute-done.7 = f32[32,1536]{1,0:T(8,128)S(1)} collective-permute-done((f32[32,1536]{1,0:T(8,128)S(1)}, f32[32,1536]{1,0:T(8,128)S(1)}, u32[]{:S(2)}, u32[]{:S(2)}) %collective-permute-start.7) | collective-permute-done | bytes 196640 | tf_op jit(solution)/shard_map/ppermute | solution.py:87
  184.2 0.0 collective-permute-done.9
  184.3 0.0 copy-done
  184.3 0.9 fusion.5
  (14 shorter events, 0.2 us)
Async XLA Ops:
  0.0 4.3 %copy-start.1 = (s32[32,12]{0,1:T(8,128)S(1)}, s32[32,12]{0,1:T(8,128)}, u32[]{:S(2)}) copy-start(s32[32,12]{0,1:T(8,128)} %param.5) | copy-start | bytes 4612
  4.3 25.5 %collective-permute-start.3 = (f32[2,96,3072]{2,1,0:T(8,128)}, f32[2,96,3072]{2,1,0:T(8,128)}, u32[]{:S(2)}, u32[]{:S(2)}) collective-permute-start(f32[2,96,3072]{2,1,0:T(8,128)} %get-tuple-element.6), channel_id=1, source_target_pairs={{0,128},{128,0},{1,129},{129,1},{2,130},{130,2},{3,131},{131,3},{4... | collective-permute-start | bytes 7077896 | tf_op jit(solution)/shard_map/ppermute | solution.py:31
  5.3 23.5 %all-to-all-start = ((f32[128,1,128]{2,1,0:T(1,128)}), f32[128,1,128]{2,1,0:T(1,128)S(1)}, u32[]{:S(2)}, u32[]{:S(2)}) async-start(f32[128,1,128]{2,1,0:T(1,128)} %bitcast.27), calls=%async_computation | async-start | bytes 131072 | tf_op jit(solution)/shard_map/all_to_all | solution.py:45
  38.9 8.4 %copy-start.2 = (f32[32,12]{0,1:T(8,128)S(1)}, f32[32,12]{0,1:T(8,128)}, u32[]{:S(2)}) copy-start(f32[32,12]{0,1:T(8,128)} %param.6) | copy-start | bytes 4612
  38.9 113.9 %all-to-all-start.1 = ((f32[32,16,3072]{2,1,0:T(8,128)}), f32[32,16,3072]{2,1,0:T(8,128)}, u32[]{:S(2)}, u32[]{:S(2)}) async-start(f32[32,16,3072]{2,1,0:T(8,128)} %fusion.3), calls=%async_computation.1 | async-start | bytes 12582912 | tf_op jit(solution)/shard_map/all_to_all | solution.py:64
  47.3 105.3 %collective-permute-start = (f32[32,24]{0,1:T(8,128)S(1)}, f32[32,24]{0,1:T(8,128)S(1)}, u32[]{:S(2)}, u32[]{:S(2)}) collective-permute-start(f32[32,24]{0,1:T(8,128)S(1)} %pad_maximum_fusion.1), channel_id=1, source_target_pairs={{0,6},{2,0},{4,2},{6,4},{1,7},{3,1},{5,3},{7,5},{8,14},{10,8},{12,... | collective-permute-start | bytes 9224 | tf_op jit(solution)/shard_map/ppermute | solution.py:68
  48.0 104.7 %collective-permute-start.1 = (f32[32,24]{0,1:T(8,128)S(1)}, f32[32,24]{0,1:T(8,128)S(1)}, u32[]{:S(2)}, u32[]{:S(2)}) collective-permute-start(f32[32,24]{0,1:T(8,128)S(1)} %pad_maximum_fusion.1), channel_id=1, source_target_pairs={{0,4},{2,6},{4,0},{6,2},{1,5},{3,7},{5,1},{7,3},{8,12},{10,14},{12... | collective-permute-start | bytes 9224 | tf_op jit(solution)/shard_map/ppermute | solution.py:68
  51.5 101.2 %collective-permute-start.2 = (f32[32,24]{0,1:T(8,128)S(1)}, f32[32,24]{0,1:T(8,128)S(1)}, u32[]{:S(2)}, u32[]{:S(2)}) collective-permute-start(f32[32,24]{0,1:T(8,128)S(1)} %pad_maximum_fusion.1), channel_id=1, source_target_pairs={{0,2},{2,4},{4,6},{6,0},{1,3},{3,5},{5,7},{7,1},{8,10},{10,12},{12... | collective-permute-start | bytes 9224 | tf_op jit(solution)/shard_map/ppermute | solution.py:68
  152.8 31.5 %copy-start = (f32[32,6144]{1,0:T(8,128)S(1)}, f32[32,6144]{1,0:T(8,128)}, u32[]{:S(2)}) copy-start(f32[32,6144]{1,0:T(8,128)} %param.4) | copy-start | bytes 2359300
  159.5 10.1 %collective-permute-start.4 = (f32[32,1536]{1,0:T(8,128)S(1)}, f32[32,1536]{1,0:T(8,128)S(1)}, u32[]{:S(2)}, u32[]{:S(2)}) collective-permute-start(f32[32,1536]{1,0:T(8,128)S(1)} %get-tuple-element.10), channel_id=1, source_target_pairs={{0,2},{2,4},{4,6},{6,0},{1,3},{3,5},{5,7},{7,1},{8,10},{10,12},{12... | collective-permute-start | bytes 589832 | tf_op jit(solution)/shard_map/ppermute | solution.py:85
  159.6 10.7 %collective-permute-start.8 = (f32[32,1536]{1,0:T(8,128)S(1)}, f32[32,1536]{1,0:T(8,128)S(1)}, u32[]{:S(2)}, u32[]{:S(2)}) collective-permute-start(f32[32,1536]{1,0:T(8,128)S(1)} %get-tuple-element.8), channel_id=1, source_target_pairs={{0,6},{2,0},{4,2},{6,4},{1,7},{3,1},{5,3},{7,5},{8,14},{10,8},{12,... | collective-permute-start | bytes 589832 | tf_op jit(solution)/shard_map/ppermute | solution.py:86
  164.3 16.3 %collective-permute-start.6 = (f32[32,1536]{1,0:T(8,128)S(1)}, f32[32,1536]{1,0:T(8,128)S(1)}, u32[]{:S(2)}, u32[]{:S(2)}) collective-permute-start(f32[32,1536]{1,0:T(8,128)S(1)} %get-tuple-element.7), channel_id=1, source_target_pairs={{0,6},{2,0},{4,2},{6,4},{1,7},{3,1},{5,3},{7,5},{8,14},{10,8},{12,... | collective-permute-start | bytes 589832 | tf_op jit(solution)/shard_map/ppermute | solution.py:88
  170.4 10.2 %collective-permute-start.5 = (f32[32,1536]{1,0:T(8,128)S(1)}, f32[32,1536]{1,0:T(8,128)S(1)}, u32[]{:S(2)}, u32[]{:S(2)}) collective-permute-start(f32[32,1536]{1,0:T(8,128)S(1)} %get-tuple-element.11), channel_id=1, source_target_pairs={{0,2},{2,4},{4,6},{6,0},{1,3},{3,5},{5,7},{7,1},{8,10},{10,12},{12... | collective-permute-start | bytes 589832 | tf_op jit(solution)/shard_map/ppermute | solution.py:89
  176.4 7.8 %collective-permute-start.7 = (f32[32,1536]{1,0:T(8,128)S(1)}, f32[32,1536]{1,0:T(8,128)S(1)}, u32[]{:S(2)}, u32[]{:S(2)}) collective-permute-start(f32[32,1536]{1,0:T(8,128)S(1)} %get-tuple-element.9), channel_id=1, source_target_pairs={{0,2},{2,4},{4,6},{6,0},{1,3},{3,5},{5,7},{7,1},{8,10},{10,12},{12... | collective-permute-start | bytes 589832 | tf_op jit(solution)/shard_map/ppermute | solution.py:87
  176.5 7.7 %collective-permute-start.9 = (f32[32,1536]{1,0:T(8,128)S(1)}, f32[32,1536]{1,0:T(8,128)S(1)}, u32[]{:S(2)}, u32[]{:S(2)}) collective-permute-start(f32[32,1536]{1,0:T(8,128)S(1)} %get-tuple-element.12), channel_id=1, source_target_pairs={{0,6},{2,0},{4,2},{6,4},{1,7},{3,1},{5,3},{7,5},{8,14},{10,8},{12,... | collective-permute-start | bytes 589832 | tf_op jit(solution)/shard_map/ppermute | solution.py:90

commit v3 on v2

--- a/solution.py
+++ b/solution.py
@@ -3,10 +3,94 @@
 from jax import lax
 from jax.sharding import Mesh
 from jax.sharding import PartitionSpec as P
+from jax.experimental import pallas as pl
+from jax.experimental.pallas import tpu as pltpu
 
 EP = ("x", "y", "zh", "zl")
 NEAR = ("x", "y", "zl")
-EXACT = lax.Precision.HIGHEST
+BLOCK = 512
+VMEM = 40 * 1024 * 1024
+
+
+def thirds(x):
+    high = x.astype(jnp.bfloat16)
+    rest = x - high.astype(jnp.float32)
+    middle = rest.astype(jnp.bfloat16)
+    low = (rest - middle.astype(jnp.float32)).astype(jnp.bfloat16)
+    return high, middle, low
+
+
+def mul(a, b):
+    return jnp.dot(a, b, preferred_element_type=jnp.float32)
+
+
+def pick_kernel(group_ref, code_ref, own_ref, taken_ref, out_ref, select):
+    @pl.when(pl.program_id(0) == 0)
+    def _():
+        slot = lax.broadcasted_iota(jnp.int32, select.shape, 1)
+        select[...] = (code_ref[...] == slot).astype(jnp.float32).astype(jnp.bfloat16)
+
+    flat = (own_ref.shape[0] * own_ref.shape[1], own_ref.shape[2])
+    table = jnp.concatenate([own_ref[...].reshape(flat), taken_ref[...].reshape(flat)], axis=0)
+    high, middle, low = thirds(table)
+    chosen = select[...]
+    out_ref[...] = mul(chosen, high) + mul(chosen, middle) + mul(chosen, low)
+
+
+def pick(group, code, expert_rows, taken):
+    exp_dev, capacity, half = taken.shape
+    steps = half // BLOCK
+    count = code.shape[0]
+    slots = 2 * exp_dev * capacity
+    block = (exp_dev, capacity, BLOCK)
+    return pl.pallas_call(
+        pick_kernel,
+        out_shape=jax.ShapeDtypeStruct((count, half), jnp.float32),
+        grid_spec=pltpu.PrefetchScalarGridSpec(
+            num_scalar_prefetch=1,
+            grid=(steps,),
+            in_specs=[
+                pl.BlockSpec((count, 1), lambda i, g: (0, 0)),
+                pl.BlockSpec(block, lambda i, g: (0, 0, g[0] * steps + i)),
+                pl.BlockSpec(block, lambda i, g: (0, 0, i)),
+            ],
+            out_specs=pl.BlockSpec((count, BLOCK), lambda i, g: (0, i)),
+            scratch_shapes=[pltpu.VMEM((count, slots), jnp.bfloat16)],
+        ),
+        compiler_params=pltpu.CompilerParams(vmem_limit_bytes=VMEM),
+        cost_estimate=pl.CostEstimate(
+            flops=6 * count * slots * half, bytes_accessed=4 * (slots + count) * half, transcendentals=0
+        ),
+        name="pick",
+    )(group, code, expert_rows, taken)
+
+
+def combine_kernel(mix_ref, rows_ref, out_ref):
+    m_high, m_middle, m_low = thirds(mix_ref[...])
+    r_high, r_middle, r_low = thirds(rows_ref[...])
+    small = mul(m_low, r_high) + mul(m_middle, r_middle) + mul(m_high, r_low)
+    small += mul(m_middle, r_high) + mul(m_high, r_middle)
+    out_ref[...] = small + mul(m_high, r_high)
+
+
+def combine(mix, rows):
+    count, depth = mix.shape
+    half = rows.shape[1]
+    return pl.pallas_call(
+        combine_kernel,
+        out_shape=jax.ShapeDtypeStruct((count, half), jnp.float32),
+        grid=(half // BLOCK,),
+        in_specs=[
+            pl.BlockSpec((count, depth), lambda i: (0, 0)),
+            pl.BlockSpec((depth, BLOCK), lambda i: (0, i)),
+        ],
+        out_specs=pl.BlockSpec((count, BLOCK), lambda i: (0, i)),
+        compiler_params=pltpu.CompilerParams(vmem_limit_bytes=VMEM),
+        cost_estimate=pl.CostEstimate(
+            flops=12 * count * depth * half, bytes_accessed=4 * (count + depth) * half, transcendentals=0
+        ),
+        name="combine",
+    )(mix, rows)
 
 
 def shift(count, by):
@@ -26,10 +110,8 @@
     per_group = exp_dev * ep_count
     experts = 2 * per_group
 
-    own = lax.dynamic_slice_in_dim(expert_rows, group * half, half, 2)
     given = lax.dynamic_slice_in_dim(expert_rows, (1 - group) * half, half, 2)
     taken = lax.ppermute(given, "grp", [(0, 1), (1, 0)])
-    table = jnp.concatenate([own, taken], axis=0).reshape(held * capacity, half)
 
     real = route_ids < experts
     ids_t = route_ids.T
@@ -43,7 +125,11 @@
         (((0,), (0,)), ((), ())), preferred_element_type=jnp.float32,
     )
     chosen = lax.all_to_all(flags[:, None, :], EP, 0, 0, tiled=True).reshape(ep_count, 128)
-    chosen = chosen.astype(jnp.bfloat16)
+    pair = jnp.concatenate([route_ids.astype(jnp.float32), route_weights], axis=1)
+    pairs = jnp.concatenate(
+        [pair] + [lax.ppermute(pair, "zh", shift(far, -o)) for o in range(1, far)], axis=0
+    )
+    chosen, pairs = lax.optimization_barrier((chosen.astype(jnp.bfloat16), pairs))
 
     row = jnp.arange(ep_count * held, dtype=jnp.int32)[:, None]
     r_exp = row % held
@@ -58,15 +144,11 @@
     rank = jnp.sum(jnp.where(mine, before, 0.0), axis=1, keepdims=True)
     hit = jnp.sum(jnp.where(mine, here, 0.0), axis=1, keepdims=True)
     code = jnp.where(hit > 0, rank.astype(jnp.int32) + capacity * r_exp, -1)
-    select = (code == jnp.arange(held * capacity, dtype=jnp.int32)[None, :]).astype(jnp.float32)
-    outgoing = jnp.dot(select, table, precision=EXACT).reshape(near, far * held, half)
+    outgoing = pick(group.astype(jnp.int32).reshape(1), code, expert_rows, taken)
+    outgoing = outgoing.reshape(near, far * held, half)
 
     rows = lax.all_to_all(outgoing, NEAR, 0, 0, tiled=True).reshape(ep_count * held, half)
 
-    pair = jnp.concatenate([route_ids.astype(jnp.float32), route_weights], axis=1)
-    pairs = jnp.concatenate(
-        [pair] + [lax.ppermute(pair, "zh", shift(far, -o)) for o in range(1, far)], axis=0
-    )
     col = jnp.arange(ep_count * held, dtype=jnp.int32)[None, :]
     c_exp = col % held
     c_far = col // held % far
@@ -79,7 +161,7 @@
         mix = mix + jnp.where(pairs[:, k : k + 1] == c_id, pairs[:, top + k : top + k + 1], 0.0)
     line = jnp.arange(far * tok_dev, dtype=jnp.int32)[:, None]
     mix = jnp.where(line // tok_dev == c_far, mix, 0.0)
-    partial = jnp.dot(mix, rows, precision=EXACT).reshape(far, tok_dev, half)
+    partial = combine(mix, rows).reshape(far, tok_dev, half)
     cut = half // 2
     up, down = shift(far, 1), shift(far, -1)
     far_up = lax.ppermute(partial[2, :, :cut], "zh", up)

time: 185 us -> 193 us (1.043)
  the two profiles are of different devices: /device:TPU:58 before, /device:TPU:76 now
where the time goes in v3:
time: 193 us
  waiting for transfers between devices  120 us (62%)
  starting transfers between devices  44.7 us (23%)
  Pallas kernels  13.7 us (7%)
  local copies, waits for them, and re-layouts  8.54 us (4%)
  other arithmetic  3.63 us (2%)
    all_to_all x1, waiting for transfers between devices, shards(): lax.all_to_all(outgoing, NEAR, 0, 0, tiled=True)  104 us
    all_to_all x1, starting transfers between devices, shards(): lax.all_to_all(flags[:, None, :], EP, 0, 0, tiled=True)  11.3 us
    ppermute x3, starting transfers between devices, shards(): lax.ppermute(pair, 'zh', shift(far, -o))  9.6 us
    all_to_all x1, starting transfers between devices, shards(): lax.all_to_all(outgoing, NEAR, 0, 0, tiled=True)  7.47 us
    all_to_all x1, waiting for transfers between devices, shards(): lax.all_to_all(flags[:, None, :], EP, 0, 0, tiled=True)  7.36 us
    pallas_call x1, Pallas kernels, pick(): pl.pallas_call(pick_kernel, out_shape=jax.ShapeDtypeStruct((count, half),...  7.06 us
    pallas_call x1, Pallas kernels, combine(): pl.pallas_call(combine_kernel, out_shape=jax.ShapeDtypeStruct((count, hal...  6.64 us
    ppermute x1, starting transfers between devices, shards(): next_right = lax.ppermute(partial[1, :, cut:], 'zh', up)  5.93 us
  transfers between devices with their start and end apart: 12, of which 6 were waited for; matrix products, arithmetic and copies ran while one was open for 2% of the time, Pallas kernels for 0%

profile of v3, /device:TPU:76, one launch (start us, length us, event | category | flops | bytes accessed | tf_op | source)
XLA Modules:
  0.0 192.8 jit_solution(9979151899913995773)
XLA Ops:
  0.0 0.0 copy-start.3
  0.0 0.0 copy-start.4
  0.0 3.4 %constant_dynamic-slice_fusion = f32[2,96,3072]{2,1,0:T(8,128)} fusion(f32[2,96,6144]{2,1,0:T(8,128)} %own_ref.1, s32[]{:T(128)S(6)} %select_n.280), kind=kLoop, calls=%fused_computation.133 | loop fusion | bytes 4718596 | tf_op jit(solution)/shard_map/dynamic_slice | solution.py:113
  3.4 0.0 collective-permute-start.3
  3.4 0.0 copy-done.3
  3.4 0.0 copy-done.4
  3.4 0.1 collective-permute-start
  3.5 6.8 %collective-permute-start.1 = (f32[32,24]{0,1:T(8,128)S(1)}, f32[32,24]{0,1:T(8,128)S(1)}, u32[]{:S(2)}, u32[]{:S(2)}) collective-permute-start(f32[32,24]{0,1:T(8,128)S(1)} %pad_maximum_fusion), channel_id=1, source_target_pairs={{0,4},{2,6},{4,0},{6,2},{1,5},{3,7},{5,1},{7,3},{8,12},{10,14},{12... | collective-permute-start | bytes 9224 | tf_op jit(solution)/shard_map/ppermute | solution.py:130
  10.3 2.7 %collective-permute-start.2 = (f32[32,24]{0,1:T(8,128)S(1)}, f32[32,24]{0,1:T(8,128)S(1)}, u32[]{:S(2)}, u32[]{:S(2)}) collective-permute-start(f32[32,24]{0,1:T(8,128)S(1)} %pad_maximum_fusion), channel_id=1, source_target_pairs={{0,2},{2,4},{4,6},{6,0},{1,3},{3,5},{5,7},{7,1},{8,10},{10,12},{12... | collective-permute-start | bytes 9224 | tf_op jit(solution)/shard_map/ppermute | solution.py:130
  13.0 1.0 fusion.11
  14.1 11.3 %all-to-all-start = ((f32[128,1,128]{2,1,0:T(1,128)}), f32[128,1,128]{2,1,0:T(1,128)S(1)}, u32[]{:S(2)}, u32[]{:S(2)}) async-start(f32[128,1,128]{2,1,0:T(1,128)} %bitcast.3), calls=%async_computation | async-start | bytes 131072 | tf_op jit(solution)/shard_map/all_to_all | solution.py:127
  25.4 0.0 collective-permute-done
  25.4 0.0 collective-permute-done.1
  25.4 0.0 collective-permute-done.2
  25.4 0.1 pad_maximum_fusion.1
  25.5 7.4 %all-to-all-done = f32[128,1,128]{2,1,0:T(1,128)S(1)} async-done(((f32[128,1,128]{2,1,0:T(1,128)}), f32[128,1,128]{2,1,0:T(1,128)S(1)}, u32[]{:S(2)}, u32[]{:S(2)}) %all-to-all-start) | async-done | bytes 65568 | tf_op jit(solution)/shard_map/all_to_all | solution.py:127
  32.9 0.3 fusion.1
  33.2 0.1 copy.12
  33.4 0.3 fusion
  33.7 0.1 fusion.5.code_ref
  33.8 0.0 collective-permute-done.3.taken_ref
  33.8 0.0 copy-start.1
  33.9 2.3 %copy-done.1 = f32[2,96,6144]{2,1,0:T(8,128)S(1)} copy-done((f32[2,96,6144]{2,1,0:T(8,128)S(1)}, f32[2,96,6144]{2,1,0:T(8,128)}, u32[]{:S(2)}) %copy-start.1) | copy-done | bytes 4718616
  36.2 7.1 %pick.1 = f32[512,3072]{1,0:T(8,128)S(1)} custom-call(s32[1]{0:T(128)} %bitcast.30.group_ref, s32[512,1]{1,0:T(8,128)S(1)} %fusion.5.code_ref, f32[2,96,6144]{2,1,0:T(8,128)S(1)} %copy-done.1, f32[2,96,3072]{2,1,0:T(8,128)S(1)} %collective-permute-done.3.taken_ref), custom_call_target="tpu_custom_call" | custom-call | flops 3623878656 | bytes 11010048 | tf_op jit(solution)/shard_map/pick/pallas_call | solution.py:46
  43.3 0.0 copy-start
  43.3 2.6 %copy-done = f32[512,3072]{1,0:T(8,128)} copy-done((f32[512,3072]{1,0:T(8,128)}, f32[512,3072]{1,0:T(8,128)S(1)}, u32[]{:S(2)}) %copy-start) | copy-done | bytes 6291480
  45.9 7.5 %all-to-all-start.1 = ((f32[32,16,3072]{2,1,0:T(8,128)}), f32[32,16,3072]{2,1,0:T(8,128)}, u32[]{:S(2)}, u32[]{:S(2)}) async-start(f32[32,16,3072]{2,1,0:T(8,128)} %bitcast.111), calls=%async_computation.1 | async-start | bytes 12582912 | tf_op jit(solution)/shard_map/all_to_all | solution.py:150
  53.4 0.5 add_select_fusion.1.mix_ref
  53.9 104.1 %all-to-all-done.1 = f32[32,16,3072]{2,1,0:T(8,128)} async-done(((f32[32,16,3072]{2,1,0:T(8,128)}), f32[32,16,3072]{2,1,0:T(8,128)}, u32[]{:S(2)}, u32[]{:S(2)}) %all-to-all-start.1) | async-done | bytes 6291488 | tf_op jit(solution)/shard_map/all_to_all | solution.py:150
  158.0 6.6 %combine.1 = f32[128,3072]{1,0:T(8,128)S(1)} custom-call(f32[128,512]{1,0:T(8,128)S(1)} %add_select_fusion.1.mix_ref, f32[512,3072]{1,0:T(8,128)} %bitcast.33.rows_ref), custom_call_target="tpu_custom_call" | custom-call | flops 2415919104 | bytes 7864320 | tf_op jit(solution)/shard_map/combine/pallas_call | solution.py:79
  164.6 0.0 copy-start.2
  164.7 0.1 slice_bitcast_fusion.3
  164.7 2.9 %collective-permute-start.4 = (f32[32,1536]{1,0:T(8,128)S(1)}, f32[32,1536]{1,0:T(8,128)S(1)}, u32[]{:S(2)}, u32[]{:S(2)}) collective-permute-start(f32[32,1536]{1,0:T(8,128)S(1)} %get-tuple-element.12), channel_id=1, source_target_pairs={{0,2},{2,4},{4,6},{6,0},{1,3},{3,5},{5,7},{7,1},{8,10},{10,12},{12... | collective-permute-start | bytes 589832 | tf_op jit(solution)/shard_map/ppermute | solution.py:167
  167.6 1.7 collective-permute-start.8
  169.3 4.0 %collective-permute-start.6 = (f32[32,1536]{1,0:T(8,128)S(1)}, f32[32,1536]{1,0:T(8,128)S(1)}, u32[]{:S(2)}, u32[]{:S(2)}) collective-permute-start(f32[32,1536]{1,0:T(8,128)S(1)} %get-tuple-element.9), channel_id=1, source_target_pairs={{0,6},{2,0},{4,2},{6,4},{1,7},{3,1},{5,3},{7,5},{8,14},{10,8},{12,... | collective-permute-start | bytes 589832 | tf_op jit(solution)/shard_map/ppermute | solution.py:170
  173.4 1.5 collective-permute-done.4
  174.9 0.5 collective-permute-done.8
  175.4 0.1 fusion.10
  175.4 1.7 collective-permute-start.5
  177.1 5.9 %collective-permute-start.7 = (f32[32,1536]{1,0:T(8,128)S(1)}, f32[32,1536]{1,0:T(8,128)S(1)}, u32[]{:S(2)}, u32[]{:S(2)}) collective-permute-start(f32[32,1536]{1,0:T(8,128)S(1)} %get-tuple-element.11), channel_id=1, source_target_pairs={{0,2},{2,4},{4,6},{6,0},{1,3},{3,5},{5,7},{7,1},{8,10},{10,12},{12... | collective-permute-start | bytes 589832 | tf_op jit(solution)/shard_map/ppermute | solution.py:169
  183.1 0.0 collective-permute-start.9
  183.1 0.0 collective-permute-done.6
  183.1 0.0 collective-permute-done.5
  183.1 1.0 add.304
  184.1 2.2 %collective-permute-done.7 = f32[32,1536]{1,0:T(8,128)S(1)} collective-permute-done((f32[32,1536]{1,0:T(8,128)S(1)}, f32[32,1536]{1,0:T(8,128)S(1)}, u32[]{:S(2)}, u32[]{:S(2)}) %collective-permute-start.7) | collective-permute-done | bytes 196640 | tf_op jit(solution)/shard_map/ppermute | solution.py:169
  186.3 4.7 %collective-permute-done.9 = f32[32,1536]{1,0:T(8,128)} collective-permute-done((f32[32,1536]{1,0:T(8,128)S(1)}, f32[32,1536]{1,0:T(8,128)}, u32[]{:S(2)}, u32[]{:S(2)}) %collective-permute-start.9) | collective-permute-done | bytes 196640 | tf_op jit(solution)/shard_map/ppermute | solution.py:172
  191.0 0.9 add.306
  191.9 0.0 copy-done.2
  191.9 0.9 fusion.2
  (12 shorter events, 0.1 us)
Async XLA Ops:
  0.0 3.4 %copy-start.3 = (s32[32,12]{0,1:T(8,128)S(1)}, s32[32,12]{0,1:T(8,128)}, u32[]{:S(2)}) copy-start(s32[32,12]{0,1:T(8,128)} %param.5) | copy-start | bytes 4612
  0.0 3.4 %copy-start.4 = (f32[32,12]{0,1:T(8,128)S(1)}, f32[32,12]{0,1:T(8,128)}, u32[]{:S(2)}) copy-start(f32[32,12]{0,1:T(8,128)} %param.6) | copy-start | bytes 4612
  3.4 30.5 %collective-permute-start.3 = (f32[2,96,3072]{2,1,0:T(8,128)}, f32[2,96,3072]{2,1,0:T(8,128)S(1)}, u32[]{:S(2)}, u32[]{:S(2)}) collective-permute-start(f32[2,96,3072]{2,1,0:T(8,128)} %constant_dynamic-slice_fusion), channel_id=1, source_target_pairs={{0,128},{128,0},{1,129},{129,1},{2,130},{130,2},{3,131},{131,3},{4... | collective-permute-start | bytes 7077896 | tf_op jit(solution)/shard_map/ppermute | solution.py:114
  3.4 22.0 %collective-permute-start = (f32[32,24]{0,1:T(8,128)S(1)}, f32[32,24]{0,1:T(8,128)S(1)}, u32[]{:S(2)}, u32[]{:S(2)}) collective-permute-start(f32[32,24]{0,1:T(8,128)S(1)} %pad_maximum_fusion), channel_id=1, source_target_pairs={{0,6},{2,0},{4,2},{6,4},{1,7},{3,1},{5,3},{7,5},{8,14},{10,8},{12,... | collective-permute-start | bytes 9224 | tf_op jit(solution)/shard_map/ppermute | solution.py:130
  3.5 21.9 %collective-permute-start.1 = (f32[32,24]{0,1:T(8,128)S(1)}, f32[32,24]{0,1:T(8,128)S(1)}, u32[]{:S(2)}, u32[]{:S(2)}) collective-permute-start(f32[32,24]{0,1:T(8,128)S(1)} %pad_maximum_fusion), channel_id=1, source_target_pairs={{0,4},{2,6},{4,0},{6,2},{1,5},{3,7},{5,1},{7,3},{8,12},{10,14},{12... | collective-permute-start | bytes 9224 | tf_op jit(solution)/shard_map/ppermute | solution.py:130
  10.3 15.1 %collective-permute-start.2 = (f32[32,24]{0,1:T(8,128)S(1)}, f32[32,24]{0,1:T(8,128)S(1)}, u32[]{:S(2)}, u32[]{:S(2)}) collective-permute-start(f32[32,24]{0,1:T(8,128)S(1)} %pad_maximum_fusion), channel_id=1, source_target_pairs={{0,2},{2,4},{4,6},{6,0},{1,3},{3,5},{5,7},{7,1},{8,10},{10,12},{12... | collective-permute-start | bytes 9224 | tf_op jit(solution)/shard_map/ppermute | solution.py:130
  14.1 18.8 %all-to-all-start = ((f32[128,1,128]{2,1,0:T(1,128)}), f32[128,1,128]{2,1,0:T(1,128)S(1)}, u32[]{:S(2)}, u32[]{:S(2)}) async-start(f32[128,1,128]{2,1,0:T(1,128)} %bitcast.3), calls=%async_computation | async-start | bytes 131072 | tf_op jit(solution)/shard_map/all_to_all | solution.py:127
  33.8 2.3 %copy-start.1 = (f32[2,96,6144]{2,1,0:T(8,128)S(1)}, f32[2,96,6144]{2,1,0:T(8,128)}, u32[]{:S(2)}) copy-start(f32[2,96,6144]{2,1,0:T(8,128)} %own_ref.1) | copy-start | bytes 14155780
  43.3 2.6 %copy-start = (f32[512,3072]{1,0:T(8,128)}, f32[512,3072]{1,0:T(8,128)S(1)}, u32[]{:S(2)}) copy-start(f32[512,3072]{1,0:T(8,128)S(1)} %pick.1) | copy-start | bytes 18874372
  45.9 112.1 %all-to-all-start.1 = ((f32[32,16,3072]{2,1,0:T(8,128)}), f32[32,16,3072]{2,1,0:T(8,128)}, u32[]{:S(2)}, u32[]{:S(2)}) async-start(f32[32,16,3072]{2,1,0:T(8,128)} %bitcast.111), calls=%async_computation.1 | async-start | bytes 12582912 | tf_op jit(solution)/shard_map/all_to_all | solution.py:150
  164.6 27.3 %copy-start.2 = (f32[32,6144]{1,0:T(8,128)S(1)}, f32[32,6144]{1,0:T(8,128)}, u32[]{:S(2)}) copy-start(f32[32,6144]{1,0:T(8,128)} %param.4) | copy-start | bytes 2359300
  164.7 10.2 %collective-permute-start.4 = (f32[32,1536]{1,0:T(8,128)S(1)}, f32[32,1536]{1,0:T(8,128)S(1)}, u32[]{:S(2)}, u32[]{:S(2)}) collective-permute-start(f32[32,1536]{1,0:T(8,128)S(1)} %get-tuple-element.12), channel_id=1, source_target_pairs={{0,2},{2,4},{4,6},{6,0},{1,3},{3,5},{5,7},{7,1},{8,10},{10,12},{12... | collective-permute-start | bytes 589832 | tf_op jit(solution)/shard_map/ppermute | solution.py:167
  167.6 7.8 %collective-permute-start.8 = (f32[32,1536]{1,0:T(8,128)S(1)}, f32[32,1536]{1,0:T(8,128)S(1)}, u32[]{:S(2)}, u32[]{:S(2)}) collective-permute-start(f32[32,1536]{1,0:T(8,128)S(1)} %get-tuple-element.10), channel_id=1, source_target_pairs={{0,6},{2,0},{4,2},{6,4},{1,7},{3,1},{5,3},{7,5},{8,14},{10,8},{12,... | collective-permute-start | bytes 589832 | tf_op jit(solution)/shard_map/ppermute | solution.py:168
  169.3 13.8 %collective-permute-start.6 = (f32[32,1536]{1,0:T(8,128)S(1)}, f32[32,1536]{1,0:T(8,128)S(1)}, u32[]{:S(2)}, u32[]{:S(2)}) collective-permute-start(f32[32,1536]{1,0:T(8,128)S(1)} %get-tuple-element.9), channel_id=1, source_target_pairs={{0,6},{2,0},{4,2},{6,4},{1,7},{3,1},{5,3},{7,5},{8,14},{10,8},{12,... | collective-permute-start | bytes 589832 | tf_op jit(solution)/shard_map/ppermute | solution.py:170
  175.4 7.7 %collective-permute-start.5 = (f32[32,1536]{1,0:T(8,128)S(1)}, f32[32,1536]{1,0:T(8,128)}, u32[]{:S(2)}, u32[]{:S(2)}) collective-permute-start(f32[32,1536]{1,0:T(8,128)S(1)} %get-tuple-element.13), channel_id=1, source_target_pairs={{0,2},{2,4},{4,6},{6,0},{1,3},{3,5},{5,7},{7,1},{8,10},{10,12},{12... | collective-permute-start | bytes 589832 | tf_op jit(solution)/shard_map/ppermute | solution.py:171
  177.1 9.1 %collective-permute-start.7 = (f32[32,1536]{1,0:T(8,128)S(1)}, f32[32,1536]{1,0:T(8,128)S(1)}, u32[]{:S(2)}, u32[]{:S(2)}) collective-permute-start(f32[32,1536]{1,0:T(8,128)S(1)} %get-tuple-element.11), channel_id=1, source_target_pairs={{0,2},{2,4},{4,6},{6,0},{1,3},{3,5},{5,7},{7,1},{8,10},{10,12},{12... | collective-permute-start | bytes 589832 | tf_op jit(solution)/shard_map/ppermute | solution.py:169
  183.1 7.9 %collective-permute-start.9 = (f32[32,1536]{1,0:T(8,128)S(1)}, f32[32,1536]{1,0:T(8,128)}, u32[]{:S(2)}, u32[]{:S(2)}) collective-permute-start(f32[32,1536]{1,0:T(8,128)S(1)} %get-tuple-element.14), channel_id=1, source_target_pairs={{0,6},{2,0},{4,2},{6,4},{1,7},{3,1},{5,3},{7,5},{8,14},{10,8},{12,... | collective-permute-start | bytes 589832 | tf_op jit(solution)/shard_map/ppermute | solution.py:172

commit v4 on v3

v4 whole, which is shorter than its diff:
```python
import jax
import jax.numpy as jnp
from jax import lax
from jax.sharding import Mesh
from jax.sharding import PartitionSpec as P
from jax.experimental import pallas as pl
from jax.experimental.pallas import tpu as pltpu

EP = ("x", "y", "zh", "zl")
NEAR = ("x", "y", "zl")
BLOCK = 512
PICK_VMEM = 20 * 1024 * 1024
MIX_VMEM = 16 * 1024 * 1024


def halves(x):
    high = x.astype(jnp.bfloat16)
    rest = x - high.astype(jnp.float32)
    middle = rest.astype(jnp.bfloat16)
    return high, middle, rest - middle.astype(jnp.float32)


def mul(a, b):
    return jnp.dot(a, b, preferred_element_type=jnp.float32)


def pick_kernel(group_ref, code_ref, own_ref, taken_ref, out_ref, select):
    @pl.when(pl.program_id(0) == 0)
    def _():
        slot = lax.broadcasted_iota(jnp.int32, select.shape, 1)
        select[...] = (code_ref[...] == slot).astype(jnp.float32).astype(jnp.bfloat16)

    targets, rows, columns = out_ref.shape
    each = targets * rows // 2
    for part, ref in enumerate((own_ref, taken_ref)):
        table = ref[...].reshape(ref.shape[0] * ref.shape[1], columns)
        high, middle, rest = halves(table)
        chosen = select[part * each : (part + 1) * each, :]
        value = mul(chosen, high) + mul(chosen, middle) + mul(chosen, rest.astype(jnp.bfloat16))
        out_ref[:, part * rows // 2 : (part + 1) * rows // 2, :] = value.reshape(targets, rows // 2, columns)


def pick(group, code, own, taken, targets):
    exp_dev, capacity, width = own.shape
    half = width // 2
    steps = half // BLOCK
    count = code.shape[0]
    slots = exp_dev * capacity
    block = pl.BlockSpec((exp_dev, capacity, BLOCK), lambda i, g: (0, 0, g[0] * steps + i))
    return pl.pallas_call(
        pick_kernel,
        out_shape=jax.ShapeDtypeStruct((targets, count // targets, half), jnp.float32),
        grid_spec=pltpu.PrefetchScalarGridSpec(
            num_scalar_prefetch=1,
            grid=(steps,),
            in_specs=[pl.BlockSpec((count, 1), lambda i, g: (0, 0)), block, block],
            out_specs=pl.BlockSpec((targets, count // targets, BLOCK), lambda i, g: (0, 0, i)),
            scratch_shapes=[pltpu.VMEM((count, slots), jnp.bfloat16)],
        ),
        compiler_params=pltpu.CompilerParams(vmem_limit_bytes=PICK_VMEM),
        cost_estimate=pl.CostEstimate(
            flops=6 * count * slots * half, bytes_accessed=4 * (2 * slots + count) * half, transcendentals=0
        ),
        name="pick",
    )(group, code, own, taken)


def combine_kernel(pairs_ref, ids_ref, rows_ref, out_ref, mix):
    count = mix.shape[0] // 2

    @pl.when(pl.program_id(0) == 0)
    def _():
        pairs = pairs_ref[...].T
        top = pairs.shape[1] // 2
        ids = ids_ref[0:1, :]
        total = jnp.zeros((count, mix.shape[1]), jnp.float32)
        for k in range(top):
            total += jnp.where(pairs[:, k : k + 1] == ids, pairs[:, top + k : top + k + 1], 0.0)
        line = lax.broadcasted_iota(jnp.int32, total.shape, 0) * 4 // count
        total = jnp.where(line.astype(jnp.float32) == ids_ref[1:2, :], total, 0.0)
        high, middle, _ = halves(total)
        mix[:count, :] = high
        mix[count:, :] = middle

    high, middle, _ = halves(rows_ref[...])
    both = mul(mix[...], high)
    out_ref[...] = both[:count] + (both[count:] + mul(mix[:count, :], middle))


def combine(pairs, ids, rows):
    count = pairs.shape[1]
    depth, half = rows.shape
    return pl.pallas_call(
        combine_kernel,
        out_shape=jax.ShapeDtypeStruct((count, half), jnp.float32),
        grid=(half // BLOCK,),
        in_specs=[
            pl.BlockSpec(pairs.shape, lambda i: (0, 0)),
            pl.BlockSpec(ids.shape, lambda i: (0, 0)),
            pl.BlockSpec((depth, BLOCK), lambda i: (0, i)),
        ],
        out_specs=pl.BlockSpec((count, BLOCK), lambda i: (0, i)),
        scratch_shapes=[pltpu.VMEM((2 * count, depth), jnp.bfloat16)],
        compiler_params=pltpu.CompilerParams(vmem_limit_bytes=MIX_VMEM),
        cost_estimate=pl.CostEstimate(
            flops=6 * count * depth * half, bytes_accessed=4 * (count + depth) * half, transcendentals=0
        ),
        name="combine",
    )(pairs, ids, rows)


def shift(count, by):
    return [(i, (i + by) % count) for i in range(count)]


def shards(tokens, route_ids, route_weights, expert_rows):
    group = lax.axis_index("grp")
    ep_count = lax.axis_size(EP)
    far = lax.axis_size("zh")
    low = lax.axis_size("zl")
    near = ep_count // far
    tok_dev, top = route_ids.shape
    exp_dev, capacity, width = expert_rows.shape
    half = width // 2
    held = 2 * exp_dev
    per_group = exp_dev * ep_count
    experts = 2 * per_group

    taken = lax.ppermute(expert_rows, "grp", [(0, 1), (1, 0)])

    ids_t = route_ids.T
    chip = jnp.where(ids_t < experts, ids_t % per_group // exp_dev, -1)
    place = (ids_t // per_group != group) * exp_dev + ids_t % exp_dev
    lanes = jnp.arange(128, dtype=jnp.int32)
    chip_hot = (chip[:, :, None] == jnp.arange(ep_count, dtype=jnp.int32)).astype(jnp.bfloat16)
    place_hot = (place[:, :, None] == lanes).astype(jnp.bfloat16)
    flags = lax.dot_general(
        chip_hot.reshape(top * tok_dev, ep_count), place_hot.reshape(top * tok_dev, 128),
        (((0,), (0,)), ((), ())), preferred_element_type=jnp.float32,
    )
    chosen = lax.all_to_all(flags[:, None, :], EP, 0, 0, tiled=True).reshape(ep_count, 128)
    pair = jnp.concatenate([ids_t.astype(jnp.float32), route_weights.T], axis=0)
    pairs = jnp.concatenate(
        [pair] + [lax.ppermute(pair, "zh", shift(far, -o)) for o in range(1, far)], axis=1
    )
    chosen, pairs = lax.optimization_barrier((chosen.astype(jnp.bfloat16), pairs))

    row = jnp.arange(ep_count * held, dtype=jnp.int32)[:, None]
    r_side = row // (ep_count * exp_dev)
    r_near = row % (ep_count * exp_dev) // (far * exp_dev)
    r_far = row % (far * exp_dev) // exp_dev
    r_exp = row % exp_dev
    zh = lax.axis_index("zh")
    home = (r_near // low * far + (zh + r_far) % far) * low + r_near % low
    homes = jnp.arange(ep_count, dtype=jnp.int32)[None, :]
    before = mul((homes < home).astype(jnp.bfloat16), chosen)
    here = mul((homes == home).astype(jnp.bfloat16), chosen)
    mine = lanes[None, :] == r_side * exp_dev + r_exp
    rank = jnp.sum(jnp.where(mine, before, 0.0), axis=1, keepdims=True)
    hit = jnp.sum(jnp.where(mine, here, 0.0), axis=1, keepdims=True)
    code = jnp.where(hit > 0, rank.astype(jnp.int32) + capacity * r_exp, -1)

    col = jnp.arange(ep_count * held, dtype=jnp.int32)
    c_near = col // (held * far)
    c_side = col % (held * far) // (exp_dev * far)
    c_far = col % (exp_dev * far) // exp_dev
    c_chip = (c_near // low * far + zh) * low + c_near % low
    c_id = (c_side + group) % 2 * per_group + c_chip * exp_dev + col % exp_dev
    ids = jnp.stack([c_id, c_far]).astype(jnp.float32)
    code, ids = lax.optimization_barrier((code, ids))

    outgoing = pick(group.astype(jnp.int32).reshape(1), code, expert_rows, taken, near)
    outgoing, pairs, ids = lax.optimization_barrier((outgoing, pairs, ids))
    rows = lax.all_to_all(outgoing, NEAR, 0, 0, tiled=True)
    rows = rows.reshape(ep_count * held, half)
    partial = combine(pairs, ids, rows).reshape(far, tok_dev, half)
    partial, route_ids, route_weights = lax.optimization_barrier((partial, route_ids, route_weights))
    cut = half // 2
    up, down = shift(far, 1), shift(far, -1)
    far_up = lax.ppermute(partial[2, :, :cut], "zh", up)
    far_down = lax.ppermute(partial[2, :, cut:], "zh", down)
    next_right = lax.ppermute(partial[1, :, cut:], "zh", up)
    prev_left = lax.ppermute(partial[3, :, :cut], "zh", down)
    next_left = lax.ppermute(partial[1, :, :cut] + far_up, "zh", up)
    prev_right = lax.ppermute(partial[3, :, cut:] + far_down, "zh", down)
    total = partial[0] + jnp.concatenate([next_left + prev_left, next_right + prev_right], axis=1)

    ident = jnp.sum(jnp.where(route_ids < experts, 0.0, route_weights), axis=1, keepdims=True)
    return total + ident * lax.dynamic_slice_in_dim(tokens, group * half, half, 1)


def solution(mesh):
    torus = Mesh(mesh.devices.reshape(mesh.shape["grp"], 4, 4, 4, 2), ("grp",) + EP)
    in_specs = (P(EP, None), P(EP, None), P(EP, None), P(("grp",) + EP, None, None))
    return jax.shard_map(
        shards, mesh=torus, in_specs=in_specs, out_specs=P(EP, "grp"), check_vma=False
    )
```

time: 193 us -> 156 us (0.81)
  the two profiles are of different devices: /device:TPU:76 before, /device:TPU:32 now
where the time goes in v4:
time: 156 us; the launch traced here: 155 us
  blocking collectives  76.2 us (49%)
  starting transfers between devices  33.5 us (21%)
  waiting for transfers between devices  25.5 us (16%)
  Pallas kernels  9.55 us (6%)
  other arithmetic  5.96 us (4%)
  local copies, waits for them, and re-layouts  2.54 us (2%)
  matrix products  1.68 us (1%)
    all_to_all x1, blocking collectives, shards(): rows = lax.all_to_all(outgoing, NEAR, 0, 0, tiled=True)  76.2 us
    ppermute x3, starting transfers between devices, shards(): lax.ppermute(pair, 'zh', shift(far, -o))  10.4 us
    all_to_all x1, waiting for transfers between devices, shards(): lax.all_to_all(flags[:, None, :], EP, 0, 0, tiled=True)  10.2 us
    all_to_all x1, starting transfers between devices, shards(): lax.all_to_all(flags[:, None, :], EP, 0, 0, tiled=True)  9.73 us
    ppermute x1, waiting for transfers between devices, shards(): next_left = lax.ppermute(partial[1, :, :cut] + far_up, 'zh', up)  7 us
    pallas_call x1, Pallas kernels, pick(): pl.pallas_call(pick_kernel, out_shape=jax.ShapeDtypeStruct((targets, coun...  5.97 us
    ppermute x1, waiting for transfers between devices, shards(): far_down = lax.ppermute(partial[2, :, cut:], 'zh', down)  5.78 us
    ppermute x1, starting transfers between devices, shards(): prev_right = lax.ppermute(partial[3, :, cut:] + far_down, 'zh', down)  3.73 us
  transfers between devices with their start and end apart: 11, of which 5 were waited for; matrix products, arithmetic and copies ran while one was open for 4% of the time, Pallas kernels for 0%

profile of v4, /device:TPU:32, one launch (start us, length us, event | category | flops | bytes accessed | tf_op | source)
XLA Modules:
  0.0 155.2 jit_solution(14242194578561798988)
XLA Ops:
  0.0 0.0 collective-permute-start.3
  0.0 0.7 bitcast_convert_fusion
  0.7 0.7 pad_maximum_fusion
  1.4 3.3 %collective-permute-start.2 = (f32[24,32]{1,0:T(8,128)S(1)}, f32[24,32]{1,0:T(8,128)S(1)}, u32[]{:S(2)}, u32[]{:S(2)}) collective-permute-start(f32[24,32]{1,0:T(8,128)S(1)} %pad_maximum_fusion), channel_id=1, source_target_pairs={{0,2},{2,4},{4,6},{6,0},{1,3},{3,5},{5,7},{7,1},{8,10},{10,12},{12... | collective-permute-start | bytes 9224 | tf_op jit(solution)/shard_map/ppermute | solution.py:144
  4.7 4.5 %collective-permute-start.1 = (f32[24,32]{1,0:T(8,128)S(1)}, f32[24,32]{1,0:T(8,128)S(1)}, u32[]{:S(2)}, u32[]{:S(2)}) collective-permute-start(f32[24,32]{1,0:T(8,128)S(1)} %pad_maximum_fusion), channel_id=1, source_target_pairs={{0,4},{2,6},{4,0},{6,2},{1,5},{3,7},{5,1},{7,3},{8,12},{10,14},{12... | collective-permute-start | bytes 9224 | tf_op jit(solution)/shard_map/ppermute | solution.py:144
  9.2 2.7 %collective-permute-start = (f32[24,32]{1,0:T(8,128)S(1)}, f32[24,32]{1,0:T(8,128)S(1)}, u32[]{:S(2)}, u32[]{:S(2)}) collective-permute-start(f32[24,32]{1,0:T(8,128)S(1)} %pad_maximum_fusion), channel_id=1, source_target_pairs={{0,6},{2,0},{4,2},{6,4},{1,7},{3,1},{5,3},{7,5},{8,14},{10,8},{12,... | collective-permute-start | bytes 9224 | tf_op jit(solution)/shard_map/ppermute | solution.py:144
  11.8 0.7 fusion.15
  12.6 1.0 fusion.9
  13.6 9.7 %all-to-all-start = ((f32[128,1,128]{2,1,0:T(1,128)}), f32[128,1,128]{2,1,0:T(1,128)S(1)}, u32[]{:S(2)}, u32[]{:S(2)}) async-start(f32[128,1,128]{2,1,0:T(1,128)} %bitcast.4), calls=%async_computation | async-start | bytes 131072 | tf_op jit(solution)/shard_map/all_to_all | solution.py:141
  23.4 0.0 collective-permute-done.2
  23.4 0.0 collective-permute-done.1
  23.4 0.0 collective-permute-done
  23.5 0.8 pad_maximum_fusion.1.pairs_ref
  24.2 10.2 %all-to-all-done = f32[128,1,128]{2,1,0:T(1,128)S(1)} async-done(((f32[128,1,128]{2,1,0:T(1,128)}), f32[128,1,128]{2,1,0:T(1,128)S(1)}, u32[]{:S(2)}, u32[]{:S(2)}) %all-to-all-start) | async-done | bytes 65568 | tf_op jit(solution)/shard_map/all_to_all | solution.py:141
  34.4 0.3 fusion.1
  34.7 0.1 copy.12
  34.9 0.3 fusion
  35.2 0.1 fusion.5.code_ref
  35.4 0.0 collective-permute-done.3.taken_ref
  35.4 0.0 copy-start
  35.4 2.3 %copy-done = f32[2,96,6144]{2,1,0:T(8,128)S(1)} copy-done((f32[2,96,6144]{2,1,0:T(8,128)S(1)}, f32[2,96,6144]{2,1,0:T(8,128)}, u32[]{:S(2)}) %copy-start) | copy-done | bytes 4718616
  37.7 6.0 %pick.1 = f32[32,16,3072]{2,1,0:T(8,128)S(1)} custom-call(s32[1]{0:T(128)} %bitcast.group_ref, s32[512,1]{1,0:T(8,128)S(1)} %fusion.5.code_ref, f32[2,96,6144]{2,1,0:T(8,128)S(1)} %copy-done, f32[2,96,6144]{2,1,0:T(8,128)} %collective-permute-done.3.taken_ref), custom_call_target="tpu_custom_call" | custom-call | flops 1811939328 | bytes 11010048 | tf_op jit(solution)/shard_map/pick/pallas_call | solution.py:50
  43.7 76.2 %all_to_all.10 = f32[32,16,3072]{2,1,0:T(8,128)S(1)} all-to-all(f32[32,16,3072]{2,1,0:T(8,128)S(1)} %pick.1), channel_id=1, replica_groups=mesh['grp'=2,'x'=4,'y'=4,'zh'=4,'zl'=2] {'x','y','zl'}, dimensions={0} | all-to-all | bytes 12582912 | tf_op jit(solution)/shard_map/all_to_all | solution.py:174
  119.9 0.0 copy-start.2
  119.9 0.0 copy-start.3
  119.9 0.0 copy-start.1
  119.9 3.6 %combine.1 = f32[128,3072]{1,0:T(8,128)S(1)} custom-call(f32[24,128]{1,0:T(8,128)S(1)} %pad_maximum_fusion.1.pairs_ref, f32[2,512]{1,0:T(2,128)S(1)} %add_convert_fusion.ids_ref, f32[512,3072]{1,0:T(8,128)S(1)} %bitcast.62), custom_call_target="tpu_custom_call" | custom-call | flops 1207959552 | bytes 7864320 | tf_op jit(solution)/shard_map/combine/pallas_call | solution.py:93
  123.5 0.1 slice_bitcast_fusion.2
  123.6 2.0 %collective-permute-start.8 = (f32[32,1536]{1,0:T(8,128)S(1)}, f32[32,1536]{1,0:T(8,128)S(1)}, u32[]{:S(2)}, u32[]{:S(2)}) collective-permute-start(f32[32,1536]{1,0:T(8,128)S(1)} %get-tuple-element.26), channel_id=1, source_target_pairs={{0,6},{2,0},{4,2},{6,4},{1,7},{3,1},{5,3},{7,5},{8,14},{10,8},{12,... | collective-permute-start | bytes 589832 | tf_op jit(solution)/shard_map/ppermute | solution.py:181
  125.5 1.0 collective-permute-start.4
  126.6 3.1 %collective-permute-start.6 = (f32[32,1536]{1,0:T(8,128)S(1)}, f32[32,1536]{1,0:T(8,128)S(1)}, u32[]{:S(2)}, u32[]{:S(2)}) collective-permute-start(f32[32,1536]{1,0:T(8,128)S(1)} %get-tuple-element.25), channel_id=1, source_target_pairs={{0,6},{2,0},{4,2},{6,4},{1,7},{3,1},{5,3},{7,5},{8,14},{10,8},{12,... | collective-permute-start | bytes 589832 | tf_op jit(solution)/shard_map/ppermute | solution.py:183
  129.7 5.8 %collective-permute-done.8 = f32[32,1536]{1,0:T(8,128)S(1)} collective-permute-done((f32[32,1536]{1,0:T(8,128)S(1)}, f32[32,1536]{1,0:T(8,128)S(1)}, u32[]{:S(2)}, u32[]{:S(2)}) %collective-permute-start.8) | collective-permute-done | bytes 196640 | tf_op jit(solution)/shard_map/ppermute | solution.py:181
  135.4 0.0 collective-permute-done.4
  135.4 0.1 bitcast_add_fusion.1
  135.5 3.2 %collective-permute-start.5 = (f32[32,1536]{1,0:T(8,128)S(1)}, f32[32,1536]{1,0:T(8,128)}, u32[]{:S(2)}, u32[]{:S(2)}) collective-permute-start(f32[32,1536]{1,0:T(8,128)S(1)} %get-tuple-element.29), channel_id=1, source_target_pairs={{0,2},{2,4},{4,6},{6,0},{1,3},{3,5},{5,7},{7,1},{8,10},{10,12},{12... | collective-permute-start | bytes 589832 | tf_op jit(solution)/shard_map/ppermute | solution.py:184
  138.7 0.4 collective-permute-start.7
  139.1 3.7 %collective-permute-start.9 = (f32[32,1536]{1,0:T(8,128)S(1)}, f32[32,1536]{1,0:T(8,128)}, u32[]{:S(2)}, u32[]{:S(2)}) collective-permute-start(f32[32,1536]{1,0:T(8,128)S(1)} %get-tuple-element.30), channel_id=1, source_target_pairs={{0,6},{2,0},{4,2},{6,4},{1,7},{3,1},{5,3},{7,5},{8,14},{10,8},{12,... | collective-permute-start | bytes 589832 | tf_op jit(solution)/shard_map/ppermute | solution.py:185
  142.8 0.0 copy-done.2
  142.8 0.0 copy-done.3
  142.8 1.5 collective-permute-done.6
  144.3 7.0 %collective-permute-done.5 = f32[32,1536]{1,0:T(8,128)} collective-permute-done((f32[32,1536]{1,0:T(8,128)S(1)}, f32[32,1536]{1,0:T(8,128)}, u32[]{:S(2)}, u32[]{:S(2)}) %collective-permute-start.5) | collective-permute-done | bytes 196640 | tf_op jit(solution)/shard_map/ppermute | solution.py:184
  151.3 0.9 add.340
  152.3 1.0 collective-permute-done.7
  153.3 0.0 collective-permute-done.9
  153.4 1.0 add.342
  154.3 0.0 copy-done.1
  154.3 0.9 fusion.2
  (7 shorter events, 0.1 us)
Async XLA Ops:
  0.0 35.4 %collective-permute-start.3 = (f32[2,96,6144]{2,1,0:T(8,128)}, f32[2,96,6144]{2,1,0:T(8,128)}, u32[]{:S(2)}, u32[]{:S(2)}) collective-permute-start(f32[2,96,6144]{2,1,0:T(8,128)} %own_ref.1), channel_id=1, source_target_pairs={{0,128},{128,0},{1,129},{129,1},{2,130},{130,2},{3,131},{131,3},{4... | collective-permute-start | bytes 14155784 | tf_op jit(solution)/shard_map/ppermute | solution.py:129
  1.4 22.0 %collective-permute-start.2 = (f32[24,32]{1,0:T(8,128)S(1)}, f32[24,32]{1,0:T(8,128)S(1)}, u32[]{:S(2)}, u32[]{:S(2)}) collective-permute-start(f32[24,32]{1,0:T(8,128)S(1)} %pad_maximum_fusion), channel_id=1, source_target_pairs={{0,2},{2,4},{4,6},{6,0},{1,3},{3,5},{5,7},{7,1},{8,10},{10,12},{12... | collective-permute-start | bytes 9224 | tf_op jit(solution)/shard_map/ppermute | solution.py:144
  4.7 18.8 %collective-permute-start.1 = (f32[24,32]{1,0:T(8,128)S(1)}, f32[24,32]{1,0:T(8,128)S(1)}, u32[]{:S(2)}, u32[]{:S(2)}) collective-permute-start(f32[24,32]{1,0:T(8,128)S(1)} %pad_maximum_fusion), channel_id=1, source_target_pairs={{0,4},{2,6},{4,0},{6,2},{1,5},{3,7},{5,1},{7,3},{8,12},{10,14},{12... | collective-permute-start | bytes 9224 | tf_op jit(solution)/shard_map/ppermute | solution.py:144
  9.2 14.3 %collective-permute-start = (f32[24,32]{1,0:T(8,128)S(1)}, f32[24,32]{1,0:T(8,128)S(1)}, u32[]{:S(2)}, u32[]{:S(2)}) collective-permute-start(f32[24,32]{1,0:T(8,128)S(1)} %pad_maximum_fusion), channel_id=1, source_target_pairs={{0,6},{2,0},{4,2},{6,4},{1,7},{3,1},{5,3},{7,5},{8,14},{10,8},{12,... | collective-permute-start | bytes 9224 | tf_op jit(solution)/shard_map/ppermute | solution.py:144
  13.6 20.8 %all-to-all-start = ((f32[128,1,128]{2,1,0:T(1,128)}), f32[128,1,128]{2,1,0:T(1,128)S(1)}, u32[]{:S(2)}, u32[]{:S(2)}) async-start(f32[128,1,128]{2,1,0:T(1,128)} %bitcast.4), calls=%async_computation | async-start | bytes 131072 | tf_op jit(solution)/shard_map/all_to_all | solution.py:141
  35.4 2.3 %copy-start = (f32[2,96,6144]{2,1,0:T(8,128)S(1)}, f32[2,96,6144]{2,1,0:T(8,128)}, u32[]{:S(2)}) copy-start(f32[2,96,6144]{2,1,0:T(8,128)} %own_ref.1) | copy-start | bytes 14155780
  119.9 22.9 %copy-start.2 = (s32[32,12]{0,1:T(8,128)S(1)}, s32[32,12]{0,1:T(8,128)}, u32[]{:S(2)}) copy-start(s32[32,12]{0,1:T(8,128)} %param.5) | copy-start | bytes 4612
  119.9 22.9 %copy-start.3 = (f32[32,12]{0,1:T(8,128)S(1)}, f32[32,12]{0,1:T(8,128)}, u32[]{:S(2)}) copy-start(f32[32,12]{0,1:T(8,128)} %param.6) | copy-start | bytes 4612
  119.9 34.4 %copy-start.1 = (f32[32,6144]{1,0:T(8,128)S(1)}, f32[32,6144]{1,0:T(8,128)}, u32[]{:S(2)}) copy-start(f32[32,6144]{1,0:T(8,128)} %param.4) | copy-start | bytes 2359300
  123.6 11.9 %collective-permute-start.8 = (f32[32,1536]{1,0:T(8,128)S(1)}, f32[32,1536]{1,0:T(8,128)S(1)}, u32[]{:S(2)}, u32[]{:S(2)}) collective-permute-start(f32[32,1536]{1,0:T(8,128)S(1)} %get-tuple-element.26), channel_id=1, source_target_pairs={{0,6},{2,0},{4,2},{6,4},{1,7},{3,1},{5,3},{7,5},{8,14},{10,8},{12,... | collective-permute-start | bytes 589832 | tf_op jit(solution)/shard_map/ppermute | solution.py:181
  125.5 9.9 %collective-permute-start.4 = (f32[32,1536]{1,0:T(8,128)S(1)}, f32[32,1536]{1,0:T(8,128)S(1)}, u32[]{:S(2)}, u32[]{:S(2)}) collective-permute-start(f32[32,1536]{1,0:T(8,128)S(1)} %get-tuple-element.28), channel_id=1, source_target_pairs={{0,2},{2,4},{4,6},{6,0},{1,3},{3,5},{5,7},{7,1},{8,10},{10,12},{12... | collective-permute-start | bytes 589832 | tf_op jit(solution)/shard_map/ppermute | solution.py:180
  126.6 17.8 %collective-permute-start.6 = (f32[32,1536]{1,0:T(8,128)S(1)}, f32[32,1536]{1,0:T(8,128)S(1)}, u32[]{:S(2)}, u32[]{:S(2)}) collective-permute-start(f32[32,1536]{1,0:T(8,128)S(1)} %get-tuple-element.25), channel_id=1, source_target_pairs={{0,6},{2,0},{4,2},{6,4},{1,7},{3,1},{5,3},{7,5},{8,14},{10,8},{12,... | collective-permute-start | bytes 589832 | tf_op jit(solution)/shard_map/ppermute | solution.py:183
  135.5 15.8 %collective-permute-start.5 = (f32[32,1536]{1,0:T(8,128)S(1)}, f32[32,1536]{1,0:T(8,128)}, u32[]{:S(2)}, u32[]{:S(2)}) collective-permute-start(f32[32,1536]{1,0:T(8,128)S(1)} %get-tuple-element.29), channel_id=1, source_target_pairs={{0,2},{2,4},{4,6},{6,0},{1,3},{3,5},{5,7},{7,1},{8,10},{10,12},{12... | collective-permute-start | bytes 589832 | tf_op jit(solution)/shard_map/ppermute | solution.py:184
  138.7 14.7 %collective-permute-start.7 = (f32[32,1536]{1,0:T(8,128)S(1)}, f32[32,1536]{1,0:T(8,128)S(1)}, u32[]{:S(2)}, u32[]{:S(2)}) collective-permute-start(f32[32,1536]{1,0:T(8,128)S(1)} %get-tuple-element.27), channel_id=1, source_target_pairs={{0,2},{2,4},{4,6},{6,0},{1,3},{3,5},{5,7},{7,1},{8,10},{10,12},{12... | collective-permute-start | bytes 589832 | tf_op jit(solution)/shard_map/ppermute | solution.py:182
  139.1 14.3 %collective-permute-start.9 = (f32[32,1536]{1,0:T(8,128)S(1)}, f32[32,1536]{1,0:T(8,128)}, u32[]{:S(2)}, u32[]{:S(2)}) collective-permute-start(f32[32,1536]{1,0:T(8,128)S(1)} %get-tuple-element.30), channel_id=1, source_target_pairs={{0,6},{2,0},{4,2},{6,4},{1,7},{3,1},{5,3},{7,5},{8,14},{10,8},{12,... | collective-permute-start | bytes 589832 | tf_op jit(solution)/shard_map/ppermute | solution.py:185

commit v5 on v4

v5 whole, which is shorter than its diff:
```python
import jax
import jax.numpy as jnp
from jax import lax
from jax.sharding import Mesh
from jax.sharding import PartitionSpec as P
from jax.experimental import pallas as pl
from jax.experimental.pallas import tpu as pltpu

EP = ("x", "y", "zh", "zl")
NEAR = ("x", "y", "zl")
BLOCK = 512
PICK_VMEM = 24 * 1024 * 1024
MIX_VMEM = 24 * 1024 * 1024


def halves(x):
    high = x.astype(jnp.bfloat16)
    rest = x - high.astype(jnp.float32)
    middle = rest.astype(jnp.bfloat16)
    return high, middle, rest - middle.astype(jnp.float32)


def mul(a, b):
    return jnp.dot(a, b, preferred_element_type=jnp.float32)


def pick_kernel(group_ref, chosen_ref, home_ref, lane_ref, own_ref, taken_ref, out_ref, held, arrived):
    sides, steps, exp_dev, capacity, block = held.shape
    start = pl.multiple_of(group_ref[0] * steps * block, block)
    copies = {}
    for i in range(steps):
        for side, ref in enumerate((own_ref, taken_ref)):
            copies[i, side] = pltpu.make_async_copy(
                ref.at[:, :, pl.ds(start + i * block, block)], held.at[side, i], arrived.at[side, i]
            )
            copies[i, side].start()

    chosen = chosen_ref[...].astype(jnp.bfloat16)
    count = home_ref.shape[0]
    homes = lax.broadcasted_iota(jnp.int32, (count, chosen.shape[0]), 1)
    before = mul((homes < home_ref[...]).astype(jnp.float32).astype(jnp.bfloat16), chosen)
    here = mul((homes == home_ref[...]).astype(jnp.float32).astype(jnp.bfloat16), chosen)
    lanes = lax.broadcasted_iota(jnp.int32, before.shape, 1)
    expert = lax.rem(lane_ref[...], exp_dev)
    code = jnp.where(here > 0, before.astype(jnp.int32) + capacity * expert, -1)
    code = jnp.sum(jnp.where(lanes == lane_ref[...], code, 0), axis=1, keepdims=True)
    slot = lax.broadcasted_iota(jnp.int32, (count, exp_dev * capacity), 1)
    select = (code == slot).astype(jnp.float32).astype(jnp.bfloat16)

    targets, rows, _ = out_ref.shape
    each = count // sides
    for i in range(steps):
        for side in range(sides):
            copies[i, side].wait()
            table = held[side, i].reshape(exp_dev * capacity, block)
            high, middle, rest = halves(table)
            mine = select[side * each : (side + 1) * each, :]
            value = mul(mine, high) + mul(mine, middle) + mul(mine, rest.astype(jnp.bfloat16))
            out_ref[:, side * rows // 2 : (side + 1) * rows // 2, i * block : (i + 1) * block] = value.reshape(
                targets, rows // 2, block
            )


def pick(group, chosen, home, lane, own, taken, targets):
    exp_dev, capacity, width = own.shape
    half = width // 2
    steps = half // BLOCK
    count = home.shape[0]
    slots = exp_dev * capacity
    vmem = pl.BlockSpec(memory_space=pltpu.VMEM)
    hbm = pl.BlockSpec(memory_space=pl.ANY)
    return pl.pallas_call(
        pick_kernel,
        out_shape=jax.ShapeDtypeStruct((targets, count // targets, half), jnp.float32),
        in_specs=[pl.BlockSpec(memory_space=pltpu.SMEM), vmem, vmem, vmem, hbm, hbm],
        out_specs=vmem,
        scratch_shapes=[
            pltpu.VMEM((2, steps, exp_dev, capacity, BLOCK), jnp.float32),
            pltpu.SemaphoreType.DMA((2, steps)),
        ],
        compiler_params=pltpu.CompilerParams(vmem_limit_bytes=PICK_VMEM),
        cost_estimate=pl.CostEstimate(
            flops=6 * count * slots * half, bytes_accessed=4 * (2 * slots + count) * half, transcendentals=0
        ),
        name="pick",
    )(group, chosen, home, lane, own, taken)


def combine_kernel(*refs):
    pair_refs, (ids_ref, rows_ref, out_ref) = refs[:-3], refs[-3:]
    pairs = jnp.concatenate([ref[...].T for ref in pair_refs], axis=0)
    count = pairs.shape[0]
    top = pairs.shape[1] // 2
    ids = ids_ref[0:1, :]
    total = jnp.zeros((count, rows_ref.shape[0]), jnp.float32)
    for k in range(top):
        total += jnp.where(pairs[:, k : k + 1] == ids, pairs[:, top + k : top + k + 1], 0.0)
    line = lax.broadcasted_iota(jnp.int32, total.shape, 0) * len(pair_refs) // count
    total = jnp.where(line.astype(jnp.float32) == ids_ref[1:2, :], total, 0.0)
    m_high, m_middle, _ = halves(total)
    both = jnp.concatenate([m_high, m_middle], axis=0)
    for i in range(rows_ref.shape[1] // BLOCK):
        here = slice(i * BLOCK, (i + 1) * BLOCK)
        high, middle, _ = halves(rows_ref[:, here])
        value = mul(both, high)
        out_ref[:, here] = value[:count] + (value[count:] + mul(m_high, middle))


def combine(pairs, ids, rows):
    count = len(pairs) * pairs[0].shape[1]
    depth, half = rows.shape
    return pl.pallas_call(
        combine_kernel,
        out_shape=jax.ShapeDtypeStruct((count, half), jnp.float32),
        in_specs=[pl.BlockSpec(memory_space=pltpu.VMEM)] * (len(pairs) + 2),
        out_specs=pl.BlockSpec(memory_space=pltpu.VMEM),
        compiler_params=pltpu.CompilerParams(vmem_limit_bytes=MIX_VMEM),
        cost_estimate=pl.CostEstimate(
            flops=6 * count * depth * half, bytes_accessed=4 * (count + depth) * half, transcendentals=0
        ),
        name="combine",
    )(*pairs, ids, rows)


def shift(count, by):
    return [(i, (i + by) % count) for i in range(count)]


def shards(tokens, route_ids, route_weights, expert_rows):
    group = lax.axis_index("grp")
    ep_count = lax.axis_size(EP)
    far = lax.axis_size("zh")
    low = lax.axis_size("zl")
    near = ep_count // far
    tok_dev, top = route_ids.shape
    exp_dev, capacity, width = expert_rows.shape
    half = width // 2
    held = 2 * exp_dev
    per_group = exp_dev * ep_count
    experts = 2 * per_group

    taken = lax.ppermute(expert_rows, "grp", [(0, 1), (1, 0)])

    ids_t = route_ids.T
    chip = jnp.where(ids_t < experts, ids_t % per_group // exp_dev, -1)
    place = (ids_t // per_group != group) * exp_dev + ids_t % exp_dev
    lanes = jnp.arange(128, dtype=jnp.int32)
    chip_hot = (chip[:, :, None] == jnp.arange(ep_count, dtype=jnp.int32)).astype(jnp.bfloat16)
    place_hot = (place[:, :, None] == lanes).astype(jnp.bfloat16)
    flags = lax.dot_general(
        chip_hot.reshape(top * tok_dev, ep_count), place_hot.reshape(top * tok_dev, 128),
        (((0,), (0,)), ((), ())), preferred_element_type=jnp.float32,
    )
    chosen = lax.all_to_all(flags[:, None, :], EP, 0, 0, tiled=True).reshape(ep_count, 128)

    row = jnp.arange(ep_count * held, dtype=jnp.int32)[:, None]
    r_side = row // (ep_count * exp_dev)
    r_near = row % (ep_count * exp_dev) // (far * exp_dev)
    r_far = row % (far * exp_dev) // exp_dev
    r_exp = row % exp_dev
    zh = lax.axis_index("zh")
    home = (r_near // low * far + (zh + r_far) % far) * low + r_near % low
    lane = r_side * exp_dev + r_exp

    col = jnp.arange(ep_count * held, dtype=jnp.int32)
    c_near = col // (held * far)
    c_side = col % (held * far) // (exp_dev * far)
    c_far = col % (exp_dev * far) // exp_dev
    c_chip = (c_near // low * far + zh) * low + c_near % low
    c_id = (c_side + group) % 2 * per_group + c_chip * exp_dev + col % exp_dev
    ids = jnp.stack([c_id, c_far]).astype(jnp.float32)

    pair = jnp.concatenate([ids_t.astype(jnp.float32), route_weights.T], axis=0)
    chosen, pair, ids, home, lane = lax.optimization_barrier((chosen, pair, ids, home, lane))
    pairs = [pair] + [lax.ppermute(pair, "zh", shift(far, -o)) for o in range(1, far)]
    outgoing = pick(group.astype(jnp.int32).reshape(1), chosen, home, lane, pltpu.with_memory_space_constraint(expert_rows, pltpu.HBM), taken, near)
    outgoing, pairs, ids = lax.optimization_barrier((outgoing, pairs, ids))
    rows = lax.all_to_all(outgoing, NEAR, 0, 0, tiled=True)
    rows = rows.reshape(ep_count * held, half)
    partial = combine(pairs, ids, rows).reshape(far, tok_dev, half)
    partial, route_ids, route_weights = lax.optimization_barrier((partial, route_ids, route_weights))
    cut = half // 2
    up, down = shift(far, 1), shift(far, -1)
    far_up = lax.ppermute(partial[2, :, :cut], "zh", up)
    far_down = lax.ppermute(partial[2, :, cut:], "zh", down)
    next_right = lax.ppermute(partial[1, :, cut:], "zh", up)
    prev_left = lax.ppermute(partial[3, :, :cut], "zh", down)
    next_left = lax.ppermute(partial[1, :, :cut] + far_up, "zh", up)
    prev_right = lax.ppermute(partial[3, :, cut:] + far_down, "zh", down)
    total = partial[0] + jnp.concatenate([next_left + prev_left, next_right + prev_right], axis=1)

    ident = jnp.sum(jnp.where(route_ids < experts, 0.0, route_weights), axis=1, keepdims=True)
    return total + ident * lax.dynamic_slice_in_dim(tokens, group * half, half, 1)


def solution(mesh):
    torus = Mesh(mesh.devices.reshape(mesh.shape["grp"], 4, 4, 4, 2), ("grp",) + EP)
    in_specs = (P(EP, None), P(EP, None), P(EP, None), P(("grp",) + EP, None, None))
    return jax.shard_map(
        shards, mesh=torus, in_specs=in_specs, out_specs=P(EP, "grp"), check_vma=False
    )
```

time: 156 us -> 151 us (0.968)
  local copies, waits for them, and re-layouts: 2.54 us -> 0.06 us
  waiting for transfers between devices: 25.5 us -> 27.6 us
    all_to_all x1, starting transfers between devices: 9.73 us -> 15 us  [shards(): lax.all_to_all(flags[:, None, :], EP, 0, 0, tiled=True)]
    ppermute x3, starting transfers between devices: 10.4 us -> 5.66 us  [shards(): lax.ppermute(pair, 'zh', shift(far, -o))]
    ppermute x1, starting transfers between devices: 0.41 us -> 3.08 us  [shards(): next_right = lax.ppermute(partial[1, :, cut:], 'zh', up)]
    ppermute x1, starting transfers between devices: 3.73 us -> 1.06 us  [shards(): prev_right = lax.ppermute(partial[3, :, cut:] + far_down, 'zh', down)]
    unnamed x8 -> x6, local copies, waits for them, and re-layouts: 2.34 us -> 0.01 us
    ppermute x1, waiting for transfers between devices: 7 us -> 9.05 us  [shards(): next_left = lax.ppermute(partial[1, :, :cut] + far_up, 'zh', up)]
  transfers between devices with their start and end apart: 11 -> 11, of which waited for: 5 -> 6; matrix products, arithmetic and copies ran while one was open for 4% -> 3% of each run, Pallas kernels for 0% -> 4%
where the time goes in v5:
time: 151 us
  blocking collectives  76.2 us (50%)
  starting transfers between devices  32.4 us (21%)
  waiting for transfers between devices  27.6 us (18%)
  Pallas kernels  8.17 us (5%)
  other arithmetic  5.38 us (4%)
    all_to_all x1, blocking collectives, shards(): rows = lax.all_to_all(outgoing, NEAR, 0, 0, tiled=True)  76.2 us
    all_to_all x1, starting transfers between devices, shards(): lax.all_to_all(flags[:, None, :], EP, 0, 0, tiled=True)  15 us
    all_to_all x1, waiting for transfers between devices, shards(): lax.all_to_all(flags[:, None, :], EP, 0, 0, tiled=True)  9.23 us
    ppermute x1, waiting for transfers between devices, shards(): next_left = lax.ppermute(partial[1, :, :cut] + far_up, 'zh', up)  9.05 us
    ppermute x1, waiting for transfers between devices, shards(): far_down = lax.ppermute(partial[2, :, cut:], 'zh', down)  6.5 us
    pallas_call x1, Pallas kernels, pick(): pl.pallas_call(pick_kernel, out_shape=jax.ShapeDtypeStruct((targets, coun...  5.83 us
    ppermute x3, starting transfers between devices, shards(): lax.ppermute(pair, 'zh', shift(far, -o))  5.66 us
    ppermute x1, starting transfers between devices, shards(): next_right = lax.ppermute(partial[1, :, cut:], 'zh', up)  3.08 us
  transfers between devices with their start and end apart: 11, of which 6 were waited for; matrix products, arithmetic and copies ran while one was open for 3% of the time, Pallas kernels for 4%

profile of v5, /device:TPU:32, one launch (start us, length us, event | category | flops | bytes accessed | tf_op | source)
XLA Modules:
  0.0 151.0 jit_solution(9933044413933952955)
XLA Ops:
  0.0 0.0 collective-permute-start
  0.0 0.7 fusion.36
  0.7 1.0 fusion.32
  1.8 15.0 %all-to-all-start = ((f32[128,1,128]{2,1,0:T(1,128)}), f32[128,1,128]{2,1,0:T(1,128)S(1)}, u32[]{:S(2)}, u32[]{:S(2)}) async-start(f32[128,1,128]{2,1,0:T(1,128)} %bitcast.4), calls=%async_computation | async-start | bytes 131072 | tf_op jit(solution)/shard_map/all_to_all | solution.py:154
  16.8 0.4 fusion.9
  17.2 0.7 bitcast_convert_fusion
  17.9 0.7 pad_maximum_fusion.refs_0_
  18.6 9.2 %all-to-all-done = f32[128,1,128]{2,1,0:T(1,128)S(1)} async-done(((f32[128,1,128]{2,1,0:T(1,128)}), f32[128,1,128]{2,1,0:T(1,128)S(1)}, u32[]{:S(2)}, u32[]{:S(2)}) %all-to-all-start) | async-done | bytes 65568 | tf_op jit(solution)/shard_map/all_to_all | solution.py:154
  27.8 0.7 collective-permute-start.3
  28.5 3.2 %collective-permute-start.2 = (f32[24,32]{1,0:T(8,128)S(1)}, f32[24,32]{1,0:T(8,128)S(1)}, u32[]{:S(2)}, u32[]{:S(2)}) collective-permute-start(f32[24,32]{1,0:T(8,128)S(1)} %pad_maximum_fusion.refs_0_), channel_id=1, source_target_pairs={{0,4},{2,6},{4,0},{6,2},{1,5},{3,7},{5,1},{7,3},{8,12},{10,14},{12... | collective-permute-start | bytes 9224 | tf_op jit(solution)/shard_map/ppermute | solution.py:175
  31.7 1.8 %collective-permute-start.1 = (f32[24,32]{1,0:T(8,128)S(1)}, f32[24,32]{1,0:T(8,128)S(1)}, u32[]{:S(2)}, u32[]{:S(2)}) collective-permute-start(f32[24,32]{1,0:T(8,128)S(1)} %pad_maximum_fusion.refs_0_), channel_id=1, source_target_pairs={{0,6},{2,0},{4,2},{6,4},{1,7},{3,1},{5,3},{7,5},{8,14},{10,8},{12,... | collective-permute-start | bytes 9224 | tf_op jit(solution)/shard_map/ppermute | solution.py:175
  33.5 0.0 collective-permute-done.taken_ref
  33.5 5.8 %pick.1 = f32[32,16,3072]{2,1,0:T(8,128)S(1)} custom-call(s32[1]{0:T(128)} %bitcast.group_ref, f32[128,128]{1,0:T(8,128)S(1)} %bitcast.61, s32[512,1]{1,0:T(8,128)S(1)} %get-tuple-element.20.home_ref, s32[512,1]{1,0:T(8,128)S(1)} %get-tuple-element.21.lane_ref, f32[2,96,6144]{2,1,0:T(8,128)} %own_ref.1, f32[2,96,6144]{2,1,0:T(8,128)} %collective-permute-done.taken_ref), custom_call_target="tpu_custom_call" | custom-call | flops 1811939328 | bytes 11010048 | tf_op jit(solution)/shard_map/pick/pallas_call | solution.py:72
  39.3 0.0 collective-permute-done.3.refs_3_
  39.4 0.0 collective-permute-done.2.refs_2_
  39.4 0.0 collective-permute-done.1.refs_1_
  39.4 76.2 %all_to_all.10 = f32[32,16,3072]{2,1,0:T(8,128)S(1)} all-to-all(f32[32,16,3072]{2,1,0:T(8,128)S(1)} %pick.1), channel_id=1, replica_groups=mesh['grp'=2,'x'=4,'y'=4,'zh'=4,'zl'=2] {'x','y','zl'}, dimensions={0} | all-to-all | bytes 12582912 | tf_op jit(solution)/shard_map/all_to_all | solution.py:178
  115.6 0.0 copy-start.1
  115.6 0.0 copy-start.2
  115.6 0.0 copy-start
  115.6 2.3 %combine.1 = f32[128,3072]{1,0:T(8,128)S(1)} custom-call(f32[24,32]{1,0:T(8,128)S(1)} %pad_maximum_fusion.refs_0_, f32[24,32]{1,0:T(8,128)S(1)} %collective-permute-done.1.refs_1_, f32[24,32]{1,0:T(8,128)S(1)} %collective-permute-done.2.refs_2_, f32[24,32]{1,0:T(8,128)S(1)} %collective-permute-done.3.refs_3_, f32[2,512]{1,0:T(2,128)S(1)} %add_convert_fusion.refs_4_, ...), custom_call_target="tpu_custom_call" | custom-call | flops 1207959552 | bytes 7864320 | tf_op jit(solution)/shard_map/combine/pallas_call | solution.py:112
  117.9 0.1 slice_bitcast_fusion.2
  118.0 1.4 collective-permute-start.8
  119.4 1.8 %collective-permute-start.4 = (f32[32,1536]{1,0:T(8,128)S(1)}, f32[32,1536]{1,0:T(8,128)S(1)}, u32[]{:S(2)}, u32[]{:S(2)}) collective-permute-start(f32[32,1536]{1,0:T(8,128)S(1)} %get-tuple-element.36), channel_id=1, source_target_pairs={{0,2},{2,4},{4,6},{6,0},{1,3},{3,5},{5,7},{7,1},{8,10},{10,12},{12... | collective-permute-start | bytes 589832 | tf_op jit(solution)/shard_map/ppermute | solution.py:184
  121.2 2.3 %collective-permute-start.6 = (f32[32,1536]{1,0:T(8,128)S(1)}, f32[32,1536]{1,0:T(8,128)S(1)}, u32[]{:S(2)}, u32[]{:S(2)}) collective-permute-start(f32[32,1536]{1,0:T(8,128)S(1)} %get-tuple-element.33), channel_id=1, source_target_pairs={{0,6},{2,0},{4,2},{6,4},{1,7},{3,1},{5,3},{7,5},{8,14},{10,8},{12,... | collective-permute-start | bytes 589832 | tf_op jit(solution)/shard_map/ppermute | solution.py:187
  123.5 6.5 %collective-permute-done.8 = f32[32,1536]{1,0:T(8,128)S(1)} collective-permute-done((f32[32,1536]{1,0:T(8,128)S(1)}, f32[32,1536]{1,0:T(8,128)S(1)}, u32[]{:S(2)}, u32[]{:S(2)}) %collective-permute-start.8) | collective-permute-done | bytes 196640 | tf_op jit(solution)/shard_map/ppermute | solution.py:185
  130.0 1.5 collective-permute-done.4
  131.5 0.1 bitcast_add_fusion.1
  131.6 2.1 %collective-permute-start.5 = (f32[32,1536]{1,0:T(8,128)S(1)}, f32[32,1536]{1,0:T(8,128)}, u32[]{:S(2)}, u32[]{:S(2)}) collective-permute-start(f32[32,1536]{1,0:T(8,128)S(1)} %get-tuple-element.37), channel_id=1, source_target_pairs={{0,2},{2,4},{4,6},{6,0},{1,3},{3,5},{5,7},{7,1},{8,10},{10,12},{12... | collective-permute-start | bytes 589832 | tf_op jit(solution)/shard_map/ppermute | solution.py:188
  133.7 3.1 %collective-permute-start.7 = (f32[32,1536]{1,0:T(8,128)S(1)}, f32[32,1536]{1,0:T(8,128)S(1)}, u32[]{:S(2)}, u32[]{:S(2)}) collective-permute-start(f32[32,1536]{1,0:T(8,128)S(1)} %get-tuple-element.35), channel_id=1, source_target_pairs={{0,2},{2,4},{4,6},{6,0},{1,3},{3,5},{5,7},{7,1},{8,10},{10,12},{12... | collective-permute-start | bytes 589832 | tf_op jit(solution)/shard_map/ppermute | solution.py:186
  136.7 1.1 collective-permute-start.9
  137.8 0.0 copy-done.1
  137.8 0.0 copy-done.2
  137.8 0.3 collective-permute-done.6
  138.1 9.0 %collective-permute-done.5 = f32[32,1536]{1,0:T(8,128)} collective-permute-done((f32[32,1536]{1,0:T(8,128)S(1)}, f32[32,1536]{1,0:T(8,128)}, u32[]{:S(2)}, u32[]{:S(2)}) %collective-permute-start.5) | collective-permute-done | bytes 196640 | tf_op jit(solution)/shard_map/ppermute | solution.py:188
  147.1 0.9 add.354
  148.1 1.0 collective-permute-done.7
  149.1 0.0 collective-permute-done.9
  149.1 1.0 add.356
  150.1 0.0 copy-done
  150.1 0.9 fusion.4
  (3 shorter events, 0.1 us)
Async XLA Ops:
  0.0 33.5 %collective-permute-start = (f32[2,96,6144]{2,1,0:T(8,128)}, f32[2,96,6144]{2,1,0:T(8,128)}, u32[]{:S(2)}, u32[]{:S(2)}) collective-permute-start(f32[2,96,6144]{2,1,0:T(8,128)} %own_ref.1), channel_id=1, source_target_pairs={{0,128},{128,0},{1,129},{129,1},{2,130},{130,2},{3,131},{131,3},{4... | collective-permute-start | bytes 14155784 | tf_op jit(solution)/shard_map/ppermute | solution.py:142
  1.8 26.1 %all-to-all-start = ((f32[128,1,128]{2,1,0:T(1,128)}), f32[128,1,128]{2,1,0:T(1,128)S(1)}, u32[]{:S(2)}, u32[]{:S(2)}) async-start(f32[128,1,128]{2,1,0:T(1,128)} %bitcast.4), calls=%async_computation | async-start | bytes 131072 | tf_op jit(solution)/shard_map/all_to_all | solution.py:154
  27.8 11.5 %collective-permute-start.3 = (f32[24,32]{1,0:T(8,128)S(1)}, f32[24,32]{1,0:T(8,128)S(1)}, u32[]{:S(2)}, u32[]{:S(2)}) collective-permute-start(f32[24,32]{1,0:T(8,128)S(1)} %pad_maximum_fusion.refs_0_), channel_id=1, source_target_pairs={{0,2},{2,4},{4,6},{6,0},{1,3},{3,5},{5,7},{7,1},{8,10},{10,12},{12... | collective-permute-start | bytes 9224 | tf_op jit(solution)/shard_map/ppermute | solution.py:175
  28.5 10.9 %collective-permute-start.2 = (f32[24,32]{1,0:T(8,128)S(1)}, f32[24,32]{1,0:T(8,128)S(1)}, u32[]{:S(2)}, u32[]{:S(2)}) collective-permute-start(f32[24,32]{1,0:T(8,128)S(1)} %pad_maximum_fusion.refs_0_), channel_id=1, source_target_pairs={{0,4},{2,6},{4,0},{6,2},{1,5},{3,7},{5,1},{7,3},{8,12},{10,14},{12... | collective-permute-start | bytes 9224 | tf_op jit(solution)/shard_map/ppermute | solution.py:175
  31.7 7.6 %collective-permute-start.1 = (f32[24,32]{1,0:T(8,128)S(1)}, f32[24,32]{1,0:T(8,128)S(1)}, u32[]{:S(2)}, u32[]{:S(2)}) collective-permute-start(f32[24,32]{1,0:T(8,128)S(1)} %pad_maximum_fusion.refs_0_), channel_id=1, source_target_pairs={{0,6},{2,0},{4,2},{6,4},{1,7},{3,1},{5,3},{7,5},{8,14},{10,8},{12,... | collective-permute-start | bytes 9224 | tf_op jit(solution)/shard_map/ppermute | solution.py:175
  115.6 22.2 %copy-start.1 = (s32[32,12]{0,1:T(8,128)S(1)}, s32[32,12]{0,1:T(8,128)}, u32[]{:S(2)}) copy-start(s32[32,12]{0,1:T(8,128)} %param.5) | copy-start | bytes 4612
  115.6 22.2 %copy-start.2 = (f32[32,12]{0,1:T(8,128)S(1)}, f32[32,12]{0,1:T(8,128)}, u32[]{:S(2)}) copy-start(f32[32,12]{0,1:T(8,128)} %param.6) | copy-start | bytes 4612
  115.6 34.5 %copy-start = (f32[32,6144]{1,0:T(8,128)S(1)}, f32[32,6144]{1,0:T(8,128)}, u32[]{:S(2)}) copy-start(f32[32,6144]{1,0:T(8,128)} %param.4) | copy-start | bytes 2359300
  118.0 12.0 %collective-permute-start.8 = (f32[32,1536]{1,0:T(8,128)S(1)}, f32[32,1536]{1,0:T(8,128)S(1)}, u32[]{:S(2)}, u32[]{:S(2)}) collective-permute-start(f32[32,1536]{1,0:T(8,128)S(1)} %get-tuple-element.34), channel_id=1, source_target_pairs={{0,6},{2,0},{4,2},{6,4},{1,7},{3,1},{5,3},{7,5},{8,14},{10,8},{12,... | collective-permute-start | bytes 589832 | tf_op jit(solution)/shard_map/ppermute | solution.py:185
  119.4 12.1 %collective-permute-start.4 = (f32[32,1536]{1,0:T(8,128)S(1)}, f32[32,1536]{1,0:T(8,128)S(1)}, u32[]{:S(2)}, u32[]{:S(2)}) collective-permute-start(f32[32,1536]{1,0:T(8,128)S(1)} %get-tuple-element.36), channel_id=1, source_target_pairs={{0,2},{2,4},{4,6},{6,0},{1,3},{3,5},{5,7},{7,1},{8,10},{10,12},{12... | collective-permute-start | bytes 589832 | tf_op jit(solution)/shard_map/ppermute | solution.py:184
  121.2 16.9 %collective-permute-start.6 = (f32[32,1536]{1,0:T(8,128)S(1)}, f32[32,1536]{1,0:T(8,128)S(1)}, u32[]{:S(2)}, u32[]{:S(2)}) collective-permute-start(f32[32,1536]{1,0:T(8,128)S(1)} %get-tuple-element.33), channel_id=1, source_target_pairs={{0,6},{2,0},{4,2},{6,4},{1,7},{3,1},{5,3},{7,5},{8,14},{10,8},{12,... | collective-permute-start | bytes 589832 | tf_op jit(solution)/shard_map/ppermute | solution.py:187
  131.6 15.6 %collective-permute-start.5 = (f32[32,1536]{1,0:T(8,128)S(1)}, f32[32,1536]{1,0:T(8,128)}, u32[]{:S(2)}, u32[]{:S(2)}) collective-permute-start(f32[32,1536]{1,0:T(8,128)S(1)} %get-tuple-element.37), channel_id=1, source_target_pairs={{0,2},{2,4},{4,6},{6,0},{1,3},{3,5},{5,7},{7,1},{8,10},{10,12},{12... | collective-permute-start | bytes 589832 | tf_op jit(solution)/shard_map/ppermute | solution.py:188
  133.7 15.5 %collective-permute-start.7 = (f32[32,1536]{1,0:T(8,128)S(1)}, f32[32,1536]{1,0:T(8,128)S(1)}, u32[]{:S(2)}, u32[]{:S(2)}) collective-permute-start(f32[32,1536]{1,0:T(8,128)S(1)} %get-tuple-element.35), channel_id=1, source_target_pairs={{0,2},{2,4},{4,6},{6,0},{1,3},{3,5},{5,7},{7,1},{8,10},{10,12},{12... | collective-permute-start | bytes 589832 | tf_op jit(solution)/shard_map/ppermute | solution.py:186
  136.7 12.4 %collective-permute-start.9 = (f32[32,1536]{1,0:T(8,128)S(1)}, f32[32,1536]{1,0:T(8,128)}, u32[]{:S(2)}, u32[]{:S(2)}) collective-permute-start(f32[32,1536]{1,0:T(8,128)S(1)} %get-tuple-element.38), channel_id=1, source_target_pairs={{0,6},{2,0},{4,2},{6,4},{1,7},{3,1},{5,3},{7,5},{8,14},{10,8},{12,... | collective-permute-start | bytes 589832 | tf_op jit(solution)/shard_map/ppermute | solution.py:189

commit v6 on v5

v6 whole, which is shorter than its diff:
```python
import functools

import jax
import jax.numpy as jnp
from jax import lax
from jax.sharding import Mesh
from jax.sharding import PartitionSpec as P
from jax.experimental import pallas as pl
from jax.experimental.pallas import tpu as pltpu

EP = ("x", "y", "zh", "zl")
NEAR = ("x", "y", "zl")
BLOCK = 512
PICK_VMEM = 24 * 1024 * 1024
MIX_VMEM = 24 * 1024 * 1024


def halves(x):
    high = x.astype(jnp.bfloat16)
    rest = x - high.astype(jnp.float32)
    middle = rest.astype(jnp.bfloat16)
    return high, middle, rest - middle.astype(jnp.float32)


def mul(a, b):
    return jnp.dot(a, b, preferred_element_type=jnp.float32)


def ask_kernel(group_ref, ids_ref, weights_ref, out_ref, both, *, exp_dev, per_group):
    top, count = ids_ref.shape
    chips = out_ref.shape[0]
    gap = 2 * exp_dev
    second = both.shape[0] // 2
    ids = ids_ref[...]
    chip = jnp.where(ids < 2 * per_group, lax.div(lax.rem(ids, per_group), exp_dev), -1)
    both[...] = jnp.zeros_like(both)
    both[0:top, :] = ids.astype(jnp.float32)
    both[second : second + top, :] = weights_ref[...]
    columns = both[...].T
    chip_lines = lax.broadcasted_iota(jnp.int32, (chips, count), 0)
    lanes = lax.broadcasted_iota(jnp.int32, (count, 128), 1)
    token = (lax.broadcasted_iota(jnp.int32, (count, 128), 0) + 1).astype(jnp.float32)
    total = jnp.zeros((chips, 128), jnp.float32)
    for k in range(top):
        names = columns[:, k : k + 1].astype(jnp.int32)
        place = jnp.where(lax.div(names, per_group) == group_ref[0], 0, exp_dev) + lax.rem(names, exp_dev)
        high, middle, low = halves(columns[:, second + k : second + k + 1])
        value = jnp.where(lanes == place, token, 0.0)
        value = jnp.where(lanes == place + gap, high.astype(jnp.float32), value)
        value = jnp.where(lanes == place + 2 * gap, middle.astype(jnp.float32), value)
        value = jnp.where(lanes == place + 3 * gap, low, value)
        where = (chip_lines == chip[k : k + 1, :]).astype(jnp.float32).astype(jnp.bfloat16)
        total += mul(where, value.astype(jnp.bfloat16))
    weight = total + pltpu.roll(total, 128 - gap, 1) + pltpu.roll(total, 128 - 2 * gap, 1)
    lanes = lax.broadcasted_iota(jnp.int32, total.shape, 1)
    out_ref[...] = jnp.where(lanes < gap, total, jnp.where(lanes < 2 * gap, weight, 0.0))


def ask(group, ids, weights, chips, exp_dev, per_group):
    top, count = ids.shape
    vmem = pl.BlockSpec(memory_space=pltpu.VMEM)
    return pl.pallas_call(
        functools.partial(ask_kernel, exp_dev=exp_dev, per_group=per_group),
        out_shape=jax.ShapeDtypeStruct((chips, 128), jnp.float32),
        in_specs=[pl.BlockSpec(memory_space=pltpu.SMEM), vmem, vmem],
        out_specs=vmem,
        scratch_shapes=[pltpu.VMEM((2 * (-(-top // 8) * 8), count), jnp.float32)],
        compiler_params=pltpu.CompilerParams(vmem_limit_bytes=MIX_VMEM),
        name="ask",
    )(group, ids, weights)


def pick_kernel(group_ref, chosen_ref, home_ref, lane_ref, own_ref, taken_ref, out_ref, held, arrived):
    sides, steps, exp_dev, capacity, block = held.shape
    start = pl.multiple_of(group_ref[0] * steps * block, block)
    copies = {}
    for i in range(steps):
        for side, ref in enumerate((own_ref, taken_ref)):
            copies[i, side] = pltpu.make_async_copy(
                ref.at[:, :, pl.ds(start + i * block, block)], held.at[side, i], arrived.at[side, i]
            )
            copies[i, side].start()

    chosen = chosen_ref[...]
    count = home_ref.shape[0]
    gap = sides * exp_dev
    homes = lax.broadcasted_iota(jnp.int32, (count, chosen.shape[0]), 1)
    earlier = (homes < home_ref[...]).astype(jnp.float32).astype(jnp.bfloat16)
    before = mul(earlier, (chosen > 0).astype(jnp.float32).astype(jnp.bfloat16))
    high, middle, low = halves(chosen)
    this = (homes == home_ref[...]).astype(jnp.float32).astype(jnp.bfloat16)
    here = mul(this, high) + mul(this, middle) + mul(this, low.astype(jnp.bfloat16))
    lanes = lax.broadcasted_iota(jnp.int32, here.shape, 1)
    mine = lanes == lane_ref[...]
    token = jnp.sum(jnp.where(mine, here, 0.0), axis=1, keepdims=True)
    weight = jnp.sum(jnp.where(lanes == lane_ref[...] + gap, here, 0.0), axis=1, keepdims=True)
    rank = jnp.sum(jnp.where(mine, before, 0.0), axis=1, keepdims=True)
    code = jnp.where(token > 0, rank.astype(jnp.int32) + capacity * lax.rem(lane_ref[...], exp_dev), -1)
    slot = lax.broadcasted_iota(jnp.int32, (count, exp_dev * capacity), 1)
    select = (code == slot).astype(jnp.float32).astype(jnp.bfloat16)

    targets, lines, group = out_ref.shape
    each = count // sides
    rows = each // targets
    lanes = lanes[:each]
    note = jnp.where(lanes == 0, token[:each], jnp.where(lanes == 1, weight[:each], 0.0))
    note = jnp.where(lanes == 2, token[each:], jnp.where(lanes == 3, weight[each:], note))
    out_ref[:, lines - rows :, :] = note.reshape(targets, rows, group)
    per = block // group
    for i in range(steps):
        for side in range(sides):
            copies[i, side].wait()
            high, middle, _ = halves(held[side, i].reshape(exp_dev * capacity, block))
            wanted = select[side * each : (side + 1) * each, :]
            value = mul(wanted, high) + mul(wanted, middle)
            for j in range(per):
                line = ((i * per + j) * sides + side) * rows
                out_ref[:, line : line + rows, :] = value[:, j * group : (j + 1) * group].reshape(targets, rows, group)


def pick(group, chosen, home, lane, own, taken, targets):
    exp_dev, capacity, width = own.shape
    half = width // 2
    steps = half // BLOCK
    count = home.shape[0]
    slots = exp_dev * capacity
    lines = count // targets * half // 128 + count // targets // 2
    vmem = pl.BlockSpec(memory_space=pltpu.VMEM)
    hbm = pl.BlockSpec(memory_space=pl.ANY)
    return pl.pallas_call(
        pick_kernel,
        out_shape=jax.ShapeDtypeStruct((targets, lines, 128), jnp.float32),
        in_specs=[pl.BlockSpec(memory_space=pltpu.SMEM), vmem, vmem, vmem, hbm, hbm],
        out_specs=vmem,
        scratch_shapes=[
            pltpu.VMEM((2, steps, exp_dev, capacity, BLOCK), jnp.float32),
            pltpu.SemaphoreType.DMA((2, steps)),
        ],
        compiler_params=pltpu.CompilerParams(vmem_limit_bytes=PICK_VMEM),
        cost_estimate=pl.CostEstimate(
            flops=4 * count * slots * half, bytes_accessed=4 * (2 * slots + count) * half, transcendentals=0
        ),
        name="pick",
    )(group, chosen, home, lane, own, taken)


def combine_kernel(rows_ref, out_ref, *, far, exp_dev):
    sources, lines, group = rows_ref.shape
    rows = far * exp_dev
    count, half = out_ref.shape
    note = rows_ref[:, lines - rows :, :].reshape(sources * rows, group)
    line = lax.broadcasted_iota(jnp.int32, (sources * rows, count), 0)
    out_line = lax.broadcasted_iota(jnp.int32, (sources * rows, count), 1)
    right = lax.div(lax.rem(line, rows), exp_dev) == lax.div(out_line, count // far)
    token = jnp.where(right, lax.rem(out_line, count // far) + 1, -1).astype(jnp.float32)
    sides = []
    for side in range(2):
        named = note[:, 2 * side : 2 * side + 1] == token
        mix = jnp.where(named, note[:, 2 * side + 1 : 2 * side + 2], 0.0)
        sides.append(mix.reshape(sources, rows, count))
    mix = jnp.concatenate(sides, axis=1).reshape(2 * sources * rows, count).T
    m_high, m_middle, _ = halves(mix)
    both = jnp.concatenate([m_high, m_middle], axis=0)
    per = BLOCK // group
    for i in range(half // BLOCK):
        parts = [rows_ref[:, 2 * rows * (i * per + j) : 2 * rows * (i * per + j + 1), :] for j in range(per)]
        block = jnp.concatenate([part.reshape(2 * sources * rows, group) for part in parts], axis=1)
        high, middle, _ = halves(block)
        value = mul(both, high)
        out_ref[:, i * BLOCK : (i + 1) * BLOCK] = value[:count] + (value[count:] + mul(m_high, middle))


def combine(rows, far, exp_dev, tok_dev, half):
    count = far * tok_dev
    depth = 2 * rows.shape[0] * far * exp_dev
    return pl.pallas_call(
        functools.partial(combine_kernel, far=far, exp_dev=exp_dev),
        out_shape=jax.ShapeDtypeStruct((count, half), jnp.float32),
        in_specs=[pl.BlockSpec(memory_space=pltpu.VMEM)],
        out_specs=pl.BlockSpec(memory_space=pltpu.VMEM),
        compiler_params=pltpu.CompilerParams(vmem_limit_bytes=MIX_VMEM),
        cost_estimate=pl.CostEstimate(
            flops=6 * count * depth * half, bytes_accessed=4 * (count + depth) * half, transcendentals=0
        ),
        name="combine",
    )(rows)


def shift(count, by):
    return [(i, (i + by) % count) for i in range(count)]


def shards(tokens, route_ids, route_weights, expert_rows):
    group = lax.axis_index("grp")
    ep_count = lax.axis_size(EP)
    far = lax.axis_size("zh")
    low = lax.axis_size("zl")
    near = ep_count // far
    tok_dev, top = route_ids.shape
    exp_dev, capacity, width = expert_rows.shape
    half = width // 2
    held = 2 * exp_dev
    per_group = exp_dev * ep_count
    experts = 2 * per_group

    taken = lax.ppermute(expert_rows, "grp", [(0, 1), (1, 0)])

    group_word = group.astype(jnp.int32).reshape(1)
    asked = ask(group_word, route_ids.T, route_weights.T, ep_count, exp_dev, per_group)
    chosen = lax.all_to_all(asked[:, None, :], EP, 0, 0, tiled=True).reshape(ep_count, 128)

    row = jnp.arange(ep_count * held, dtype=jnp.int32)[:, None]
    r_side = row // (ep_count * exp_dev)
    r_near = row % (ep_count * exp_dev) // (far * exp_dev)
    r_far = row % (far * exp_dev) // exp_dev
    r_exp = row % exp_dev
    zh = lax.axis_index("zh")
    home = (r_near // low * far + (zh + r_far) % far) * low + r_near % low
    lane = r_side * exp_dev + r_exp

    chosen, home, lane, taken = lax.optimization_barrier((chosen, home, lane, taken))
    own = pltpu.with_memory_space_constraint(expert_rows, pltpu.HBM)
    outgoing = pick(group_word, chosen, home, lane, own, taken, near)

    rows = lax.all_to_all(outgoing, NEAR, 0, 0, tiled=True)
    partial = combine(rows, far, exp_dev, tok_dev, half).reshape(far, tok_dev, half)
    partial, route_ids, route_weights = lax.optimization_barrier((partial, route_ids, route_weights))
    cut = half // 2
    up, down = shift(far, 1), shift(far, -1)
    far_up = lax.ppermute(partial[2, :, :cut], "zh", up)
    far_down = lax.ppermute(partial[2, :, cut:], "zh", down)
    next_right = lax.ppermute(partial[1, :, cut:], "zh", up)
    prev_left = lax.ppermute(partial[3, :, :cut], "zh", down)
    next_left = lax.ppermute(partial[1, :, :cut] + far_up, "zh", up)
    prev_right = lax.ppermute(partial[3, :, cut:] + far_down, "zh", down)
    total = partial[0] + jnp.concatenate([next_left + prev_left, next_right + prev_right], axis=1)

    ident = jnp.sum(jnp.where(route_ids < experts, 0.0, route_weights), axis=1, keepdims=True)
    return total + ident * lax.dynamic_slice_in_dim(tokens, group * half, half, 1)


def solution(mesh):
    torus = Mesh(mesh.devices.reshape(mesh.shape["grp"], 4, 4, 4, 2), ("grp",) + EP)
    in_specs = (P(EP, None), P(EP, None), P(EP, None), P(("grp",) + EP, None, None))
    return jax.shard_map(
        shards, mesh=torus, in_specs=in_specs, out_specs=P(EP, "grp"), check_vma=False
    )
```

time: 151 us -> 147 us (0.974)
  the two profiles are of different devices: /device:TPU:32 before, /device:TPU:1 now
where the time goes in v6:
time: 147 us
  blocking collectives  76.8 us (52%)
  waiting for transfers between devices  29.6 us (20%)
  starting transfers between devices  26.4 us (18%)
  Pallas kernels  9.4 us (6%)
  other arithmetic  3.2 us (2%)
    all_to_all x1, blocking collectives, shards(): rows = lax.all_to_all(outgoing, NEAR, 0, 0, tiled=True)  76.8 us
    all_to_all x1, starting transfers between devices, shards(): lax.all_to_all(asked[:, None, :], EP, 0, 0, tiled=True)  13.8 us
    all_to_all x1, waiting for transfers between devices, shards(): lax.all_to_all(asked[:, None, :], EP, 0, 0, tiled=True)  10.2 us
    ppermute x1, waiting for transfers between devices, shards(): far_down = lax.ppermute(partial[2, :, cut:], 'zh', down)  7.34 us
    pallas_call x1, Pallas kernels, pick(): pl.pallas_call(pick_kernel, out_shape=jax.ShapeDtypeStruct((targets, line...  6.15 us
    ppermute x1, waiting for transfers between devices, shards(): prev_left = lax.ppermute(partial[3, :, :cut], 'zh', down)  4.97 us
    ppermute x1, waiting for transfers between devices, shards(): next_right = lax.ppermute(partial[1, :, cut:], 'zh', up)  4.46 us
    ppermute x1, starting transfers between devices, shards(): taken = lax.ppermute(expert_rows, 'grp', [(0, 1), (1, 0)])  3.24 us
  transfers between devices with their start and end apart: 8, of which 5 were waited for; matrix products, arithmetic and copies ran while one was open for 1% of the time, Pallas kernels for 1%

profile of v6, /device:TPU:1, one launch (start us, length us, event | category | flops | bytes accessed | tf_op | source)
XLA Modules:
  0.0 147.0 jit_solution(14985567239254664681)
XLA Ops:
  0.0 3.2 %collective-permute-start = (f32[2,96,6144]{2,1,0:T(8,128)}, f32[2,96,6144]{2,1,0:T(8,128)}, u32[]{:S(2)}, u32[]{:S(2)}) collective-permute-start(f32[2,96,6144]{2,1,0:T(8,128)} %own_ref.1), channel_id=1, source_target_pairs={{0,128},{128,0},{1,129},{129,1},{2,130},{130,2},{3,131},{131,3},{4... | collective-permute-start | bytes 14155784 | tf_op jit(solution)/shard_map/ppermute | solution.py:206
  3.2 0.0 copy-start
  3.2 0.7 copy-done
  3.9 0.0 copy-start.2
  3.9 0.7 copy-done.2
  4.6 1.4 ask.1
  6.1 13.8 %all-to-all-start = ((f32[128,1,128]{2,1,0:T(1,128)}), f32[128,1,128]{2,1,0:T(1,128)S(1)}, u32[]{:S(2)}, u32[]{:S(2)}) async-start(f32[128,1,128]{2,1,0:T(1,128)} %bitcast.4), calls=%async_computation | async-start | bytes 131072 | tf_op jit(solution)/shard_map/all_to_all | solution.py:210
  19.8 0.4 fusion.9
  20.2 10.2 %all-to-all-done = f32[128,1,128]{2,1,0:T(1,128)S(1)} async-done(((f32[128,1,128]{2,1,0:T(1,128)}), f32[128,1,128]{2,1,0:T(1,128)S(1)}, u32[]{:S(2)}, u32[]{:S(2)}) %all-to-all-start) | async-done | bytes 65568 | tf_op jit(solution)/shard_map/all_to_all | solution.py:210
  30.4 0.0 collective-permute-done.taken_ref
  30.4 6.1 %pick.1 = f32[32,392,128]{2,1,0:T(8,128)S(1)} custom-call(s32[1]{0:T(128)} %bitcast.group_ref, f32[128,128]{1,0:T(8,128)S(1)} %bitcast.25, s32[512,1]{1,0:T(8,128)S(1)} %get-tuple-element.13.home_ref, s32[512,1]{1,0:T(8,128)S(1)} %get-tuple-element.14.lane_ref, f32[2,96,6144]{2,1,0:T(8,128)} %own_ref.1, f32[2,96,6144]{2,1,0:T(8,128)} %collective-permute-done.taken_ref), custom_call_target="tpu_custom_call" | custom-call | flops 1207959552 | bytes 11010048 | tf_op jit(solution)/shard_map/pick/pallas_call | solution.py:130
  36.5 76.8 %all_to_all.10.rows_ref = f32[32,392,128]{2,1,0:T(8,128)S(1)} all-to-all(f32[32,392,128]{2,1,0:T(8,128)S(1)} %pick.1), channel_id=1, replica_groups=mesh['grp'=2,'x'=4,'y'=4,'zh'=4,'zl'=2] {'x','y','zl'}, dimensions={0} | all-to-all | bytes 12845056 | tf_op jit(solution)/shard_map/all_to_all | solution.py:225
  113.3 0.0 copy-start.1
  113.3 0.0 copy-start.3
  113.3 0.0 copy-start.4
  113.3 1.8 %combine.1 = f32[128,3072]{1,0:T(8,128)S(1)} custom-call(f32[32,392,128]{2,1,0:T(8,128)S(1)} %all_to_all.10.rows_ref), custom_call_target="tpu_custom_call" | custom-call | flops 1207959552 | bytes 7864320 | tf_op jit(solution)/shard_map/combine/pallas_call | solution.py:176
  115.2 0.1 slice_bitcast_fusion.2
  115.2 1.7 %collective-permute-start.5 = (f32[32,1536]{1,0:T(8,128)S(1)}, f32[32,1536]{1,0:T(8,128)S(1)}, u32[]{:S(2)}, u32[]{:S(2)}) collective-permute-start(f32[32,1536]{1,0:T(8,128)S(1)} %get-tuple-element.20), channel_id=1, source_target_pairs={{0,6},{2,0},{4,2},{6,4},{1,7},{3,1},{5,3},{7,5},{8,14},{10,8},{12,... | collective-permute-start | bytes 589832 | tf_op jit(solution)/shard_map/ppermute | solution.py:231
  116.9 0.7 collective-permute-start.1
  117.7 2.8 %collective-permute-start.3 = (f32[32,1536]{1,0:T(8,128)S(1)}, f32[32,1536]{1,0:T(8,128)S(1)}, u32[]{:S(2)}, u32[]{:S(2)}) collective-permute-start(f32[32,1536]{1,0:T(8,128)S(1)} %get-tuple-element.19), channel_id=1, source_target_pairs={{0,6},{2,0},{4,2},{6,4},{1,7},{3,1},{5,3},{7,5},{8,14},{10,8},{12,... | collective-permute-start | bytes 589832 | tf_op jit(solution)/shard_map/ppermute | solution.py:233
  120.5 7.3 %collective-permute-done.5 = f32[32,1536]{1,0:T(8,128)S(1)} collective-permute-done((f32[32,1536]{1,0:T(8,128)S(1)}, f32[32,1536]{1,0:T(8,128)S(1)}, u32[]{:S(2)}, u32[]{:S(2)}) %collective-permute-start.5) | collective-permute-done | bytes 196640 | tf_op jit(solution)/shard_map/ppermute | solution.py:231
  127.9 0.0 collective-permute-done.1
  127.9 0.1 bitcast_add_fusion.1
  127.9 0.6 collective-permute-start.2
  128.5 0.4 collective-permute-start.4
  128.9 3.2 %collective-permute-start.6 = (f32[32,1536]{1,0:T(8,128)S(1)}, f32[32,1536]{1,0:T(8,128)}, u32[]{:S(2)}, u32[]{:S(2)}) collective-permute-start(f32[32,1536]{1,0:T(8,128)S(1)} %get-tuple-element.24), channel_id=1, source_target_pairs={{0,6},{2,0},{4,2},{6,4},{1,7},{3,1},{5,3},{7,5},{8,14},{10,8},{12,... | collective-permute-start | bytes 589832 | tf_op jit(solution)/shard_map/ppermute | solution.py:235
  132.1 0.0 copy-done.1
  132.1 0.0 copy-done.3
  132.1 5.0 %collective-permute-done.3 = f32[32,1536]{1,0:T(8,128)S(1)} collective-permute-done((f32[32,1536]{1,0:T(8,128)S(1)}, f32[32,1536]{1,0:T(8,128)S(1)}, u32[]{:S(2)}, u32[]{:S(2)}) %collective-permute-start.3) | collective-permute-done | bytes 196640 | tf_op jit(solution)/shard_map/ppermute | solution.py:233
  137.1 2.7 %collective-permute-done.2 = f32[32,1536]{1,0:T(8,128)} collective-permute-done((f32[32,1536]{1,0:T(8,128)S(1)}, f32[32,1536]{1,0:T(8,128)}, u32[]{:S(2)}, u32[]{:S(2)}) %collective-permute-start.2) | collective-permute-done | bytes 196640 | tf_op jit(solution)/shard_map/ppermute | solution.py:234
  139.8 0.9 add.179
  140.7 4.5 %collective-permute-done.4 = f32[32,1536]{1,0:T(8,128)S(1)} collective-permute-done((f32[32,1536]{1,0:T(8,128)S(1)}, f32[32,1536]{1,0:T(8,128)S(1)}, u32[]{:S(2)}, u32[]{:S(2)}) %collective-permute-start.4) | collective-permute-done | bytes 196640 | tf_op jit(solution)/shard_map/ppermute | solution.py:232
  145.2 0.0 collective-permute-done.6
  145.2 1.0 add.181
  146.1 0.0 copy-done.4
  146.1 0.9 fusion.4
  (1 shorter events, 0.0 us)
Async XLA Ops:
  0.0 30.4 %collective-permute-start = (f32[2,96,6144]{2,1,0:T(8,128)}, f32[2,96,6144]{2,1,0:T(8,128)}, u32[]{:S(2)}, u32[]{:S(2)}) collective-permute-start(f32[2,96,6144]{2,1,0:T(8,128)} %own_ref.1), channel_id=1, source_target_pairs={{0,128},{128,0},{1,129},{129,1},{2,130},{130,2},{3,131},{131,3},{4... | collective-permute-start | bytes 14155784 | tf_op jit(solution)/shard_map/ppermute | solution.py:206
  3.2 0.7 copy-start
  3.9 0.7 copy-start.2
  6.1 24.3 %all-to-all-start = ((f32[128,1,128]{2,1,0:T(1,128)}), f32[128,1,128]{2,1,0:T(1,128)S(1)}, u32[]{:S(2)}, u32[]{:S(2)}) async-start(f32[128,1,128]{2,1,0:T(1,128)} %bitcast.4), calls=%async_computation | async-start | bytes 131072 | tf_op jit(solution)/shard_map/all_to_all | solution.py:210
  113.3 18.7 %copy-start.1 = (s32[32,12]{0,1:T(8,128)S(1)}, s32[32,12]{0,1:T(8,128)}, u32[]{:S(2)}) copy-start(s32[32,12]{0,1:T(8,128)} %param.5) | copy-start | bytes 4612
  113.3 18.7 %copy-start.3 = (f32[32,12]{0,1:T(8,128)S(1)}, f32[32,12]{0,1:T(8,128)}, u32[]{:S(2)}) copy-start(f32[32,12]{0,1:T(8,128)} %param.6) | copy-start | bytes 4612
  113.3 32.8 %copy-start.4 = (f32[32,6144]{1,0:T(8,128)S(1)}, f32[32,6144]{1,0:T(8,128)}, u32[]{:S(2)}) copy-start(f32[32,6144]{1,0:T(8,128)} %param.4) | copy-start | bytes 2359300
  115.2 12.6 %collective-permute-start.5 = (f32[32,1536]{1,0:T(8,128)S(1)}, f32[32,1536]{1,0:T(8,128)S(1)}, u32[]{:S(2)}, u32[]{:S(2)}) collective-permute-start(f32[32,1536]{1,0:T(8,128)S(1)} %get-tuple-element.20), channel_id=1, source_target_pairs={{0,6},{2,0},{4,2},{6,4},{1,7},{3,1},{5,3},{7,5},{8,14},{10,8},{12,... | collective-permute-start | bytes 589832 | tf_op jit(solution)/shard_map/ppermute | solution.py:231
  116.9 10.9 %collective-permute-start.1 = (f32[32,1536]{1,0:T(8,128)S(1)}, f32[32,1536]{1,0:T(8,128)S(1)}, u32[]{:S(2)}, u32[]{:S(2)}) collective-permute-start(f32[32,1536]{1,0:T(8,128)S(1)} %get-tuple-element.22), channel_id=1, source_target_pairs={{0,2},{2,4},{4,6},{6,0},{1,3},{3,5},{5,7},{7,1},{8,10},{10,12},{12... | collective-permute-start | bytes 589832 | tf_op jit(solution)/shard_map/ppermute | solution.py:230
  117.7 19.4 %collective-permute-start.3 = (f32[32,1536]{1,0:T(8,128)S(1)}, f32[32,1536]{1,0:T(8,128)S(1)}, u32[]{:S(2)}, u32[]{:S(2)}) collective-permute-start(f32[32,1536]{1,0:T(8,128)S(1)} %get-tuple-element.19), channel_id=1, source_target_pairs={{0,6},{2,0},{4,2},{6,4},{1,7},{3,1},{5,3},{7,5},{8,14},{10,8},{12,... | collective-permute-start | bytes 589832 | tf_op jit(solution)/shard_map/ppermute | solution.py:233
  127.9 11.8 %collective-permute-start.2 = (f32[32,1536]{1,0:T(8,128)S(1)}, f32[32,1536]{1,0:T(8,128)}, u32[]{:S(2)}, u32[]{:S(2)}) collective-permute-start(f32[32,1536]{1,0:T(8,128)S(1)} %get-tuple-element.23), channel_id=1, source_target_pairs={{0,2},{2,4},{4,6},{6,0},{1,3},{3,5},{5,7},{7,1},{8,10},{10,12},{12... | collective-permute-start | bytes 589832 | tf_op jit(solution)/shard_map/ppermute | solution.py:234
  128.5 16.7 %collective-permute-start.4 = (f32[32,1536]{1,0:T(8,128)S(1)}, f32[32,1536]{1,0:T(8,128)S(1)}, u32[]{:S(2)}, u32[]{:S(2)}) collective-permute-start(f32[32,1536]{1,0:T(8,128)S(1)} %get-tuple-element.21), channel_id=1, source_target_pairs={{0,2},{2,4},{4,6},{6,0},{1,3},{3,5},{5,7},{7,1},{8,10},{10,12},{12... | collective-permute-start | bytes 589832 | tf_op jit(solution)/shard_map/ppermute | solution.py:232
  128.9 16.3 %collective-permute-start.6 = (f32[32,1536]{1,0:T(8,128)S(1)}, f32[32,1536]{1,0:T(8,128)}, u32[]{:S(2)}, u32[]{:S(2)}) collective-permute-start(f32[32,1536]{1,0:T(8,128)S(1)} %get-tuple-element.24), channel_id=1, source_target_pairs={{0,6},{2,0},{4,2},{6,4},{1,7},{3,1},{5,3},{7,5},{8,14},{10,8},{12,... | collective-permute-start | bytes 589832 | tf_op jit(solution)/shard_map/ppermute | solution.py:235

commit v7 on v6

--- a/solution.py
+++ b/solution.py
@@ -22,11 +22,25 @@
     return high, middle, rest - middle.astype(jnp.float32)
 
 
+def in_hbm(x):
+    return pltpu.with_memory_space_constraint(x, pltpu.HBM)
+
+
 def mul(a, b):
     return jnp.dot(a, b, preferred_element_type=jnp.float32)
 
 
-def ask_kernel(group_ref, ids_ref, weights_ref, out_ref, both, *, exp_dev, per_group):
+def ask_kernel(
+    group_ref, ids_hbm, weights_hbm, out_ref, ident_ref, ids_ref, weights_ref, both, arrived, *, exp_dev, per_group
+):
+    copies = [
+        pltpu.make_async_copy(ids_hbm, ids_ref, arrived.at[0]),
+        pltpu.make_async_copy(weights_hbm, weights_ref, arrived.at[1]),
+    ]
+    for copy in copies:
+        copy.start()
+    for copy in copies:
+        copy.wait()
     top, count = ids_ref.shape
     chips = out_ref.shape[0]
     gap = 2 * exp_dev
@@ -41,8 +55,10 @@
     lanes = lax.broadcasted_iota(jnp.int32, (count, 128), 1)
     token = (lax.broadcasted_iota(jnp.int32, (count, 128), 0) + 1).astype(jnp.float32)
     total = jnp.zeros((chips, 128), jnp.float32)
+    ident = jnp.zeros((count, 1), jnp.float32)
     for k in range(top):
         names = columns[:, k : k + 1].astype(jnp.int32)
+        ident += jnp.where(names < 2 * per_group, 0.0, columns[:, second + k : second + k + 1])
         place = jnp.where(lax.div(names, per_group) == group_ref[0], 0, exp_dev) + lax.rem(names, exp_dev)
         high, middle, low = halves(columns[:, second + k : second + k + 1])
         value = jnp.where(lanes == place, token, 0.0)
@@ -51,6 +67,7 @@
         value = jnp.where(lanes == place + 3 * gap, low, value)
         where = (chip_lines == chip[k : k + 1, :]).astype(jnp.float32).astype(jnp.bfloat16)
         total += mul(where, value.astype(jnp.bfloat16))
+    ident_ref[...] = jnp.broadcast_to(ident, ident_ref.shape)
     weight = total + pltpu.roll(total, 128 - gap, 1) + pltpu.roll(total, 128 - 2 * gap, 1)
     lanes = lax.broadcasted_iota(jnp.int32, total.shape, 1)
     out_ref[...] = jnp.where(lanes < gap, total, jnp.where(lanes < 2 * gap, weight, 0.0))
@@ -59,15 +76,24 @@
 def ask(group, ids, weights, chips, exp_dev, per_group):
     top, count = ids.shape
     vmem = pl.BlockSpec(memory_space=pltpu.VMEM)
+    hbm = pl.BlockSpec(memory_space=pl.ANY)
     return pl.pallas_call(
         functools.partial(ask_kernel, exp_dev=exp_dev, per_group=per_group),
-        out_shape=jax.ShapeDtypeStruct((chips, 128), jnp.float32),
-        in_specs=[pl.BlockSpec(memory_space=pltpu.SMEM), vmem, vmem],
-        out_specs=vmem,
-        scratch_shapes=[pltpu.VMEM((2 * (-(-top // 8) * 8), count), jnp.float32)],
+        out_shape=(
+            jax.ShapeDtypeStruct((chips, 128), jnp.float32),
+            jax.ShapeDtypeStruct((count, 128), jnp.float32),
+        ),
+        in_specs=[pl.BlockSpec(memory_space=pltpu.SMEM), hbm, hbm],
+        out_specs=(vmem, vmem),
+        scratch_shapes=[
+            pltpu.VMEM((top, count), jnp.int32),
+            pltpu.VMEM((top, count), jnp.float32),
+            pltpu.VMEM((2 * (-(-top // 8) * 8), count), jnp.float32),
+            pltpu.SemaphoreType.DMA((2,)),
+        ],
         compiler_params=pltpu.CompilerParams(vmem_limit_bytes=MIX_VMEM),
         name="ask",
-    )(group, ids, weights)
+    )(group, in_hbm(ids), in_hbm(weights))
 
 
 def pick_kernel(group_ref, chosen_ref, home_ref, lane_ref, own_ref, taken_ref, out_ref, held, arrived):
@@ -88,12 +114,16 @@
     earlier = (homes < home_ref[...]).astype(jnp.float32).astype(jnp.bfloat16)
     before = mul(earlier, (chosen > 0).astype(jnp.float32).astype(jnp.bfloat16))
     high, middle, low = halves(chosen)
+    home_lanes = lax.broadcasted_iota(jnp.int32, chosen.shape, 1)
+    packed = jnp.where(home_lanes < 4 * gap, pltpu.roll(middle.astype(jnp.float32), 2 * gap, 1), pltpu.roll(low, 4 * gap, 1))
+    packed = jnp.where(home_lanes < 2 * gap, high.astype(jnp.float32), packed)
     this = (homes == home_ref[...]).astype(jnp.float32).astype(jnp.bfloat16)
-    here = mul(this, high) + mul(this, middle) + mul(this, low.astype(jnp.bfloat16))
+    here = mul(this, packed.astype(jnp.bfloat16))
     lanes = lax.broadcasted_iota(jnp.int32, here.shape, 1)
     mine = lanes == lane_ref[...]
     token = jnp.sum(jnp.where(mine, here, 0.0), axis=1, keepdims=True)
-    weight = jnp.sum(jnp.where(lanes == lane_ref[...] + gap, here, 0.0), axis=1, keepdims=True)
+    parts = (lax.rem(lanes, 2 * gap) == lane_ref[...] + gap) & (lanes < 6 * gap)
+    weight = jnp.sum(jnp.where(parts, here, 0.0), axis=1, keepdims=True)
     rank = jnp.sum(jnp.where(mine, before, 0.0), axis=1, keepdims=True)
     code = jnp.where(token > 0, rank.astype(jnp.int32) + capacity * lax.rem(lane_ref[...], exp_dev), -1)
     slot = lax.broadcasted_iota(jnp.int32, (count, exp_dev * capacity), 1)
@@ -144,15 +174,23 @@
     )(group, chosen, home, lane, own, taken)
 
 
-def combine_kernel(rows_ref, out_ref, *, far, exp_dev):
+def combine_kernel(
+    group_ref, rows_ref, ident_ref, tokens_ref, base_ref, up_ref, down_ref, left_ref, right_ref, own, arrived, *, exp_dev
+):
+    tok_dev, half = base_ref.shape
+    copy = pltpu.make_async_copy(
+        tokens_ref.at[:, pl.ds(pl.multiple_of(group_ref[0] * half, half), half)], own, arrived
+    )
+    copy.start()
     sources, lines, group = rows_ref.shape
+    far = 4
     rows = far * exp_dev
-    count, half = out_ref.shape
+    count = far * tok_dev
     note = rows_ref[:, lines - rows :, :].reshape(sources * rows, group)
     line = lax.broadcasted_iota(jnp.int32, (sources * rows, count), 0)
     out_line = lax.broadcasted_iota(jnp.int32, (sources * rows, count), 1)
-    right = lax.div(lax.rem(line, rows), exp_dev) == lax.div(out_line, count // far)
-    token = jnp.where(right, lax.rem(out_line, count // far) + 1, -1).astype(jnp.float32)
+    fits = lax.div(lax.rem(line, rows), exp_dev) == lax.div(out_line, tok_dev)
+    token = jnp.where(fits, lax.rem(out_line, tok_dev) + 1, -1).astype(jnp.float32)
     sides = []
     for side in range(2):
         named = note[:, 2 * side : 2 * side + 1] == token
@@ -162,28 +200,67 @@
     m_high, m_middle, _ = halves(mix)
     both = jnp.concatenate([m_high, m_middle], axis=0)
     per = BLOCK // group
-    for i in range(half // BLOCK):
+    steps = half // BLOCK
+    copy.wait()
+    ident = ident_ref[:, 0:1]
+    for i in range(steps):
         parts = [rows_ref[:, 2 * rows * (i * per + j) : 2 * rows * (i * per + j + 1), :] for j in range(per)]
         block = jnp.concatenate([part.reshape(2 * sources * rows, group) for part in parts], axis=1)
         high, middle, _ = halves(block)
         value = mul(both, high)
-        out_ref[:, i * BLOCK : (i + 1) * BLOCK] = value[:count] + (value[count:] + mul(m_high, middle))
-
-
-def combine(rows, far, exp_dev, tok_dev, half):
-    count = far * tok_dev
-    depth = 2 * rows.shape[0] * far * exp_dev
+        value = value[:count] + (value[count:] + mul(m_high, middle))
+        near, nxt, opposite, prev = (value[o * tok_dev : (o + 1) * tok_dev] for o in range(far))
+        here = slice(i * BLOCK, (i + 1) * BLOCK)
+        base_ref[:, here] = near + ident * own[:, here]
+        side = slice(i % (steps // 2) * BLOCK, (i % (steps // 2) + 1) * BLOCK)
+        if i < steps // 2:
+            up_ref[:tok_dev, side] = opposite
+            down_ref[tok_dev:, side] = prev
+            left_ref[:, side] = nxt
+        else:
+            down_ref[:tok_dev, side] = opposite
+            up_ref[tok_dev:, side] = nxt
+            right_ref[:, side] = prev
+
+
+def combine(group, rows, ident, tokens, exp_dev):
+    tok_dev, width = tokens.shape
+    half = width // 2
+    count, depth = 4 * tok_dev, 8 * rows.shape[0] * exp_dev
+    vmem = pl.BlockSpec(memory_space=pltpu.VMEM)
     return pl.pallas_call(
-        functools.partial(combine_kernel, far=far, exp_dev=exp_dev),
-        out_shape=jax.ShapeDtypeStruct((count, half), jnp.float32),
-        in_specs=[pl.BlockSpec(memory_space=pltpu.VMEM)],
-        out_specs=pl.BlockSpec(memory_space=pltpu.VMEM),
+        functools.partial(combine_kernel, exp_dev=exp_dev),
+        out_shape=[
+            jax.ShapeDtypeStruct(shape, jnp.float32)
+            for shape in ((tok_dev, half), *[(2 * tok_dev, half // 2)] * 2, *[(tok_dev, half // 2)] * 2)
+        ],
+        in_specs=[pl.BlockSpec(memory_space=pltpu.SMEM), vmem, vmem, pl.BlockSpec(memory_space=pl.ANY)],
+        out_specs=[vmem] * 5,
+        scratch_shapes=[pltpu.VMEM((tok_dev, half), jnp.float32), pltpu.SemaphoreType.DMA],
         compiler_params=pltpu.CompilerParams(vmem_limit_bytes=MIX_VMEM),
         cost_estimate=pl.CostEstimate(
             flops=6 * count * depth * half, bytes_accessed=4 * (count + depth) * half, transcendentals=0
         ),
         name="combine",
-    )(rows)
+    )(group, rows, ident, in_hbm(tokens))
+
+
+def finish_kernel(base_ref, up_ref, down_ref, left_ref, right_ref, out_ref):
+    tok_dev, cut = left_ref.shape
+    out_ref[:, :cut] = base_ref[:, :cut] + down_ref[tok_dev:, :] + left_ref[...]
+    out_ref[:, cut:] = base_ref[:, cut:] + up_ref[tok_dev:, :] + right_ref[...]
+
+
+def finish(base, *parts):
+    vmem = pl.BlockSpec(memory_space=pltpu.VMEM)
+    return pl.pallas_call(
+        finish_kernel,
+        out_shape=jax.ShapeDtypeStruct(base.shape, jnp.float32),
+        in_specs=[vmem] * 5,
+        out_specs=vmem,
+        compiler_params=pltpu.CompilerParams(vmem_limit_bytes=MIX_VMEM),
+        name="finish",
+    )(base, *parts)
 
 
 def shift(count, by):
@@ -206,7 +283,7 @@
     taken = lax.ppermute(expert_rows, "grp", [(0, 1), (1, 0)])
 
     group_word = group.astype(jnp.int32).reshape(1)
-    asked = ask(group_word, route_ids.T, route_weights.T, ep_count, exp_dev, per_group)
+    asked, ident = ask(group_word, route_ids.T, route_weights.T, ep_count, exp_dev, per_group)
     chosen = lax.all_to_all(asked[:, None, :], EP, 0, 0, tiled=True).reshape(ep_count, 128)
 
     row = jnp.arange(ep_count * held, dtype=jnp.int32)[:, None]
@@ -219,24 +296,15 @@
     lane = r_side * exp_dev + r_exp
 
     chosen, home, lane, taken = lax.optimization_barrier((chosen, home, lane, taken))
-    own = pltpu.with_memory_space_constraint(expert_rows, pltpu.HBM)
-    outgoing = pick(group_word, chosen, home, lane, own, taken, near)
+    outgoing = pick(group_word, chosen, home, lane, in_hbm(expert_rows), taken, near)
 
     rows = lax.all_to_all(outgoing, NEAR, 0, 0, tiled=True)
-    partial = combine(rows, far, exp_dev, tok_dev, half).reshape(far, tok_dev, half)
-    partial, route_ids, route_weights = lax.optimization_barrier((partial, route_ids, route_weights))
-    cut = half // 2
     up, down = shift(far, 1), shift(far, -1)
-    far_up = lax.ppermute(partial[2, :, :cut], "zh", up)
-    far_down = lax.ppermute(partial[2, :, cut:], "zh", down)
-    next_right = lax.ppermute(partial[1, :, cut:], "zh", up)
-    prev_left = lax.ppermute(partial[3, :, :cut], "zh", down)
-    next_left = lax.ppermute(partial[1, :, :cut] + far_up, "zh", up)
-    prev_right = lax.ppermute(partial[3, :, cut:] + far_down, "zh", down)
-    total = partial[0] + jnp.concatenate([next_left + prev_left, next_right + prev_right], axis=1)
-
-    ident = jnp.sum(jnp.where(route_ids < experts, 0.0, route_weights), axis=1, keepdims=True)
-    return total + ident * lax.dynamic_slice_in_dim(tokens, group * half, half, 1)
+    base, to_up, to_down, left, right = combine(group_word, rows, ident, tokens, exp_dev)
+    from_up, from_down = lax.ppermute(to_up, "zh", up), lax.ppermute(to_down, "zh", down)
+    left = lax.ppermute(left + from_up[:tok_dev], "zh", up)
+    right = lax.ppermute(right + from_down[:tok_dev], "zh", down)
+    return finish(base, from_up, from_down, left, right)
 
 
 def solution(mesh):

time: 147 us -> 147 us (level)
  the two profiles are of different devices: /device:TPU:1 before, /device:TPU:32 now
where the time goes in v7:
time: 147 us; the launch traced here: 145 us
  blocking collectives  78.2 us (53%)
  waiting for transfers between devices  32.6 us (22%)
  starting transfers between devices  23.5 us (16%)
  Pallas kernels  10.4 us (7%)
    all_to_all x1, blocking collectives, shards(): rows = lax.all_to_all(outgoing, NEAR, 0, 0, tiled=True)  78.2 us
    ppermute x1, waiting for transfers between devices, shards(): lax.ppermute(to_up, 'zh', up)  15.8 us
    all_to_all x1, starting transfers between devices, shards(): lax.all_to_all(asked[:, None, :], EP, 0, 0, tiled=True)  15 us
    all_to_all x1, waiting for transfers between devices, shards(): lax.all_to_all(asked[:, None, :], EP, 0, 0, tiled=True)  10.7 us
    pallas_call x1, Pallas kernels, pick(): pl.pallas_call(pick_kernel, out_shape=jax.ShapeDtypeStruct((targets, line...  4.84 us
    ppermute x1, waiting for transfers between devices, shards(): left = lax.ppermute(left + from_up[:tok_dev], 'zh', up)  4.67 us
    ppermute x1, starting transfers between devices, shards(): right = lax.ppermute(right + from_down[:tok_dev], 'zh', down)  4.02 us
    ppermute x1, starting transfers between devices, shards(): lax.ppermute(to_down, 'zh', down)  3.5 us
  transfers between devices with their start and end apart: 6, of which 4 were waited for; matrix products, arithmetic and copies ran while one was open for 0% of the time, Pallas kernels for 2%

profile of v7, /device:TPU:32, one launch (start us, length us, event | category | flops | bytes accessed | tf_op | source)
XLA Modules:
  0.0 145.2 jit_solution(15331155082669366871)
XLA Ops:
  0.0 0.0 collective-permute-start
  0.0 2.2 %ask.1 = (f32[128,128]{1,0:T(8,128)}, f32[32,128]{1,0:T(8,128)S(1)}) custom-call(s32[1]{0:T(128)} %bitcast.group_ref, s32[12,32]{1,0:T(8,128)} %bitcast.8, f32[12,32]{1,0:T(8,128)} %bitcast.9), custom_call_target="tpu_custom_call" | custom-call | tf_op jit(solution)/shard_map/ask/pallas_call | solution.py:80
  2.2 15.0 %all-to-all-start = ((f32[128,1,128]{2,1,0:T(1,128)}), f32[128,1,128]{2,1,0:T(1,128)S(1)}, u32[]{:S(2)}, u32[]{:S(2)}) async-start(f32[128,1,128]{2,1,0:T(1,128)} %bitcast.4), calls=%async_computation | async-start | bytes 131072 | tf_op jit(solution)/shard_map/all_to_all | solution.py:287
  17.2 0.4 fusion.8
  17.6 10.7 %all-to-all-done = f32[128,1,128]{2,1,0:T(1,128)S(1)} async-done(((f32[128,1,128]{2,1,0:T(1,128)}), f32[128,1,128]{2,1,0:T(1,128)S(1)}, u32[]{:S(2)}, u32[]{:S(2)}) %all-to-all-start) | async-done | bytes 65568 | tf_op jit(solution)/shard_map/all_to_all | solution.py:287
  28.3 0.0 collective-permute-done.taken_ref
  28.3 4.8 %pick.1 = f32[32,392,128]{2,1,0:T(8,128)S(1)} custom-call(s32[1]{0:T(128)} %bitcast.group_ref, f32[128,128]{1,0:T(8,128)S(1)} %bitcast.7, s32[512,1]{1,0:T(8,128)S(1)} %get-tuple-element.18.home_ref, s32[512,1]{1,0:T(8,128)S(1)} %get-tuple-element.19.lane_ref, f32[2,96,6144]{2,1,0:T(8,128)} %own_ref.1, f32[2,96,6144]{2,1,0:T(8,128)} %collective-permute-done.taken_ref), custom_call_target="tpu_custom_call" | custom-call | flops 1207959552 | bytes 11010048 | tf_op jit(solution)/shard_map/pick/pallas_call | solution.py:160
  33.2 78.2 %all_to_all.10.rows_ref = f32[32,392,128]{2,1,0:T(8,128)S(1)} all-to-all(f32[32,392,128]{2,1,0:T(8,128)S(1)} %pick.1), channel_id=1, replica_groups=mesh['grp'=2,'x'=4,'y'=4,'zh'=4,'zl'=2] {'x','y','zl'}, dimensions={0} | all-to-all | bytes 12845056 | tf_op jit(solution)/shard_map/all_to_all | solution.py:301
  111.3 2.6 %combine.1 = (f32[32,3072]{1,0:T(8,128)S(1)}, f32[64,1536]{1,0:T(8,128)S(1)}, f32[64,1536]{1,0:T(8,128)S(1)}, f32[32,1536]{1,0:T(8,128)S(1)}, f32[32,1536]{1,0:T(8,128)S(1)}) custom-call(s32[1]{0:T(128)} %bitcast.group_ref, f32[32,392,128]{2,1,0:T(8,128)S(1)} %all_to_all.10.rows_ref, f32[32,128]{1,0:T(8,128)S(1)} %get-tuple-element.21.ident_ref, ...), custom_call_target="tpu_custom_call" | custom-call | flops 1207959552 | bytes 7864320 | tf_op jit(solution)/shard_map/combine/pallas_call | solution.py:231
  113.9 0.7 collective-permute-start.1
  114.6 3.5 %collective-permute-start.2 = (f32[64,1536]{1,0:T(8,128)S(1)}, f32[64,1536]{1,0:T(8,128)S(1)}, u32[]{:S(2)}, u32[]{:S(2)}) collective-permute-start(f32[64,1536]{1,0:T(8,128)S(1)} %get-tuple-element.24), channel_id=1, source_target_pairs={{0,6},{2,0},{4,2},{6,4},{1,7},{3,1},{5,3},{7,5},{8,14},{10,8},{12,... | collective-permute-start | bytes 1179656 | tf_op jit(solution)/shard_map/ppermute | solution.py:304
  118.1 15.8 %collective-permute-done.1.up_ref = f32[64,1536]{1,0:T(8,128)S(1)} collective-permute-done((f32[64,1536]{1,0:T(8,128)S(1)}, f32[64,1536]{1,0:T(8,128)S(1)}, u32[]{:S(2)}, u32[]{:S(2)}) %collective-permute-start.1) | collective-permute-done | bytes 393248 | tf_op jit(solution)/shard_map/ppermute | solution.py:304
  134.0 0.3 collective-permute-start.3
  134.2 0.0 collective-permute-done.2.down_ref
  134.3 4.0 %collective-permute-start.4 = (f32[32,1536]{1,0:T(8,128)S(1)}, f32[32,1536]{1,0:T(8,128)S(1)}, u32[]{:S(2)}, u32[]{:S(2)}) collective-permute-start(f32[32,1536]{1,0:T(8,128)S(1)} %slice_add_fusion), channel_id=1, source_target_pairs={{0,6},{2,0},{4,2},{6,4},{1,7},{3,1},{5,3},{7,5},{8,14},{10,8},{12,... | collective-permute-start | bytes 589832 | tf_op jit(solution)/shard_map/ppermute | solution.py:306
  138.3 4.7 %collective-permute-done.3.left_ref = f32[32,1536]{1,0:T(8,128)S(1)} collective-permute-done((f32[32,1536]{1,0:T(8,128)S(1)}, f32[32,1536]{1,0:T(8,128)S(1)}, u32[]{:S(2)}, u32[]{:S(2)}) %collective-permute-start.3) | collective-permute-done | bytes 196640 | tf_op jit(solution)/shard_map/ppermute | solution.py:305
  143.0 1.4 collective-permute-done.4.right_ref
  144.3 0.8 finish.1
  (2 shorter events, 0.1 us)
Async XLA Ops:
  0.0 28.3 %collective-permute-start = (f32[2,96,6144]{2,1,0:T(8,128)}, f32[2,96,6144]{2,1,0:T(8,128)}, u32[]{:S(2)}, u32[]{:S(2)}) collective-permute-start(f32[2,96,6144]{2,1,0:T(8,128)} %own_ref.1), channel_id=1, source_target_pairs={{0,128},{128,0},{1,129},{129,1},{2,130},{130,2},{3,131},{131,3},{4... | collective-permute-start | bytes 14155784 | tf_op jit(solution)/shard_map/ppermute | solution.py:283
  2.2 26.1 %all-to-all-start = ((f32[128,1,128]{2,1,0:T(1,128)}), f32[128,1,128]{2,1,0:T(1,128)S(1)}, u32[]{:S(2)}, u32[]{:S(2)}) async-start(f32[128,1,128]{2,1,0:T(1,128)} %bitcast.4), calls=%async_computation | async-start | bytes 131072 | tf_op jit(solution)/shard_map/all_to_all | solution.py:287
  113.9 20.0 %collective-permute-start.1 = (f32[64,1536]{1,0:T(8,128)S(1)}, f32[64,1536]{1,0:T(8,128)S(1)}, u32[]{:S(2)}, u32[]{:S(2)}) collective-permute-start(f32[64,1536]{1,0:T(8,128)S(1)} %get-tuple-element.23), channel_id=1, source_target_pairs={{0,2},{2,4},{4,6},{6,0},{1,3},{3,5},{5,7},{7,1},{8,10},{10,12},{12... | collective-permute-start | bytes 1179656 | tf_op jit(solution)/shard_map/ppermute | solution.py:304
  114.6 19.6 %collective-permute-start.2 = (f32[64,1536]{1,0:T(8,128)S(1)}, f32[64,1536]{1,0:T(8,128)S(1)}, u32[]{:S(2)}, u32[]{:S(2)}) collective-permute-start(f32[64,1536]{1,0:T(8,128)S(1)} %get-tuple-element.24), channel_id=1, source_target_pairs={{0,6},{2,0},{4,2},{6,4},{1,7},{3,1},{5,3},{7,5},{8,14},{10,8},{12,... | collective-permute-start | bytes 1179656 | tf_op jit(solution)/shard_map/ppermute | solution.py:304
  134.0 9.0 %collective-permute-start.3 = (f32[32,1536]{1,0:T(8,128)S(1)}, f32[32,1536]{1,0:T(8,128)S(1)}, u32[]{:S(2)}, u32[]{:S(2)}) collective-permute-start(f32[32,1536]{1,0:T(8,128)S(1)} %slice_add_fusion.1), channel_id=1, source_target_pairs={{0,2},{2,4},{4,6},{6,0},{1,3},{3,5},{5,7},{7,1},{8,10},{10,12},{12... | collective-permute-start | bytes 589832 | tf_op jit(solution)/shard_map/ppermute | solution.py:305
  134.3 10.1 %collective-permute-start.4 = (f32[32,1536]{1,0:T(8,128)S(1)}, f32[32,1536]{1,0:T(8,128)S(1)}, u32[]{:S(2)}, u32[]{:S(2)}) collective-permute-start(f32[32,1536]{1,0:T(8,128)S(1)} %slice_add_fusion), channel_id=1, source_target_pairs={{0,6},{2,0},{4,2},{6,4},{1,7},{3,1},{5,3},{7,5},{8,14},{10,8},{12,... | collective-permute-start | bytes 589832 | tf_op jit(solution)/shard_map/ppermute | solution.py:306

commit v8 on v7

--- a/solution.py
+++ b/solution.py
@@ -174,22 +174,15 @@
     )(group, chosen, home, lane, own, taken)
 
 
-def combine_kernel(
-    group_ref, rows_ref, ident_ref, tokens_ref, base_ref, up_ref, down_ref, left_ref, right_ref, own, arrived, *, exp_dev
-):
-    tok_dev, half = base_ref.shape
-    copy = pltpu.make_async_copy(
-        tokens_ref.at[:, pl.ds(pl.multiple_of(group_ref[0] * half, half), half)], own, arrived
-    )
-    copy.start()
+def mixed(rows_ref, tok_dev, exp_dev, offsets):
+    far = 4
     sources, lines, group = rows_ref.shape
-    far = 4
     rows = far * exp_dev
-    count = far * tok_dev
+    count = len(offsets) * tok_dev
     note = rows_ref[:, lines - rows :, :].reshape(sources * rows, group)
     line = lax.broadcasted_iota(jnp.int32, (sources * rows, count), 0)
     out_line = lax.broadcasted_iota(jnp.int32, (sources * rows, count), 1)
-    fits = lax.div(lax.rem(line, rows), exp_dev) == lax.div(out_line, tok_dev)
+    fits = lax.div(lax.rem(line, rows), exp_dev) == lax.div(out_line, tok_dev) + offsets[0]
     token = jnp.where(fits, lax.rem(out_line, tok_dev) + 1, -1).astype(jnp.float32)
     sides = []
     for side in range(2):
@@ -200,55 +193,77 @@
     m_high, m_middle, _ = halves(mix)
     both = jnp.concatenate([m_high, m_middle], axis=0)
     per = BLOCK // group
-    steps = half // BLOCK
-    copy.wait()
-    ident = ident_ref[:, 0:1]
-    for i in range(steps):
+    for i in range((lines - rows) // (2 * rows * per)):
         parts = [rows_ref[:, 2 * rows * (i * per + j) : 2 * rows * (i * per + j + 1), :] for j in range(per)]
         block = jnp.concatenate([part.reshape(2 * sources * rows, group) for part in parts], axis=1)
         high, middle, _ = halves(block)
         value = mul(both, high)
         value = value[:count] + (value[count:] + mul(m_high, middle))
-        near, nxt, opposite, prev = (value[o * tok_dev : (o + 1) * tok_dev] for o in range(far))
+        yield i, [value[o * tok_dev : (o + 1) * tok_dev] for o in range(len(offsets))]
+
+
+def combine_kernel(rows_ref, far_up, far_down, near_left, near_right, prev_left, prev_right, *, exp_dev):
+    tok_dev, cut = far_up.shape
+    for i, (nxt, opposite, prev) in mixed(rows_ref, tok_dev, exp_dev, (1, 2, 3)):
+        first = i * BLOCK < cut
+        here = slice(i * BLOCK % cut, i * BLOCK % cut + BLOCK)
+        (far_up if first else far_down)[:, here] = opposite
+        (near_left if first else near_right)[:, here] = nxt
+        (prev_left if first else prev_right)[:, here] = prev
+
+
+def own_kernel(group_ref, rows_ref, ident_ref, tokens_ref, base_ref, own, arrived, *, exp_dev):
+    tok_dev, half = base_ref.shape
+    copy = pltpu.make_async_copy(
+        tokens_ref.at[:, pl.ds(pl.multiple_of(group_ref[0] * half, half), half)], own, arrived
+    )
+    copy.start()
+    copy.wait()
+    for i, (near,) in mixed(rows_ref, tok_dev, exp_dev, (0,)):
         here = slice(i * BLOCK, (i + 1) * BLOCK)
-        base_ref[:, here] = near + ident * own[:, here]
-        side = slice(i % (steps // 2) * BLOCK, (i % (steps // 2) + 1) * BLOCK)
-        if i < steps // 2:
-            up_ref[:tok_dev, side] = opposite
-            down_ref[tok_dev:, side] = prev
-            left_ref[:, side] = nxt
-        else:
-            down_ref[:tok_dev, side] = opposite
-            up_ref[tok_dev:, side] = nxt
-            right_ref[:, side] = prev
-
-
-def combine(group, rows, ident, tokens, exp_dev):
+        base_ref[:, here] = near + ident_ref[:, 0:1] * own[:, here]
+
+
+def cost(offsets, tok_dev, rows, half):
+    depth = rows.shape[0] * (rows.shape[1] * 128 // half)
+    return pl.CostEstimate(
+        flops=6 * offsets * tok_dev * depth * half, bytes_accessed=4 * depth * half, transcendentals=0
+    )
+
+
+def combine(rows, tok_dev, half, exp_dev):
+    vmem = pl.BlockSpec(memory_space=pltpu.VMEM)
+    return pl.pallas_call(
+        functools.partial(combine_kernel, exp_dev=exp_dev),
+        out_shape=[jax.ShapeDtypeStruct((tok_dev, half // 2), jnp.float32)] * 6,
+        in_specs=[vmem],
+        out_specs=[vmem] * 6,
+        compiler_params=pltpu.CompilerParams(vmem_limit_bytes=MIX_VMEM),
+        cost_estimate=cost(3, tok_dev, rows, half),
+        name="combine",
+    )(rows)
+
+
+def own_sum(group, rows, ident, tokens, exp_dev):
     tok_dev, width = tokens.shape
     half = width // 2
-    count, depth = 4 * tok_dev, 8 * rows.shape[0] * exp_dev
-    vmem = pl.BlockSpec(memory_space=pltpu.VMEM)
-    return pl.pallas_call(
-        functools.partial(combine_kernel, exp_dev=exp_dev),
-        out_shape=[
-            jax.ShapeDtypeStruct(shape, jnp.float32)
-            for shape in ((tok_dev, half), *[(2 * tok_dev, half // 2)] * 2, *[(tok_dev, half // 2)] * 2)
-        ],
+    vmem = pl.BlockSpec(memory_space=pltpu.VMEM)
+    return pl.pallas_call(
+        functools.partial(own_kernel, exp_dev=exp_dev),
+        out_shape=jax.ShapeDtypeStruct((tok_dev, half), jnp.float32),
         in_specs=[pl.BlockSpec(memory_space=pltpu.SMEM), vmem, vmem, pl.BlockSpec(memory_space=pl.ANY)],
-        out_specs=[vmem] * 5,
+        out_specs=vmem,
         scratch_shapes=[pltpu.VMEM((tok_dev, half), jnp.float32), pltpu.SemaphoreType.DMA],
         compiler_params=pltpu.CompilerParams(vmem_limit_bytes=MIX_VMEM),
-        cost_estimate=pl.CostEstimate(
-            flops=6 * count * depth * half, bytes_accessed=4 * (count + depth) * half, transcendentals=0
-        ),
-        name="combine",
+        cost_estimate=cost(1, tok_dev, rows, half),
+        name="own_sum",
     )(group, rows, ident, in_hbm(tokens))
 
 
-def finish_kernel(base_ref, up_ref, down_ref, left_ref, right_ref, out_ref):
-    tok_dev, cut = left_ref.shape
-    out_ref[:, :cut] = base_ref[:, :cut] + down_ref[tok_dev:, :] + left_ref[...]
-    out_ref[:, cut:] = base_ref[:, cut:] + up_ref[tok_dev:, :] + right_ref[...]
+def finish_kernel(base_ref, left_ref, more_left_ref, right_ref, more_right_ref, out_ref):
+    _, cut = left_ref.shape
+    out_ref[:, :cut] = base_ref[:, :cut] + more_left_ref[...] + left_ref[...]
+    out_ref[:, cut:] = base_ref[:, cut:] + more_right_ref[...] + right_ref[...]
 
 
 def finish(base, *parts):
@@ -300,11 +315,13 @@
 
     rows = lax.all_to_all(outgoing, NEAR, 0, 0, tiled=True)
     up, down = shift(far, 1), shift(far, -1)
-    base, to_up, to_down, left, right = combine(group_word, rows, ident, tokens, exp_dev)
-    from_up, from_down = lax.ppermute(to_up, "zh", up), lax.ppermute(to_down, "zh", down)
-    left = lax.ppermute(left + from_up[:tok_dev], "zh", up)
-    right = lax.ppermute(right + from_down[:tok_dev], "zh", down)
-    return finish(base, from_up, from_down, left, right)
+    far_up, far_down, near_left, near_right, prev_left, prev_right = combine(rows, tok_dev, half, exp_dev)
+    far_up, far_down = lax.ppermute(far_up, "zh", up), lax.ppermute(far_down, "zh", down)
+    more_right, more_left = lax.ppermute(near_right, "zh", up), lax.ppermute(prev_left, "zh", down)
+    base = own_sum(group_word, rows, ident, tokens, exp_dev)
+    left = lax.ppermute(near_left + far_up, "zh", up)
+    right = lax.ppermute(prev_right + far_down, "zh", down)
+    return finish(base, left, more_left, right, more_right)
 
 
 def solution(mesh):

time: 147 us -> 143 us (0.973); the launches traced: 145 us -> 143 us
  waiting for transfers between devices: 32.6 us -> 25.7 us
  starting transfers between devices: 23.5 us -> 26.4 us
  Pallas kernels: 10.4 us -> 12.2 us
    ppermute x4 -> x6, waiting for transfers between devices: 21.9 us -> 15 us  [the longest x1 9.12 us: shards(): lax.ppermute(far_up, 'zh', up)]
    ppermute x4 -> x6, starting transfers between devices: 8.5 us -> 11.4 us  [the longest x1 4.19 us: shards(): right = lax.ppermute(prev_right + far_down, 'zh', down)]
    pallas_call x0 -> x1, Pallas kernels: none -> 2.56 us  [own_sum(): pl.pallas_call(functools.partial(own_kernel, exp_dev=exp_dev), out_shape=...]
  transfers between devices with their start and end apart: 6 -> 8, of which waited for: 4 -> 5; matrix products, arithmetic and copies ran while one was open for 0% -> 0% of each run, Pallas kernels for 2% -> 3%
where the time goes in v8:
time: 143 us
  blocking collectives  78.2 us (55%)
  starting transfers between devices  26.4 us (18%)
  waiting for transfers between devices  25.7 us (18%)
  Pallas kernels  12.2 us (9%)
    all_to_all x1, blocking collectives, shards(): rows = lax.all_to_all(outgoing, NEAR, 0, 0, tiled=True)  78.2 us
    all_to_all x1, starting transfers between devices, shards(): lax.all_to_all(asked[:, None, :], EP, 0, 0, tiled=True)  15 us
    all_to_all x1, waiting for transfers between devices, shards(): lax.all_to_all(asked[:, None, :], EP, 0, 0, tiled=True)  10.7 us
    ppermute x1, waiting for transfers between devices, shards(): lax.ppermute(far_up, 'zh', up)  9.12 us
    pallas_call x1, Pallas kernels, pick(): pl.pallas_call(pick_kernel, out_shape=jax.ShapeDtypeStruct((targets, line...  4.84 us
    ppermute x1, starting transfers between devices, shards(): right = lax.ppermute(prev_right + far_down, 'zh', down)  4.19 us
    ppermute x1, starting transfers between devices, shards(): lax.ppermute(far_down, 'zh', down)  3.5 us
  transfers between devices with their start and end apart: 8, of which 5 were waited for; matrix products, arithmetic and copies ran while one was open for 0% of the time, Pallas kernels for 3%

profile of v8, /device:TPU:32, one launch (start us, length us, event | category | flops | bytes accessed | tf_op | source)
XLA Modules:
  0.0 143.0 jit_solution(5246797626444360902)
XLA Ops:
  0.0 0.0 collective-permute-start
  0.0 2.2 %ask.1 = (f32[128,128]{1,0:T(8,128)}, f32[32,128]{1,0:T(8,128)S(1)}) custom-call(s32[1]{0:T(128)} %bitcast.group_ref, s32[12,32]{1,0:T(8,128)} %bitcast.8, f32[12,32]{1,0:T(8,128)} %bitcast.9), custom_call_target="tpu_custom_call" | custom-call | tf_op jit(solution)/shard_map/ask/pallas_call | solution.py:80
  2.2 15.0 %all-to-all-start = ((f32[128,1,128]{2,1,0:T(1,128)}), f32[128,1,128]{2,1,0:T(1,128)S(1)}, u32[]{:S(2)}, u32[]{:S(2)}) async-start(f32[128,1,128]{2,1,0:T(1,128)} %bitcast.4), calls=%async_computation | async-start | bytes 131072 | tf_op jit(solution)/shard_map/all_to_all | solution.py:302
  17.2 0.4 fusion.8
  17.6 10.7 %all-to-all-done = f32[128,1,128]{2,1,0:T(1,128)S(1)} async-done(((f32[128,1,128]{2,1,0:T(1,128)}), f32[128,1,128]{2,1,0:T(1,128)S(1)}, u32[]{:S(2)}, u32[]{:S(2)}) %all-to-all-start) | async-done | bytes 65568 | tf_op jit(solution)/shard_map/all_to_all | solution.py:302
  28.3 0.0 collective-permute-done.taken_ref
  28.3 4.8 %pick.1 = f32[32,392,128]{2,1,0:T(8,128)S(1)} custom-call(s32[1]{0:T(128)} %bitcast.group_ref, f32[128,128]{1,0:T(8,128)S(1)} %bitcast.7, s32[512,1]{1,0:T(8,128)S(1)} %get-tuple-element.19.home_ref, s32[512,1]{1,0:T(8,128)S(1)} %get-tuple-element.20.lane_ref, f32[2,96,6144]{2,1,0:T(8,128)} %own_ref.1, f32[2,96,6144]{2,1,0:T(8,128)} %collective-permute-done.taken_ref), custom_call_target="tpu_custom_call" | custom-call | flops 1207959552 | bytes 11010048 | tf_op jit(solution)/shard_map/pick/pallas_call | solution.py:160
  33.2 78.2 %all_to_all.10.rows_ref = f32[32,392,128]{2,1,0:T(8,128)S(1)} all-to-all(f32[32,392,128]{2,1,0:T(8,128)S(1)} %pick.1), channel_id=1, replica_groups=mesh['grp'=2,'x'=4,'y'=4,'zh'=4,'zl'=2] {'x','y','zl'}, dimensions={0} | all-to-all | bytes 12845056 | tf_op jit(solution)/shard_map/all_to_all | solution.py:316
  111.3 1.8 %combine.1 = (f32[32,1536]{1,0:T(8,128)S(1)}, f32[32,1536]{1,0:T(8,128)S(1)}, f32[32,1536]{1,0:T(8,128)S(1)}, f32[32,1536]{1,0:T(8,128)S(1)}, f32[32,1536]{1,0:T(8,128)S(1)}, /*index=5*/f32[32,1536]{1,0:T(8,128)S(1)}) custom-call(f32[32,392,128]{2,1,0:T(8,128)S(1)} %all_to_all.10.rows_ref), custom_call_target="tpu_custom_call" | custom-call | flops 905969664 | bytes 6291456 | tf_op jit(solution)/shard_map/combine/pallas_call | solution.py:236
  113.1 0.7 collective-permute-start.1
  113.8 3.5 %collective-permute-start.4 = (f32[32,1536]{1,0:T(8,128)S(1)}, f32[32,1536]{1,0:T(8,128)S(1)}, u32[]{:S(2)}, u32[]{:S(2)}) collective-permute-start(f32[32,1536]{1,0:T(8,128)S(1)} %get-tuple-element.27), channel_id=1, source_target_pairs={{0,6},{2,0},{4,2},{6,4},{1,7},{3,1},{5,3},{7,5},{8,14},{10,8},{12,... | collective-permute-start | bytes 589832 | tf_op jit(solution)/shard_map/ppermute | solution.py:319
  117.3 0.8 collective-permute-start.3
  118.1 2.1 %collective-permute-start.6 = (f32[32,1536]{1,0:T(8,128)S(1)}, f32[32,1536]{1,0:T(8,128)S(1)}, u32[]{:S(2)}, u32[]{:S(2)}) collective-permute-start(f32[32,1536]{1,0:T(8,128)S(1)} %get-tuple-element.28), channel_id=1, source_target_pairs={{0,2},{2,4},{4,6},{6,0},{1,3},{3,5},{5,7},{7,1},{8,10},{10,12},{12... | collective-permute-start | bytes 589832 | tf_op jit(solution)/shard_map/ppermute | solution.py:320
  120.2 9.1 %collective-permute-done.1 = f32[32,1536]{1,0:T(8,128)S(1)} collective-permute-done((f32[32,1536]{1,0:T(8,128)S(1)}, f32[32,1536]{1,0:T(8,128)S(1)}, u32[]{:S(2)}, u32[]{:S(2)}) %collective-permute-start.1) | collective-permute-done | bytes 196640 | tf_op jit(solution)/shard_map/ppermute | solution.py:319
  129.4 0.1 collective-permute-start.2
  129.5 0.0 collective-permute-done.4
  129.5 4.2 %collective-permute-start.5 = (f32[32,1536]{1,0:T(8,128)S(1)}, f32[32,1536]{1,0:T(8,128)S(1)}, u32[]{:S(2)}, u32[]{:S(2)}) collective-permute-start(f32[32,1536]{1,0:T(8,128)S(1)} %add.164), channel_id=1, source_target_pairs={{0,6},{2,0},{4,2},{6,4},{1,7},{3,1},{5,3},{7,5},{8,14},{10,8},{12,... | collective-permute-start | bytes 589832 | tf_op jit(solution)/shard_map/ppermute | solution.py:323
  133.7 2.6 %own_sum.1.base_ref = f32[32,3072]{1,0:T(8,128)S(1)} custom-call(s32[1]{0:T(128)} %bitcast.group_ref, f32[32,392,128]{2,1,0:T(8,128)S(1)} %all_to_all.10.rows_ref, f32[32,128]{1,0:T(8,128)S(1)} %get-tuple-element.22.ident_ref, f32[32,6144]{1,0:T(8,128)} %tokens_ref.1), custom_call_target="tpu_custom_call" | custom-call | flops 301989888 | bytes 6291456 | tf_op jit(solution)/shard_map/own_sum/pallas_call | solution.py:251
  136.3 0.0 collective-permute-done.3.more_left_ref
  136.3 2.8 %collective-permute-done.6.more_right_ref = f32[32,1536]{1,0:T(8,128)S(1)} collective-permute-done((f32[32,1536]{1,0:T(8,128)S(1)}, f32[32,1536]{1,0:T(8,128)S(1)}, u32[]{:S(2)}, u32[]{:S(2)}) %collective-permute-start.6) | collective-permute-done | bytes 196640 | tf_op jit(solution)/shard_map/ppermute | solution.py:320
  139.1 2.4 %collective-permute-done.2.left_ref = f32[32,1536]{1,0:T(8,128)S(1)} collective-permute-done((f32[32,1536]{1,0:T(8,128)S(1)}, f32[32,1536]{1,0:T(8,128)S(1)}, u32[]{:S(2)}, u32[]{:S(2)}) %collective-permute-start.2) | collective-permute-done | bytes 196640 | tf_op jit(solution)/shard_map/ppermute | solution.py:322
  141.4 0.7 collective-permute-done.5.right_ref
  142.2 0.8 finish.1
  (2 shorter events, 0.1 us)
Async XLA Ops:
  0.0 28.3 %collective-permute-start = (f32[2,96,6144]{2,1,0:T(8,128)}, f32[2,96,6144]{2,1,0:T(8,128)}, u32[]{:S(2)}, u32[]{:S(2)}) collective-permute-start(f32[2,96,6144]{2,1,0:T(8,128)} %own_ref.1), channel_id=1, source_target_pairs={{0,128},{128,0},{1,129},{129,1},{2,130},{130,2},{3,131},{131,3},{4... | collective-permute-start | bytes 14155784 | tf_op jit(solution)/shard_map/ppermute | solution.py:298
  2.2 26.1 %all-to-all-start = ((f32[128,1,128]{2,1,0:T(1,128)}), f32[128,1,128]{2,1,0:T(1,128)S(1)}, u32[]{:S(2)}, u32[]{:S(2)}) async-start(f32[128,1,128]{2,1,0:T(1,128)} %bitcast.4), calls=%async_computation | async-start | bytes 131072 | tf_op jit(solution)/shard_map/all_to_all | solution.py:302
  113.1 16.3 %collective-permute-start.1 = (f32[32,1536]{1,0:T(8,128)S(1)}, f32[32,1536]{1,0:T(8,128)S(1)}, u32[]{:S(2)}, u32[]{:S(2)}) collective-permute-start(f32[32,1536]{1,0:T(8,128)S(1)} %get-tuple-element.24), channel_id=1, source_target_pairs={{0,2},{2,4},{4,6},{6,0},{1,3},{3,5},{5,7},{7,1},{8,10},{10,12},{12... | collective-permute-start | bytes 589832 | tf_op jit(solution)/shard_map/ppermute | solution.py:319
  113.8 15.7 %collective-permute-start.4 = (f32[32,1536]{1,0:T(8,128)S(1)}, f32[32,1536]{1,0:T(8,128)S(1)}, u32[]{:S(2)}, u32[]{:S(2)}) collective-permute-start(f32[32,1536]{1,0:T(8,128)S(1)} %get-tuple-element.27), channel_id=1, source_target_pairs={{0,6},{2,0},{4,2},{6,4},{1,7},{3,1},{5,3},{7,5},{8,14},{10,8},{12,... | collective-permute-start | bytes 589832 | tf_op jit(solution)/shard_map/ppermute | solution.py:319
  117.3 19.0 %collective-permute-start.3 = (f32[32,1536]{1,0:T(8,128)S(1)}, f32[32,1536]{1,0:T(8,128)S(1)}, u32[]{:S(2)}, u32[]{:S(2)}) collective-permute-start(f32[32,1536]{1,0:T(8,128)S(1)} %get-tuple-element.25), channel_id=1, source_target_pairs={{0,6},{2,0},{4,2},{6,4},{1,7},{3,1},{5,3},{7,5},{8,14},{10,8},{12,... | collective-permute-start | bytes 589832 | tf_op jit(solution)/shard_map/ppermute | solution.py:320
  118.1 20.9 %collective-permute-start.6 = (f32[32,1536]{1,0:T(8,128)S(1)}, f32[32,1536]{1,0:T(8,128)S(1)}, u32[]{:S(2)}, u32[]{:S(2)}) collective-permute-start(f32[32,1536]{1,0:T(8,128)S(1)} %get-tuple-element.28), channel_id=1, source_target_pairs={{0,2},{2,4},{4,6},{6,0},{1,3},{3,5},{5,7},{7,1},{8,10},{10,12},{12... | collective-permute-start | bytes 589832 | tf_op jit(solution)/shard_map/ppermute | solution.py:320
  129.4 12.1 %collective-permute-start.2 = (f32[32,1536]{1,0:T(8,128)S(1)}, f32[32,1536]{1,0:T(8,128)S(1)}, u32[]{:S(2)}, u32[]{:S(2)}) collective-permute-start(f32[32,1536]{1,0:T(8,128)S(1)} %add.163), channel_id=1, source_target_pairs={{0,2},{2,4},{4,6},{6,0},{1,3},{3,5},{5,7},{7,1},{8,10},{10,12},{12... | collective-permute-start | bytes 589832 | tf_op jit(solution)/shard_map/ppermute | solution.py:322
  129.5 12.7 %collective-permute-start.5 = (f32[32,1536]{1,0:T(8,128)S(1)}, f32[32,1536]{1,0:T(8,128)S(1)}, u32[]{:S(2)}, u32[]{:S(2)}) collective-permute-start(f32[32,1536]{1,0:T(8,128)S(1)} %add.164), channel_id=1, source_target_pairs={{0,6},{2,0},{4,2},{6,4},{1,7},{3,1},{5,3},{7,5},{8,14},{10,8},{12,... | collective-permute-start | bytes 589832 | tf_op jit(solution)/shard_map/ppermute | solution.py:323

commit v9 on v8

--- a/solution.py
+++ b/solution.py
@@ -182,7 +182,7 @@
     note = rows_ref[:, lines - rows :, :].reshape(sources * rows, group)
     line = lax.broadcasted_iota(jnp.int32, (sources * rows, count), 0)
     out_line = lax.broadcasted_iota(jnp.int32, (sources * rows, count), 1)
-    fits = lax.div(lax.rem(line, rows), exp_dev) == lax.div(out_line, tok_dev) + offsets[0]
+    fits = lax.div(lax.rem(line, rows), exp_dev) == lax.rem(lax.div(out_line, tok_dev) + offsets[0], far)
     token = jnp.where(fits, lax.rem(out_line, tok_dev) + 1, -1).astype(jnp.float32)
     sides = []
     for side in range(2):
@@ -202,26 +202,31 @@
         yield i, [value[o * tok_dev : (o + 1) * tok_dev] for o in range(len(offsets))]
 
 
-def combine_kernel(rows_ref, far_up, far_down, near_left, near_right, prev_left, prev_right, *, exp_dev):
-    tok_dev, cut = far_up.shape
-    for i, (nxt, opposite, prev) in mixed(rows_ref, tok_dev, exp_dev, (1, 2, 3)):
-        first = i * BLOCK < cut
+def far_kernel(rows_ref, up_ref, down_ref, *, exp_dev):
+    tok_dev, cut = up_ref.shape
+    for i, (opposite,) in mixed(rows_ref, tok_dev, exp_dev, (2,)):
         here = slice(i * BLOCK % cut, i * BLOCK % cut + BLOCK)
-        (far_up if first else far_down)[:, here] = opposite
-        (near_left if first else near_right)[:, here] = nxt
-        (prev_left if first else prev_right)[:, here] = prev
-
-
-def own_kernel(group_ref, rows_ref, ident_ref, tokens_ref, base_ref, own, arrived, *, exp_dev):
+        (up_ref if i * BLOCK < cut else down_ref)[:, here] = opposite
+
+
+def rest_kernel(
+    group_ref, rows_ref, ident_ref, tokens_ref, base_ref, near_left, near_right, prev_left, prev_right, own, arrived, *, exp_dev
+):
     tok_dev, half = base_ref.shape
+    cut = half // 2
     copy = pltpu.make_async_copy(
         tokens_ref.at[:, pl.ds(pl.multiple_of(group_ref[0] * half, half), half)], own, arrived
     )
     copy.start()
-    copy.wait()
-    for i, (near,) in mixed(rows_ref, tok_dev, exp_dev, (0,)):
+    for i, (prev, home, nxt) in mixed(rows_ref, tok_dev, exp_dev, (3, 0, 1)):
+        if i == 0:
+            copy.wait()
         here = slice(i * BLOCK, (i + 1) * BLOCK)
-        base_ref[:, here] = near + ident_ref[:, 0:1] * own[:, here]
+        base_ref[:, here] = home + ident_ref[:, 0:1] * own[:, here]
+        first = i * BLOCK < cut
+        here = slice(i * BLOCK % cut, i * BLOCK % cut + BLOCK)
+        (near_left if first else near_right)[:, here] = nxt
+        (prev_left if first else prev_right)[:, here] = prev
 
 
 def cost(offsets, tok_dev, rows, half):
@@ -231,32 +236,33 @@
     )
 
 
-def combine(rows, tok_dev, half, exp_dev):
-    vmem = pl.BlockSpec(memory_space=pltpu.VMEM)
-    return pl.pallas_call(
-        functools.partial(combine_kernel, exp_dev=exp_dev),
-        out_shape=[jax.ShapeDtypeStruct((tok_dev, half // 2), jnp.float32)] * 6,
+def far_sum(rows, tok_dev, half, exp_dev):
+    vmem = pl.BlockSpec(memory_space=pltpu.VMEM)
+    return pl.pallas_call(
+        functools.partial(far_kernel, exp_dev=exp_dev),
+        out_shape=[jax.ShapeDtypeStruct((tok_dev, half // 2), jnp.float32)] * 2,
         in_specs=[vmem],
-        out_specs=[vmem] * 6,
+        out_specs=[vmem] * 2,
+        compiler_params=pltpu.CompilerParams(vmem_limit_bytes=MIX_VMEM),
+        cost_estimate=cost(1, tok_dev, rows, half),
+        name="far_sum",
+    )(rows)
+
+
+def rest_sum(group, rows, ident, tokens, exp_dev):
+    tok_dev, width = tokens.shape
+    half = width // 2
+    vmem = pl.BlockSpec(memory_space=pltpu.VMEM)
+    return pl.pallas_call(
+        functools.partial(rest_kernel, exp_dev=exp_dev),
+        out_shape=[jax.ShapeDtypeStruct((tok_dev, half), jnp.float32)]
+        + [jax.ShapeDtypeStruct((tok_dev, half // 2), jnp.float32)] * 4,
+        in_specs=[pl.BlockSpec(memory_space=pltpu.SMEM), vmem, vmem, pl.BlockSpec(memory_space=pl.ANY)],
+        out_specs=[vmem] * 5,
+        scratch_shapes=[pltpu.VMEM((tok_dev, half), jnp.float32), pltpu.SemaphoreType.DMA],
         compiler_params=pltpu.CompilerParams(vmem_limit_bytes=MIX_VMEM),
         cost_estimate=cost(3, tok_dev, rows, half),
-        name="combine",
-    )(rows)
-
-
-def own_sum(group, rows, ident, tokens, exp_dev):
-    tok_dev, width = tokens.shape
-    half = width // 2
-    vmem = pl.BlockSpec(memory_space=pltpu.VMEM)
-    return pl.pallas_call(
-        functools.partial(own_kernel, exp_dev=exp_dev),
-        out_shape=jax.ShapeDtypeStruct((tok_dev, half), jnp.float32),
-        in_specs=[pl.BlockSpec(memory_space=pltpu.SMEM), vmem, vmem, pl.BlockSpec(memory_space=pl.ANY)],
-        out_specs=vmem,
-        scratch_shapes=[pltpu.VMEM((tok_dev, half), jnp.float32), pltpu.SemaphoreType.DMA],
-        compiler_params=pltpu.CompilerParams(vmem_limit_bytes=MIX_VMEM),
-        cost_estimate=cost(1, tok_dev, rows, half),
-        name="own_sum",
+        name="rest_sum",
     )(group, rows, ident, in_hbm(tokens))
 
 
@@ -315,10 +321,11 @@
 
     rows = lax.all_to_all(outgoing, NEAR, 0, 0, tiled=True)
     up, down = shift(far, 1), shift(far, -1)
-    far_up, far_down, near_left, near_right, prev_left, prev_right = combine(rows, tok_dev, half, exp_dev)
+    far_up, far_down = far_sum(rows, tok_dev, half, exp_dev)
+    rows, far_up, far_down = lax.optimization_barrier((rows, far_up, far_down))
     far_up, far_down = lax.ppermute(far_up, "zh", up), lax.ppermute(far_down, "zh", down)
+    base, near_left, near_right, prev_left, prev_right = rest_sum(group_word, rows, ident, tokens, exp_dev)
     more_right, more_left = lax.ppermute(near_right, "zh", up), lax.ppermute(prev_left, "zh", down)
-    base = own_sum(group_word, rows, ident, tokens, exp_dev)
     left = lax.ppermute(near_left + far_up, "zh", up)
     right = lax.ppermute(prev_right + far_down, "zh", down)
     return finish(base, left, more_left, right, more_right)

time: 143 us -> 143 us (level); the launches traced: 143 us -> 141 us
  waiting for transfers between devices: 25.7 us -> 23.7 us
    ppermute x1, waiting for transfers between devices: 9.12 us -> 3.96 us  [shards(): lax.ppermute(far_up, 'zh', up)]
    ppermute x1, waiting for transfers between devices: 0.01 us -> 3.19 us  [shards(): lax.ppermute(prev_left, 'zh', down)]
    ppermute x1, waiting for transfers between devices: 2.78 us -> 0.01 us  [shards(): lax.ppermute(near_right, 'zh', up)]
    ppermute x1, waiting for transfers between devices: 2.39 us -> 4.67 us  [shards(): left = lax.ppermute(near_left + far_up, 'zh', up)]
where the time goes in v9:
time: 143 us; the launch traced here: 141 us
  blocking collectives  78.2 us (55%)
  starting transfers between devices  27 us (19%)
  waiting for transfers between devices  23.7 us (17%)
  Pallas kernels  11.8 us (8%)
    all_to_all x1, blocking collectives, shards(): rows = lax.all_to_all(outgoing, NEAR, 0, 0, tiled=True)  78.2 us
    all_to_all x1, starting transfers between devices, shards(): lax.all_to_all(asked[:, None, :], EP, 0, 0, tiled=True)  15 us
    all_to_all x1, waiting for transfers between devices, shards(): lax.all_to_all(asked[:, None, :], EP, 0, 0, tiled=True)  10.7 us
    pallas_call x1, Pallas kernels, pick(): pl.pallas_call(pick_kernel, out_shape=jax.ShapeDtypeStruct((targets, line...  4.84 us
    ppermute x1, starting transfers between devices, shards(): right = lax.ppermute(prev_right + far_down, 'zh', down)  4.74 us
    ppermute x1, waiting for transfers between devices, shards(): left = lax.ppermute(near_left + far_up, 'zh', up)  4.67 us
    ppermute x1, waiting for transfers between devices, shards(): lax.ppermute(far_up, 'zh', up)  3.96 us
    ppermute x1, starting transfers between devices, shards(): lax.ppermute(far_down, 'zh', down)  3.5 us
  transfers between devices with their start and end apart: 8, of which 5 were waited for; matrix products, arithmetic and copies ran while one was open for 0% of the time, Pallas kernels for 3%

profile of v9, /device:TPU:32, one launch (start us, length us, event | category | flops | bytes accessed | tf_op | source)
XLA Modules:
  0.0 141.2 jit_solution(12642895311571135391)
XLA Ops:
  0.0 0.0 collective-permute-start
  0.0 2.2 %ask.1 = (f32[128,128]{1,0:T(8,128)}, f32[32,128]{1,0:T(8,128)S(1)}) custom-call(s32[1]{0:T(128)} %bitcast.group_ref, s32[12,32]{1,0:T(8,128)} %bitcast.8, f32[12,32]{1,0:T(8,128)} %bitcast.9), custom_call_target="tpu_custom_call" | custom-call | tf_op jit(solution)/shard_map/ask/pallas_call | solution.py:80
  2.2 15.0 %all-to-all-start = ((f32[128,1,128]{2,1,0:T(1,128)}), f32[128,1,128]{2,1,0:T(1,128)S(1)}, u32[]{:S(2)}, u32[]{:S(2)}) async-start(f32[128,1,128]{2,1,0:T(1,128)} %bitcast.4), calls=%async_computation | async-start | bytes 131072 | tf_op jit(solution)/shard_map/all_to_all | solution.py:308
  17.2 0.4 fusion.8
  17.6 10.7 %all-to-all-done = f32[128,1,128]{2,1,0:T(1,128)S(1)} async-done(((f32[128,1,128]{2,1,0:T(1,128)}), f32[128,1,128]{2,1,0:T(1,128)S(1)}, u32[]{:S(2)}, u32[]{:S(2)}) %all-to-all-start) | async-done | bytes 65568 | tf_op jit(solution)/shard_map/all_to_all | solution.py:308
  28.3 0.0 collective-permute-done.taken_ref
  28.3 4.8 %pick.1 = f32[32,392,128]{2,1,0:T(8,128)S(1)} custom-call(s32[1]{0:T(128)} %bitcast.group_ref, f32[128,128]{1,0:T(8,128)S(1)} %bitcast.7, s32[512,1]{1,0:T(8,128)S(1)} %get-tuple-element.23.home_ref, s32[512,1]{1,0:T(8,128)S(1)} %get-tuple-element.24.lane_ref, f32[2,96,6144]{2,1,0:T(8,128)} %own_ref.1, f32[2,96,6144]{2,1,0:T(8,128)} %collective-permute-done.taken_ref), custom_call_target="tpu_custom_call" | custom-call | flops 1207959552 | bytes 11010048 | tf_op jit(solution)/shard_map/pick/pallas_call | solution.py:160
  33.2 78.2 %all_to_all.10.rows_ref = f32[32,392,128]{2,1,0:T(8,128)S(1)} all-to-all(f32[32,392,128]{2,1,0:T(8,128)S(1)} %pick.1), channel_id=1, replica_groups=mesh['grp'=2,'x'=4,'y'=4,'zh'=4,'zl'=2] {'x','y','zl'}, dimensions={0} | all-to-all | bytes 12845056 | tf_op jit(solution)/shard_map/all_to_all | solution.py:322
  111.3 1.7 %far_sum.1 = (f32[32,1536]{1,0:T(8,128)S(1)}, f32[32,1536]{1,0:T(8,128)S(1)}) custom-call(f32[32,392,128]{2,1,0:T(8,128)S(1)} %all_to_all.10.rows_ref), custom_call_target="tpu_custom_call" | custom-call | flops 301989888 | bytes 6291456 | tf_op jit(solution)/shard_map/far_sum/pallas_call | solution.py:241
  113.0 0.7 collective-permute-start.1
  113.6 3.5 %collective-permute-start.4 = (f32[32,1536]{1,0:T(8,128)S(1)}, f32[32,1536]{1,0:T(8,128)S(1)}, u32[]{:S(2)}, u32[]{:S(2)}) collective-permute-start(f32[32,1536]{1,0:T(8,128)S(1)} %get-tuple-element.35), channel_id=1, source_target_pairs={{0,6},{2,0},{4,2},{6,4},{1,7},{3,1},{5,3},{7,5},{8,14},{10,8},{12,... | collective-permute-start | bytes 589832 | tf_op jit(solution)/shard_map/ppermute | solution.py:326
  117.1 2.3 %rest_sum.1 = (f32[32,3072]{1,0:T(8,128)S(1)}, f32[32,1536]{1,0:T(8,128)S(1)}, f32[32,1536]{1,0:T(8,128)S(1)}, f32[32,1536]{1,0:T(8,128)S(1)}, f32[32,1536]{1,0:T(8,128)S(1)}) custom-call(s32[1]{0:T(128)} %bitcast.group_ref, f32[32,392,128]{2,1,0:T(8,128)S(1)} %all_to_all.10.rows_ref, f32[32,128]{1,0:T(8,128)S(1)} %get-tuple-element.29.ident_ref, ...), custom_call_target="tpu_custom_call" | custom-call | flops 905969664 | bytes 6291456 | tf_op jit(solution)/shard_map/rest_sum/pallas_call | solution.py:256
  119.4 0.9 collective-permute-start.3
  120.3 2.1 %collective-permute-start.6 = (f32[32,1536]{1,0:T(8,128)S(1)}, f32[32,1536]{1,0:T(8,128)S(1)}, u32[]{:S(2)}, u32[]{:S(2)}) collective-permute-start(f32[32,1536]{1,0:T(8,128)S(1)} %get-tuple-element.36), channel_id=1, source_target_pairs={{0,2},{2,4},{4,6},{6,0},{1,3},{3,5},{5,7},{7,1},{8,10},{10,12},{12... | collective-permute-start | bytes 589832 | tf_op jit(solution)/shard_map/ppermute | solution.py:328
  122.4 4.0 %collective-permute-done.1 = f32[32,1536]{1,0:T(8,128)S(1)} collective-permute-done((f32[32,1536]{1,0:T(8,128)S(1)}, f32[32,1536]{1,0:T(8,128)S(1)}, u32[]{:S(2)}, u32[]{:S(2)}) %collective-permute-start.1) | collective-permute-done | bytes 196640 | tf_op jit(solution)/shard_map/ppermute | solution.py:326
  126.4 0.1 collective-permute-start.2
  126.5 0.0 collective-permute-done.4
  126.5 4.7 %collective-permute-start.5 = (f32[32,1536]{1,0:T(8,128)S(1)}, f32[32,1536]{1,0:T(8,128)S(1)}, u32[]{:S(2)}, u32[]{:S(2)}) collective-permute-start(f32[32,1536]{1,0:T(8,128)S(1)} %add.164), channel_id=1, source_target_pairs={{0,6},{2,0},{4,2},{6,4},{1,7},{3,1},{5,3},{7,5},{8,14},{10,8},{12,... | collective-permute-start | bytes 589832 | tf_op jit(solution)/shard_map/ppermute | solution.py:330
  131.3 3.2 %collective-permute-done.3.more_left_ref = f32[32,1536]{1,0:T(8,128)S(1)} collective-permute-done((f32[32,1536]{1,0:T(8,128)S(1)}, f32[32,1536]{1,0:T(8,128)S(1)}, u32[]{:S(2)}, u32[]{:S(2)}) %collective-permute-start.3) | collective-permute-done | bytes 196640 | tf_op jit(solution)/shard_map/ppermute | solution.py:328
  134.5 0.0 collective-permute-done.6.more_right_ref
  134.5 4.7 %collective-permute-done.2.left_ref = f32[32,1536]{1,0:T(8,128)S(1)} collective-permute-done((f32[32,1536]{1,0:T(8,128)S(1)}, f32[32,1536]{1,0:T(8,128)S(1)}, u32[]{:S(2)}, u32[]{:S(2)}) %collective-permute-start.2) | collective-permute-done | bytes 196640 | tf_op jit(solution)/shard_map/ppermute | solution.py:329
  139.1 1.2 collective-permute-done.5.right_ref
  140.3 0.8 finish.1
  (2 shorter events, 0.1 us)
Async XLA Ops:
  0.0 28.3 %collective-permute-start = (f32[2,96,6144]{2,1,0:T(8,128)}, f32[2,96,6144]{2,1,0:T(8,128)}, u32[]{:S(2)}, u32[]{:S(2)}) collective-permute-start(f32[2,96,6144]{2,1,0:T(8,128)} %own_ref.1), channel_id=1, source_target_pairs={{0,128},{128,0},{1,129},{129,1},{2,130},{130,2},{3,131},{131,3},{4... | collective-permute-start | bytes 14155784 | tf_op jit(solution)/shard_map/ppermute | solution.py:304
  2.2 26.1 %all-to-all-start = ((f32[128,1,128]{2,1,0:T(1,128)}), f32[128,1,128]{2,1,0:T(1,128)S(1)}, u32[]{:S(2)}, u32[]{:S(2)}) async-start(f32[128,1,128]{2,1,0:T(1,128)} %bitcast.4), calls=%async_computation | async-start | bytes 131072 | tf_op jit(solution)/shard_map/all_to_all | solution.py:308
  113.0 13.4 %collective-permute-start.1 = (f32[32,1536]{1,0:T(8,128)S(1)}, f32[32,1536]{1,0:T(8,128)S(1)}, u32[]{:S(2)}, u32[]{:S(2)}) collective-permute-start(f32[32,1536]{1,0:T(8,128)S(1)} %get-tuple-element.32), channel_id=1, source_target_pairs={{0,2},{2,4},{4,6},{6,0},{1,3},{3,5},{5,7},{7,1},{8,10},{10,12},{12... | collective-permute-start | bytes 589832 | tf_op jit(solution)/shard_map/ppermute | solution.py:326
  113.6 12.9 %collective-permute-start.4 = (f32[32,1536]{1,0:T(8,128)S(1)}, f32[32,1536]{1,0:T(8,128)S(1)}, u32[]{:S(2)}, u32[]{:S(2)}) collective-permute-start(f32[32,1536]{1,0:T(8,128)S(1)} %get-tuple-element.35), channel_id=1, source_target_pairs={{0,6},{2,0},{4,2},{6,4},{1,7},{3,1},{5,3},{7,5},{8,14},{10,8},{12,... | collective-permute-start | bytes 589832 | tf_op jit(solution)/shard_map/ppermute | solution.py:326
  119.4 15.1 %collective-permute-start.3 = (f32[32,1536]{1,0:T(8,128)S(1)}, f32[32,1536]{1,0:T(8,128)S(1)}, u32[]{:S(2)}, u32[]{:S(2)}) collective-permute-start(f32[32,1536]{1,0:T(8,128)S(1)} %get-tuple-element.33), channel_id=1, source_target_pairs={{0,6},{2,0},{4,2},{6,4},{1,7},{3,1},{5,3},{7,5},{8,14},{10,8},{12,... | collective-permute-start | bytes 589832 | tf_op jit(solution)/shard_map/ppermute | solution.py:328
  120.3 14.1 %collective-permute-start.6 = (f32[32,1536]{1,0:T(8,128)S(1)}, f32[32,1536]{1,0:T(8,128)S(1)}, u32[]{:S(2)}, u32[]{:S(2)}) collective-permute-start(f32[32,1536]{1,0:T(8,128)S(1)} %get-tuple-element.36), channel_id=1, source_target_pairs={{0,2},{2,4},{4,6},{6,0},{1,3},{3,5},{5,7},{7,1},{8,10},{10,12},{12... | collective-permute-start | bytes 589832 | tf_op jit(solution)/shard_map/ppermute | solution.py:328
  126.4 12.7 %collective-permute-start.2 = (f32[32,1536]{1,0:T(8,128)S(1)}, f32[32,1536]{1,0:T(8,128)S(1)}, u32[]{:S(2)}, u32[]{:S(2)}) collective-permute-start(f32[32,1536]{1,0:T(8,128)S(1)} %add.163), channel_id=1, source_target_pairs={{0,2},{2,4},{4,6},{6,0},{1,3},{3,5},{5,7},{7,1},{8,10},{10,12},{12... | collective-permute-start | bytes 589832 | tf_op jit(solution)/shard_map/ppermute | solution.py:329
  126.5 13.8 %collective-permute-start.5 = (f32[32,1536]{1,0:T(8,128)S(1)}, f32[32,1536]{1,0:T(8,128)S(1)}, u32[]{:S(2)}, u32[]{:S(2)}) collective-permute-start(f32[32,1536]{1,0:T(8,128)S(1)} %add.164), channel_id=1, source_target_pairs={{0,6},{2,0},{4,2},{6,4},{1,7},{3,1},{5,3},{7,5},{8,14},{10,8},{12,... | collective-permute-start | bytes 589832 | tf_op jit(solution)/shard_map/ppermute | solution.py:330

commit v10 on v8

--- a/solution.py
+++ b/solution.py
@@ -11,6 +11,7 @@
 EP = ("x", "y", "zh", "zl")
 NEAR = ("x", "y", "zl")
 BLOCK = 512
+PICK_BLOCK = 1024
 PICK_VMEM = 24 * 1024 * 1024
 MIX_VMEM = 24 * 1024 * 1024
 
@@ -51,7 +52,9 @@
     both[0:top, :] = ids.astype(jnp.float32)
     both[second : second + top, :] = weights_ref[...]
     columns = both[...].T
-    chip_lines = lax.broadcasted_iota(jnp.int32, (chips, count), 0)
+    together = 128 // count
+    chip_lines = lax.broadcasted_iota(jnp.int32, (chips, 128), 0)
+    values = []
     lanes = lax.broadcasted_iota(jnp.int32, (count, 128), 1)
     token = (lax.broadcasted_iota(jnp.int32, (count, 128), 0) + 1).astype(jnp.float32)
     total = jnp.zeros((chips, 128), jnp.float32)
@@ -65,8 +68,12 @@
         value = jnp.where(lanes == place + gap, high.astype(jnp.float32), value)
         value = jnp.where(lanes == place + 2 * gap, middle.astype(jnp.float32), value)
         value = jnp.where(lanes == place + 3 * gap, low, value)
-        where = (chip_lines == chip[k : k + 1, :]).astype(jnp.float32).astype(jnp.bfloat16)
-        total += mul(where, value.astype(jnp.bfloat16))
+        values.append(value)
+        if len(values) == together:
+            names = jnp.concatenate([chip[j : j + 1, :] for j in range(k + 1 - together, k + 1)], axis=1)
+            where = (chip_lines == names).astype(jnp.float32).astype(jnp.bfloat16)
+            total += mul(where, jnp.concatenate(values, axis=0).astype(jnp.bfloat16))
+            values = []
     ident_ref[...] = jnp.broadcast_to(ident, ident_ref.shape)
     weight = total + pltpu.roll(total, 128 - gap, 1) + pltpu.roll(total, 128 - 2 * gap, 1)
     lanes = lax.broadcasted_iota(jnp.int32, total.shape, 1)
@@ -151,7 +158,7 @@
 def pick(group, chosen, home, lane, own, taken, targets):
     exp_dev, capacity, width = own.shape
     half = width // 2
-    steps = half // BLOCK
+    steps = half // PICK_BLOCK
     count = home.shape[0]
     slots = exp_dev * capacity
     lines = count // targets * half // 128 + count // targets // 2
@@ -163,7 +170,7 @@
         in_specs=[pl.BlockSpec(memory_space=pltpu.SMEM), vmem, vmem, vmem, hbm, hbm],
         out_specs=vmem,
         scratch_shapes=[
-            pltpu.VMEM((2, steps, exp_dev, capacity, BLOCK), jnp.float32),
+            pltpu.VMEM((2, steps, exp_dev, capacity, PICK_BLOCK), jnp.float32),
             pltpu.SemaphoreType.DMA((2, steps)),
         ],
         compiler_params=pltpu.CompilerParams(vmem_limit_bytes=PICK_VMEM),

time: 143 us -> 142 us (level)
    ppermute x1, waiting for transfers between devices: 2.78 us -> 1.3 us  [shards(): lax.ppermute(near_right, 'zh', up)]
  transfers between devices with their start and end apart: 8 -> 8, of which waited for: 5 -> 6; matrix products, arithmetic and copies ran while one was open for 0% -> 0% of each run, Pallas kernels for 3% -> 3%
where the time goes in v10:
time: 142 us
  blocking collectives  78.2 us (55%)
  starting transfers between devices  26.4 us (19%)
  waiting for transfers between devices  25.9 us (18%)
  Pallas kernels  11.2 us (8%)
    all_to_all x1, blocking collectives, shards(): rows = lax.all_to_all(outgoing, NEAR, 0, 0, tiled=True)  78.2 us
    all_to_all x1, starting transfers between devices, shards(): lax.all_to_all(asked[:, None, :], EP, 0, 0, tiled=True)  15 us
    all_to_all x1, waiting for transfers between devices, shards(): lax.all_to_all(asked[:, None, :], EP, 0, 0, tiled=True)  10.7 us
    ppermute x1, waiting for transfers between devices, shards(): lax.ppermute(far_up, 'zh', up)  9.27 us
    ppermute x1, starting transfers between devices, shards(): right = lax.ppermute(prev_right + far_down, 'zh', down)  4.19 us
    pallas_call x1, Pallas kernels, pick(): pl.pallas_call(pick_kernel, out_shape=jax.ShapeDtypeStruct((targets, line...  3.9 us
    ppermute x1, starting transfers between devices, shards(): lax.ppermute(far_down, 'zh', down)  3.51 us
  transfers between devices with their start and end apart: 8, of which 6 were waited for; matrix products, arithmetic and copies ran while one was open for 0% of the time, Pallas kernels for 3%

profile of v10, /device:TPU:32, one launch (start us, length us, event | category | flops | bytes accessed | tf_op | source)
XLA Modules:
  0.0 142.2 jit_solution(6175237441658490992)
XLA Ops:
  0.0 0.0 collective-permute-start
  0.0 2.2 %ask.1 = (f32[128,128]{1,0:T(8,128)}, f32[32,128]{1,0:T(8,128)S(1)}) custom-call(s32[1]{0:T(128)} %bitcast.group_ref, s32[12,32]{1,0:T(8,128)} %bitcast.8, f32[12,32]{1,0:T(8,128)} %bitcast.9), custom_call_target="tpu_custom_call" | custom-call | tf_op jit(solution)/shard_map/ask/pallas_call | solution.py:87
  2.2 15.0 %all-to-all-start = ((f32[128,1,128]{2,1,0:T(1,128)}), f32[128,1,128]{2,1,0:T(1,128)S(1)}, u32[]{:S(2)}, u32[]{:S(2)}) async-start(f32[128,1,128]{2,1,0:T(1,128)} %bitcast.4), calls=%async_computation | async-start | bytes 131072 | tf_op jit(solution)/shard_map/all_to_all | solution.py:309
  17.2 0.4 fusion.8
  17.6 10.7 %all-to-all-done = f32[128,1,128]{2,1,0:T(1,128)S(1)} async-done(((f32[128,1,128]{2,1,0:T(1,128)}), f32[128,1,128]{2,1,0:T(1,128)S(1)}, u32[]{:S(2)}, u32[]{:S(2)}) %all-to-all-start) | async-done | bytes 65568 | tf_op jit(solution)/shard_map/all_to_all | solution.py:309
  28.3 0.0 collective-permute-done.taken_ref
  28.3 3.9 %pick.1 = f32[32,392,128]{2,1,0:T(8,128)S(1)} custom-call(s32[1]{0:T(128)} %bitcast.group_ref, f32[128,128]{1,0:T(8,128)S(1)} %bitcast.7, s32[512,1]{1,0:T(8,128)S(1)} %get-tuple-element.19.home_ref, s32[512,1]{1,0:T(8,128)S(1)} %get-tuple-element.20.lane_ref, f32[2,96,6144]{2,1,0:T(8,128)} %own_ref.1, f32[2,96,6144]{2,1,0:T(8,128)} %collective-permute-done.taken_ref), custom_call_target="tpu_custom_call" | custom-call | flops 1207959552 | bytes 11010048 | tf_op jit(solution)/shard_map/pick/pallas_call | solution.py:167
  32.2 78.2 %all_to_all.10.rows_ref = f32[32,392,128]{2,1,0:T(8,128)S(1)} all-to-all(f32[32,392,128]{2,1,0:T(8,128)S(1)} %pick.1), channel_id=1, replica_groups=mesh['grp'=2,'x'=4,'y'=4,'zh'=4,'zl'=2] {'x','y','zl'}, dimensions={0} | all-to-all | bytes 12845056 | tf_op jit(solution)/shard_map/all_to_all | solution.py:323
  110.4 1.8 %combine.1 = (f32[32,1536]{1,0:T(8,128)S(1)}, f32[32,1536]{1,0:T(8,128)S(1)}, f32[32,1536]{1,0:T(8,128)S(1)}, f32[32,1536]{1,0:T(8,128)S(1)}, f32[32,1536]{1,0:T(8,128)S(1)}, /*index=5*/f32[32,1536]{1,0:T(8,128)S(1)}) custom-call(f32[32,392,128]{2,1,0:T(8,128)S(1)} %all_to_all.10.rows_ref), custom_call_target="tpu_custom_call" | custom-call | flops 905969664 | bytes 6291456 | tf_op jit(solution)/shard_map/combine/pallas_call | solution.py:243
  112.1 0.7 collective-permute-start.1
  112.9 3.5 %collective-permute-start.4 = (f32[32,1536]{1,0:T(8,128)S(1)}, f32[32,1536]{1,0:T(8,128)S(1)}, u32[]{:S(2)}, u32[]{:S(2)}) collective-permute-start(f32[32,1536]{1,0:T(8,128)S(1)} %get-tuple-element.27), channel_id=1, source_target_pairs={{0,6},{2,0},{4,2},{6,4},{1,7},{3,1},{5,3},{7,5},{8,14},{10,8},{12,... | collective-permute-start | bytes 589832 | tf_op jit(solution)/shard_map/ppermute | solution.py:326
  116.4 0.8 collective-permute-start.3
  117.2 2.1 %collective-permute-start.6 = (f32[32,1536]{1,0:T(8,128)S(1)}, f32[32,1536]{1,0:T(8,128)S(1)}, u32[]{:S(2)}, u32[]{:S(2)}) collective-permute-start(f32[32,1536]{1,0:T(8,128)S(1)} %get-tuple-element.28), channel_id=1, source_target_pairs={{0,2},{2,4},{4,6},{6,0},{1,3},{3,5},{5,7},{7,1},{8,10},{10,12},{12... | collective-permute-start | bytes 589832 | tf_op jit(solution)/shard_map/ppermute | solution.py:327
  119.3 9.3 %collective-permute-done.1 = f32[32,1536]{1,0:T(8,128)S(1)} collective-permute-done((f32[32,1536]{1,0:T(8,128)S(1)}, f32[32,1536]{1,0:T(8,128)S(1)}, u32[]{:S(2)}, u32[]{:S(2)}) %collective-permute-start.1) | collective-permute-done | bytes 196640 | tf_op jit(solution)/shard_map/ppermute | solution.py:326
  128.6 0.1 collective-permute-start.2
  128.7 0.0 collective-permute-done.4
  128.7 4.2 %collective-permute-start.5 = (f32[32,1536]{1,0:T(8,128)S(1)}, f32[32,1536]{1,0:T(8,128)S(1)}, u32[]{:S(2)}, u32[]{:S(2)}) collective-permute-start(f32[32,1536]{1,0:T(8,128)S(1)} %add.164), channel_id=1, source_target_pairs={{0,6},{2,0},{4,2},{6,4},{1,7},{3,1},{5,3},{7,5},{8,14},{10,8},{12,... | collective-permute-start | bytes 589832 | tf_op jit(solution)/shard_map/ppermute | solution.py:330
  132.9 2.6 %own_sum.1.base_ref = f32[32,3072]{1,0:T(8,128)S(1)} custom-call(s32[1]{0:T(128)} %bitcast.group_ref, f32[32,392,128]{2,1,0:T(8,128)S(1)} %all_to_all.10.rows_ref, f32[32,128]{1,0:T(8,128)S(1)} %get-tuple-element.22.ident_ref, f32[32,6144]{1,0:T(8,128)} %tokens_ref.1), custom_call_target="tpu_custom_call" | custom-call | flops 301989888 | bytes 6291456 | tf_op jit(solution)/shard_map/own_sum/pallas_call | solution.py:258
  135.5 1.3 collective-permute-done.3.more_left_ref
  136.8 1.3 collective-permute-done.6.more_right_ref
  138.1 2.4 %collective-permute-done.2.left_ref = f32[32,1536]{1,0:T(8,128)S(1)} collective-permute-done((f32[32,1536]{1,0:T(8,128)S(1)}, f32[32,1536]{1,0:T(8,128)S(1)}, u32[]{:S(2)}, u32[]{:S(2)}) %collective-permute-start.2) | collective-permute-done | bytes 196640 | tf_op jit(solution)/shard_map/ppermute | solution.py:329
  140.5 0.9 collective-permute-done.5.right_ref
  141.4 0.8 finish.1
  (2 shorter events, 0.1 us)
Async XLA Ops:
  0.0 28.3 %collective-permute-start = (f32[2,96,6144]{2,1,0:T(8,128)}, f32[2,96,6144]{2,1,0:T(8,128)}, u32[]{:S(2)}, u32[]{:S(2)}) collective-permute-start(f32[2,96,6144]{2,1,0:T(8,128)} %own_ref.1), channel_id=1, source_target_pairs={{0,128},{128,0},{1,129},{129,1},{2,130},{130,2},{3,131},{131,3},{4... | collective-permute-start | bytes 14155784 | tf_op jit(solution)/shard_map/ppermute | solution.py:305
  2.2 26.1 %all-to-all-start = ((f32[128,1,128]{2,1,0:T(1,128)}), f32[128,1,128]{2,1,0:T(1,128)S(1)}, u32[]{:S(2)}, u32[]{:S(2)}) async-start(f32[128,1,128]{2,1,0:T(1,128)} %bitcast.4), calls=%async_computation | async-start | bytes 131072 | tf_op jit(solution)/shard_map/all_to_all | solution.py:309
  112.1 16.4 %collective-permute-start.1 = (f32[32,1536]{1,0:T(8,128)S(1)}, f32[32,1536]{1,0:T(8,128)S(1)}, u32[]{:S(2)}, u32[]{:S(2)}) collective-permute-start(f32[32,1536]{1,0:T(8,128)S(1)} %get-tuple-element.24), channel_id=1, source_target_pairs={{0,2},{2,4},{4,6},{6,0},{1,3},{3,5},{5,7},{7,1},{8,10},{10,12},{12... | collective-permute-start | bytes 589832 | tf_op jit(solution)/shard_map/ppermute | solution.py:326
  112.9 15.8 %collective-permute-start.4 = (f32[32,1536]{1,0:T(8,128)S(1)}, f32[32,1536]{1,0:T(8,128)S(1)}, u32[]{:S(2)}, u32[]{:S(2)}) collective-permute-start(f32[32,1536]{1,0:T(8,128)S(1)} %get-tuple-element.27), channel_id=1, source_target_pairs={{0,6},{2,0},{4,2},{6,4},{1,7},{3,1},{5,3},{7,5},{8,14},{10,8},{12,... | collective-permute-start | bytes 589832 | tf_op jit(solution)/shard_map/ppermute | solution.py:326
  116.4 20.4 %collective-permute-start.3 = (f32[32,1536]{1,0:T(8,128)S(1)}, f32[32,1536]{1,0:T(8,128)S(1)}, u32[]{:S(2)}, u32[]{:S(2)}) collective-permute-start(f32[32,1536]{1,0:T(8,128)S(1)} %get-tuple-element.25), channel_id=1, source_target_pairs={{0,6},{2,0},{4,2},{6,4},{1,7},{3,1},{5,3},{7,5},{8,14},{10,8},{12,... | collective-permute-start | bytes 589832 | tf_op jit(solution)/shard_map/ppermute | solution.py:327
  117.2 20.9 %collective-permute-start.6 = (f32[32,1536]{1,0:T(8,128)S(1)}, f32[32,1536]{1,0:T(8,128)S(1)}, u32[]{:S(2)}, u32[]{:S(2)}) collective-permute-start(f32[32,1536]{1,0:T(8,128)S(1)} %get-tuple-element.28), channel_id=1, source_target_pairs={{0,2},{2,4},{4,6},{6,0},{1,3},{3,5},{5,7},{7,1},{8,10},{10,12},{12... | collective-permute-start | bytes 589832 | tf_op jit(solution)/shard_map/ppermute | solution.py:327
  128.6 11.9 %collective-permute-start.2 = (f32[32,1536]{1,0:T(8,128)S(1)}, f32[32,1536]{1,0:T(8,128)S(1)}, u32[]{:S(2)}, u32[]{:S(2)}) collective-permute-start(f32[32,1536]{1,0:T(8,128)S(1)} %add.163), channel_id=1, source_target_pairs={{0,2},{2,4},{4,6},{6,0},{1,3},{3,5},{5,7},{7,1},{8,10},{10,12},{12... | collective-permute-start | bytes 589832 | tf_op jit(solution)/shard_map/ppermute | solution.py:329
  128.7 12.7 %collective-permute-start.5 = (f32[32,1536]{1,0:T(8,128)S(1)}, f32[32,1536]{1,0:T(8,128)S(1)}, u32[]{:S(2)}, u32[]{:S(2)}) collective-permute-start(f32[32,1536]{1,0:T(8,128)S(1)} %add.164), channel_id=1, source_target_pairs={{0,6},{2,0},{4,2},{6,4},{1,7},{3,1},{5,3},{7,5},{8,14},{10,8},{12,... | collective-permute-start | bytes 589832 | tf_op jit(solution)/shard_map/ppermute | solution.py:330

commit v11 on v10

--- a/solution.py
+++ b/solution.py
@@ -10,8 +10,8 @@
 
 EP = ("x", "y", "zh", "zl")
 NEAR = ("x", "y", "zl")
-BLOCK = 512
-PICK_BLOCK = 1024
+BLOCK = 768
+PICK_BLOCK = 1536
 PICK_VMEM = 24 * 1024 * 1024
 MIX_VMEM = 24 * 1024 * 1024
 

time: 142 us -> 142 us (level)
  no operation moved by 1% of the time
where the time goes in v11:
time: 142 us
  blocking collectives  78.1 us (55%)
  starting transfers between devices  26.4 us (19%)
  waiting for transfers between devices  25.8 us (18%)
  Pallas kernels  10.9 us (8%)
    all_to_all x1, blocking collectives, shards(): rows = lax.all_to_all(outgoing, NEAR, 0, 0, tiled=True)  78.1 us
    all_to_all x1, starting transfers between devices, shards(): lax.all_to_all(asked[:, None, :], EP, 0, 0, tiled=True)  15 us
    all_to_all x1, waiting for transfers between devices, shards(): lax.all_to_all(asked[:, None, :], EP, 0, 0, tiled=True)  10.7 us
    ppermute x1, waiting for transfers between devices, shards(): lax.ppermute(far_up, 'zh', up)  9.09 us
    ppermute x1, starting transfers between devices, shards(): right = lax.ppermute(prev_right + far_down, 'zh', down)  4.19 us
    pallas_call x1, Pallas kernels, pick(): pl.pallas_call(pick_kernel, out_shape=jax.ShapeDtypeStruct((targets, line...  3.69 us
    ppermute x1, starting transfers between devices, shards(): lax.ppermute(far_down, 'zh', down)  3.51 us
  transfers between devices with their start and end apart: 8, of which 6 were waited for; matrix products, arithmetic and copies ran while one was open for 0% of the time, Pallas kernels for 3%

profile of v11, /device:TPU:32, one launch (start us, length us, event | category | flops | bytes accessed | tf_op | source)
XLA Modules:
  0.0 141.8 jit_solution(17005033302846468405)
XLA Ops:
  0.0 0.0 collective-permute-start
  0.0 2.2 %ask.1 = (f32[128,128]{1,0:T(8,128)}, f32[32,128]{1,0:T(8,128)S(1)}) custom-call(s32[1]{0:T(128)} %bitcast.group_ref, s32[12,32]{1,0:T(8,128)} %bitcast.8, f32[12,32]{1,0:T(8,128)} %bitcast.9), custom_call_target="tpu_custom_call" | custom-call | tf_op jit(solution)/shard_map/ask/pallas_call | solution.py:87
  2.2 15.0 %all-to-all-start = ((f32[128,1,128]{2,1,0:T(1,128)}), f32[128,1,128]{2,1,0:T(1,128)S(1)}, u32[]{:S(2)}, u32[]{:S(2)}) async-start(f32[128,1,128]{2,1,0:T(1,128)} %bitcast.4), calls=%async_computation | async-start | bytes 131072 | tf_op jit(solution)/shard_map/all_to_all | solution.py:309
  17.2 0.4 fusion.8
  17.6 10.7 %all-to-all-done = f32[128,1,128]{2,1,0:T(1,128)S(1)} async-done(((f32[128,1,128]{2,1,0:T(1,128)}), f32[128,1,128]{2,1,0:T(1,128)S(1)}, u32[]{:S(2)}, u32[]{:S(2)}) %all-to-all-start) | async-done | bytes 65568 | tf_op jit(solution)/shard_map/all_to_all | solution.py:309
  28.3 0.0 collective-permute-done.taken_ref
  28.3 3.7 %pick.1 = f32[32,392,128]{2,1,0:T(8,128)S(1)} custom-call(s32[1]{0:T(128)} %bitcast.group_ref, f32[128,128]{1,0:T(8,128)S(1)} %bitcast.7, s32[512,1]{1,0:T(8,128)S(1)} %get-tuple-element.19.home_ref, s32[512,1]{1,0:T(8,128)S(1)} %get-tuple-element.20.lane_ref, f32[2,96,6144]{2,1,0:T(8,128)} %own_ref.1, f32[2,96,6144]{2,1,0:T(8,128)} %collective-permute-done.taken_ref), custom_call_target="tpu_custom_call" | custom-call | flops 1207959552 | bytes 11010048 | tf_op jit(solution)/shard_map/pick/pallas_call | solution.py:167
  32.0 78.1 %all_to_all.10.rows_ref = f32[32,392,128]{2,1,0:T(8,128)S(1)} all-to-all(f32[32,392,128]{2,1,0:T(8,128)S(1)} %pick.1), channel_id=1, replica_groups=mesh['grp'=2,'x'=4,'y'=4,'zh'=4,'zl'=2] {'x','y','zl'}, dimensions={0} | all-to-all | bytes 12845056 | tf_op jit(solution)/shard_map/all_to_all | solution.py:323
  110.2 1.7 %combine.1 = (f32[32,1536]{1,0:T(8,128)S(1)}, f32[32,1536]{1,0:T(8,128)S(1)}, f32[32,1536]{1,0:T(8,128)S(1)}, f32[32,1536]{1,0:T(8,128)S(1)}, f32[32,1536]{1,0:T(8,128)S(1)}, /*index=5*/f32[32,1536]{1,0:T(8,128)S(1)}) custom-call(f32[32,392,128]{2,1,0:T(8,128)S(1)} %all_to_all.10.rows_ref), custom_call_target="tpu_custom_call" | custom-call | flops 905969664 | bytes 6291456 | tf_op jit(solution)/shard_map/combine/pallas_call | solution.py:243
  111.8 0.7 collective-permute-start.1
  112.5 3.5 %collective-permute-start.4 = (f32[32,1536]{1,0:T(8,128)S(1)}, f32[32,1536]{1,0:T(8,128)S(1)}, u32[]{:S(2)}, u32[]{:S(2)}) collective-permute-start(f32[32,1536]{1,0:T(8,128)S(1)} %get-tuple-element.27), channel_id=1, source_target_pairs={{0,6},{2,0},{4,2},{6,4},{1,7},{3,1},{5,3},{7,5},{8,14},{10,8},{12,... | collective-permute-start | bytes 589832 | tf_op jit(solution)/shard_map/ppermute | solution.py:326
  116.0 0.8 collective-permute-start.3
  116.8 2.1 %collective-permute-start.6 = (f32[32,1536]{1,0:T(8,128)S(1)}, f32[32,1536]{1,0:T(8,128)S(1)}, u32[]{:S(2)}, u32[]{:S(2)}) collective-permute-start(f32[32,1536]{1,0:T(8,128)S(1)} %get-tuple-element.28), channel_id=1, source_target_pairs={{0,2},{2,4},{4,6},{6,0},{1,3},{3,5},{5,7},{7,1},{8,10},{10,12},{12... | collective-permute-start | bytes 589832 | tf_op jit(solution)/shard_map/ppermute | solution.py:327
  118.9 9.1 %collective-permute-done.1 = f32[32,1536]{1,0:T(8,128)S(1)} collective-permute-done((f32[32,1536]{1,0:T(8,128)S(1)}, f32[32,1536]{1,0:T(8,128)S(1)}, u32[]{:S(2)}, u32[]{:S(2)}) %collective-permute-start.1) | collective-permute-done | bytes 196640 | tf_op jit(solution)/shard_map/ppermute | solution.py:326
  128.1 0.1 collective-permute-start.2
  128.2 0.0 collective-permute-done.4
  128.2 4.2 %collective-permute-start.5 = (f32[32,1536]{1,0:T(8,128)S(1)}, f32[32,1536]{1,0:T(8,128)S(1)}, u32[]{:S(2)}, u32[]{:S(2)}) collective-permute-start(f32[32,1536]{1,0:T(8,128)S(1)} %add.164), channel_id=1, source_target_pairs={{0,6},{2,0},{4,2},{6,4},{1,7},{3,1},{5,3},{7,5},{8,14},{10,8},{12,... | collective-permute-start | bytes 589832 | tf_op jit(solution)/shard_map/ppermute | solution.py:330
  132.4 2.5 %own_sum.1.base_ref = f32[32,3072]{1,0:T(8,128)S(1)} custom-call(s32[1]{0:T(128)} %bitcast.group_ref, f32[32,392,128]{2,1,0:T(8,128)S(1)} %all_to_all.10.rows_ref, f32[32,128]{1,0:T(8,128)S(1)} %get-tuple-element.22.ident_ref, f32[32,6144]{1,0:T(8,128)} %tokens_ref.1), custom_call_target="tpu_custom_call" | custom-call | flops 301989888 | bytes 6291456 | tf_op jit(solution)/shard_map/own_sum/pallas_call | solution.py:258
  134.9 1.6 %collective-permute-done.3.more_left_ref = f32[32,1536]{1,0:T(8,128)S(1)} collective-permute-done((f32[32,1536]{1,0:T(8,128)S(1)}, f32[32,1536]{1,0:T(8,128)S(1)}, u32[]{:S(2)}, u32[]{:S(2)}) %collective-permute-start.3) | collective-permute-done | bytes 196640 | tf_op jit(solution)/shard_map/ppermute | solution.py:327
  136.5 1.3 collective-permute-done.6.more_right_ref
  137.8 2.4 %collective-permute-done.2.left_ref = f32[32,1536]{1,0:T(8,128)S(1)} collective-permute-done((f32[32,1536]{1,0:T(8,128)S(1)}, f32[32,1536]{1,0:T(8,128)S(1)}, u32[]{:S(2)}, u32[]{:S(2)}) %collective-permute-start.2) | collective-permute-done | bytes 196640 | tf_op jit(solution)/shard_map/ppermute | solution.py:329
  140.1 0.8 collective-permute-done.5.right_ref
  140.9 0.8 finish.1
  (2 shorter events, 0.1 us)
Async XLA Ops:
  0.0 28.3 %collective-permute-start = (f32[2,96,6144]{2,1,0:T(8,128)}, f32[2,96,6144]{2,1,0:T(8,128)}, u32[]{:S(2)}, u32[]{:S(2)}) collective-permute-start(f32[2,96,6144]{2,1,0:T(8,128)} %own_ref.1), channel_id=1, source_target_pairs={{0,128},{128,0},{1,129},{129,1},{2,130},{130,2},{3,131},{131,3},{4... | collective-permute-start | bytes 14155784 | tf_op jit(solution)/shard_map/ppermute | solution.py:305
  2.2 26.1 %all-to-all-start = ((f32[128,1,128]{2,1,0:T(1,128)}), f32[128,1,128]{2,1,0:T(1,128)S(1)}, u32[]{:S(2)}, u32[]{:S(2)}) async-start(f32[128,1,128]{2,1,0:T(1,128)} %bitcast.4), calls=%async_computation | async-start | bytes 131072 | tf_op jit(solution)/shard_map/all_to_all | solution.py:309
  111.8 16.2 %collective-permute-start.1 = (f32[32,1536]{1,0:T(8,128)S(1)}, f32[32,1536]{1,0:T(8,128)S(1)}, u32[]{:S(2)}, u32[]{:S(2)}) collective-permute-start(f32[32,1536]{1,0:T(8,128)S(1)} %get-tuple-element.24), channel_id=1, source_target_pairs={{0,2},{2,4},{4,6},{6,0},{1,3},{3,5},{5,7},{7,1},{8,10},{10,12},{12... | collective-permute-start | bytes 589832 | tf_op jit(solution)/shard_map/ppermute | solution.py:326
  112.5 15.6 %collective-permute-start.4 = (f32[32,1536]{1,0:T(8,128)S(1)}, f32[32,1536]{1,0:T(8,128)S(1)}, u32[]{:S(2)}, u32[]{:S(2)}) collective-permute-start(f32[32,1536]{1,0:T(8,128)S(1)} %get-tuple-element.27), channel_id=1, source_target_pairs={{0,6},{2,0},{4,2},{6,4},{1,7},{3,1},{5,3},{7,5},{8,14},{10,8},{12,... | collective-permute-start | bytes 589832 | tf_op jit(solution)/shard_map/ppermute | solution.py:326
  116.0 20.5 %collective-permute-start.3 = (f32[32,1536]{1,0:T(8,128)S(1)}, f32[32,1536]{1,0:T(8,128)S(1)}, u32[]{:S(2)}, u32[]{:S(2)}) collective-permute-start(f32[32,1536]{1,0:T(8,128)S(1)} %get-tuple-element.25), channel_id=1, source_target_pairs={{0,6},{2,0},{4,2},{6,4},{1,7},{3,1},{5,3},{7,5},{8,14},{10,8},{12,... | collective-permute-start | bytes 589832 | tf_op jit(solution)/shard_map/ppermute | solution.py:327
  116.8 21.0 %collective-permute-start.6 = (f32[32,1536]{1,0:T(8,128)S(1)}, f32[32,1536]{1,0:T(8,128)S(1)}, u32[]{:S(2)}, u32[]{:S(2)}) collective-permute-start(f32[32,1536]{1,0:T(8,128)S(1)} %get-tuple-element.28), channel_id=1, source_target_pairs={{0,2},{2,4},{4,6},{6,0},{1,3},{3,5},{5,7},{7,1},{8,10},{10,12},{12... | collective-permute-start | bytes 589832 | tf_op jit(solution)/shard_map/ppermute | solution.py:327
  128.1 12.1 %collective-permute-start.2 = (f32[32,1536]{1,0:T(8,128)S(1)}, f32[32,1536]{1,0:T(8,128)S(1)}, u32[]{:S(2)}, u32[]{:S(2)}) collective-permute-start(f32[32,1536]{1,0:T(8,128)S(1)} %add.163), channel_id=1, source_target_pairs={{0,2},{2,4},{4,6},{6,0},{1,3},{3,5},{5,7},{7,1},{8,10},{10,12},{12... | collective-permute-start | bytes 589832 | tf_op jit(solution)/shard_map/ppermute | solution.py:329
  128.2 12.7 %collective-permute-start.5 = (f32[32,1536]{1,0:T(8,128)S(1)}, f32[32,1536]{1,0:T(8,128)S(1)}, u32[]{:S(2)}, u32[]{:S(2)}) collective-permute-start(f32[32,1536]{1,0:T(8,128)S(1)} %add.164), channel_id=1, source_target_pairs={{0,6},{2,0},{4,2},{6,4},{1,7},{3,1},{5,3},{7,5},{8,14},{10,8},{12,... | collective-permute-start | bytes 589832 | tf_op jit(solution)/shard_map/ppermute | solution.py:330

commit v12 on v11

--- a/solution.py
+++ b/solution.py
@@ -10,7 +10,7 @@
 
 EP = ("x", "y", "zh", "zl")
 NEAR = ("x", "y", "zl")
-BLOCK = 768
+BLOCK = 1536
 PICK_BLOCK = 1536
 PICK_VMEM = 24 * 1024 * 1024
 MIX_VMEM = 24 * 1024 * 1024

time: 142 us -> 142 us (level)
  no operation moved by 1% of the time
where the time goes in v12:
time: 142 us
  blocking collectives  78.1 us (55%)
  starting transfers between devices  26.4 us (19%)
  waiting for transfers between devices  25.6 us (18%)
  Pallas kernels  11.2 us (8%)
    all_to_all x1, blocking collectives, shards(): rows = lax.all_to_all(outgoing, NEAR, 0, 0, tiled=True)  78.1 us
    all_to_all x1, starting transfers between devices, shards(): lax.all_to_all(asked[:, None, :], EP, 0, 0, tiled=True)  15 us
    all_to_all x1, waiting for transfers between devices, shards(): lax.all_to_all(asked[:, None, :], EP, 0, 0, tiled=True)  10.7 us
    ppermute x1, waiting for transfers between devices, shards(): lax.ppermute(far_up, 'zh', up)  9.08 us
    ppermute x1, starting transfers between devices, shards(): right = lax.ppermute(prev_right + far_down, 'zh', down)  4.19 us
    pallas_call x1, Pallas kernels, pick(): pl.pallas_call(pick_kernel, out_shape=jax.ShapeDtypeStruct((targets, line...  3.69 us
    ppermute x1, starting transfers between devices, shards(): lax.ppermute(far_down, 'zh', down)  3.51 us
  transfers between devices with their start and end apart: 8, of which 6 were waited for; matrix products, arithmetic and copies ran while one was open for 0% of the time, Pallas kernels for 3%

profile of v12, /device:TPU:32, one launch (start us, length us, event | category | flops | bytes accessed | tf_op | source)
XLA Modules:
  0.0 141.9 jit_solution(14300983373328830241)
XLA Ops:
  0.0 0.0 collective-permute-start
  0.0 2.2 %ask.1 = (f32[128,128]{1,0:T(8,128)}, f32[32,128]{1,0:T(8,128)S(1)}) custom-call(s32[1]{0:T(128)} %bitcast.group_ref, s32[12,32]{1,0:T(8,128)} %bitcast.8, f32[12,32]{1,0:T(8,128)} %bitcast.9), custom_call_target="tpu_custom_call" | custom-call | tf_op jit(solution)/shard_map/ask/pallas_call | solution.py:87
  2.2 15.0 %all-to-all-start = ((f32[128,1,128]{2,1,0:T(1,128)}), f32[128,1,128]{2,1,0:T(1,128)S(1)}, u32[]{:S(2)}, u32[]{:S(2)}) async-start(f32[128,1,128]{2,1,0:T(1,128)} %bitcast.4), calls=%async_computation | async-start | bytes 131072 | tf_op jit(solution)/shard_map/all_to_all | solution.py:309
  17.2 0.4 fusion.8
  17.6 10.7 %all-to-all-done = f32[128,1,128]{2,1,0:T(1,128)S(1)} async-done(((f32[128,1,128]{2,1,0:T(1,128)}), f32[128,1,128]{2,1,0:T(1,128)S(1)}, u32[]{:S(2)}, u32[]{:S(2)}) %all-to-all-start) | async-done | bytes 65568 | tf_op jit(solution)/shard_map/all_to_all | solution.py:309
  28.3 0.0 collective-permute-done.taken_ref
  28.3 3.7 %pick.1 = f32[32,392,128]{2,1,0:T(8,128)S(1)} custom-call(s32[1]{0:T(128)} %bitcast.group_ref, f32[128,128]{1,0:T(8,128)S(1)} %bitcast.7, s32[512,1]{1,0:T(8,128)S(1)} %get-tuple-element.19.home_ref, s32[512,1]{1,0:T(8,128)S(1)} %get-tuple-element.20.lane_ref, f32[2,96,6144]{2,1,0:T(8,128)} %own_ref.1, f32[2,96,6144]{2,1,0:T(8,128)} %collective-permute-done.taken_ref), custom_call_target="tpu_custom_call" | custom-call | flops 1207959552 | bytes 11010048 | tf_op jit(solution)/shard_map/pick/pallas_call | solution.py:167
  32.0 78.1 %all_to_all.10.rows_ref = f32[32,392,128]{2,1,0:T(8,128)S(1)} all-to-all(f32[32,392,128]{2,1,0:T(8,128)S(1)} %pick.1), channel_id=1, replica_groups=mesh['grp'=2,'x'=4,'y'=4,'zh'=4,'zl'=2] {'x','y','zl'}, dimensions={0} | all-to-all | bytes 12845056 | tf_op jit(solution)/shard_map/all_to_all | solution.py:323
  110.2 1.9 %combine.1 = (f32[32,1536]{1,0:T(8,128)S(1)}, f32[32,1536]{1,0:T(8,128)S(1)}, f32[32,1536]{1,0:T(8,128)S(1)}, f32[32,1536]{1,0:T(8,128)S(1)}, f32[32,1536]{1,0:T(8,128)S(1)}, /*index=5*/f32[32,1536]{1,0:T(8,128)S(1)}) custom-call(f32[32,392,128]{2,1,0:T(8,128)S(1)} %all_to_all.10.rows_ref), custom_call_target="tpu_custom_call" | custom-call | flops 905969664 | bytes 6291456 | tf_op jit(solution)/shard_map/combine/pallas_call | solution.py:243
  112.0 0.7 collective-permute-start.1
  112.7 3.5 %collective-permute-start.4 = (f32[32,1536]{1,0:T(8,128)S(1)}, f32[32,1536]{1,0:T(8,128)S(1)}, u32[]{:S(2)}, u32[]{:S(2)}) collective-permute-start(f32[32,1536]{1,0:T(8,128)S(1)} %get-tuple-element.27), channel_id=1, source_target_pairs={{0,6},{2,0},{4,2},{6,4},{1,7},{3,1},{5,3},{7,5},{8,14},{10,8},{12,... | collective-permute-start | bytes 589832 | tf_op jit(solution)/shard_map/ppermute | solution.py:326
  116.2 0.8 collective-permute-start.3
  117.0 2.1 %collective-permute-start.6 = (f32[32,1536]{1,0:T(8,128)S(1)}, f32[32,1536]{1,0:T(8,128)S(1)}, u32[]{:S(2)}, u32[]{:S(2)}) collective-permute-start(f32[32,1536]{1,0:T(8,128)S(1)} %get-tuple-element.28), channel_id=1, source_target_pairs={{0,2},{2,4},{4,6},{6,0},{1,3},{3,5},{5,7},{7,1},{8,10},{10,12},{12... | collective-permute-start | bytes 589832 | tf_op jit(solution)/shard_map/ppermute | solution.py:327
  119.1 9.1 %collective-permute-done.1 = f32[32,1536]{1,0:T(8,128)S(1)} collective-permute-done((f32[32,1536]{1,0:T(8,128)S(1)}, f32[32,1536]{1,0:T(8,128)S(1)}, u32[]{:S(2)}, u32[]{:S(2)}) %collective-permute-start.1) | collective-permute-done | bytes 196640 | tf_op jit(solution)/shard_map/ppermute | solution.py:326
  128.3 0.1 collective-permute-start.2
  128.3 0.0 collective-permute-done.4
  128.4 4.2 %collective-permute-start.5 = (f32[32,1536]{1,0:T(8,128)S(1)}, f32[32,1536]{1,0:T(8,128)S(1)}, u32[]{:S(2)}, u32[]{:S(2)}) collective-permute-start(f32[32,1536]{1,0:T(8,128)S(1)} %add.164), channel_id=1, source_target_pairs={{0,6},{2,0},{4,2},{6,4},{1,7},{3,1},{5,3},{7,5},{8,14},{10,8},{12,... | collective-permute-start | bytes 589832 | tf_op jit(solution)/shard_map/ppermute | solution.py:330
  132.6 2.7 %own_sum.1.base_ref = f32[32,3072]{1,0:T(8,128)S(1)} custom-call(s32[1]{0:T(128)} %bitcast.group_ref, f32[32,392,128]{2,1,0:T(8,128)S(1)} %all_to_all.10.rows_ref, f32[32,128]{1,0:T(8,128)S(1)} %get-tuple-element.22.ident_ref, f32[32,6144]{1,0:T(8,128)} %tokens_ref.1), custom_call_target="tpu_custom_call" | custom-call | flops 301989888 | bytes 6291456 | tf_op jit(solution)/shard_map/own_sum/pallas_call | solution.py:258
  135.3 1.5 %collective-permute-done.3.more_left_ref = f32[32,1536]{1,0:T(8,128)S(1)} collective-permute-done((f32[32,1536]{1,0:T(8,128)S(1)}, f32[32,1536]{1,0:T(8,128)S(1)}, u32[]{:S(2)}, u32[]{:S(2)}) %collective-permute-start.3) | collective-permute-done | bytes 196640 | tf_op jit(solution)/shard_map/ppermute | solution.py:327
  136.8 1.2 collective-permute-done.6.more_right_ref
  138.0 2.4 %collective-permute-done.2.left_ref = f32[32,1536]{1,0:T(8,128)S(1)} collective-permute-done((f32[32,1536]{1,0:T(8,128)S(1)}, f32[32,1536]{1,0:T(8,128)S(1)}, u32[]{:S(2)}, u32[]{:S(2)}) %collective-permute-start.2) | collective-permute-done | bytes 196640 | tf_op jit(solution)/shard_map/ppermute | solution.py:329
  140.4 0.8 collective-permute-done.5.right_ref
  141.1 0.8 finish.1
  (2 shorter events, 0.1 us)
Async XLA Ops:
  0.0 28.3 %collective-permute-start = (f32[2,96,6144]{2,1,0:T(8,128)}, f32[2,96,6144]{2,1,0:T(8,128)}, u32[]{:S(2)}, u32[]{:S(2)}) collective-permute-start(f32[2,96,6144]{2,1,0:T(8,128)} %own_ref.1), channel_id=1, source_target_pairs={{0,128},{128,0},{1,129},{129,1},{2,130},{130,2},{3,131},{131,3},{4... | collective-permute-start | bytes 14155784 | tf_op jit(solution)/shard_map/ppermute | solution.py:305
  2.2 26.1 %all-to-all-start = ((f32[128,1,128]{2,1,0:T(1,128)}), f32[128,1,128]{2,1,0:T(1,128)S(1)}, u32[]{:S(2)}, u32[]{:S(2)}) async-start(f32[128,1,128]{2,1,0:T(1,128)} %bitcast.4), calls=%async_computation | async-start | bytes 131072 | tf_op jit(solution)/shard_map/all_to_all | solution.py:309
  112.0 16.2 %collective-permute-start.1 = (f32[32,1536]{1,0:T(8,128)S(1)}, f32[32,1536]{1,0:T(8,128)S(1)}, u32[]{:S(2)}, u32[]{:S(2)}) collective-permute-start(f32[32,1536]{1,0:T(8,128)S(1)} %get-tuple-element.24), channel_id=1, source_target_pairs={{0,2},{2,4},{4,6},{6,0},{1,3},{3,5},{5,7},{7,1},{8,10},{10,12},{12... | collective-permute-start | bytes 589832 | tf_op jit(solution)/shard_map/ppermute | solution.py:326
  112.7 15.6 %collective-permute-start.4 = (f32[32,1536]{1,0:T(8,128)S(1)}, f32[32,1536]{1,0:T(8,128)S(1)}, u32[]{:S(2)}, u32[]{:S(2)}) collective-permute-start(f32[32,1536]{1,0:T(8,128)S(1)} %get-tuple-element.27), channel_id=1, source_target_pairs={{0,6},{2,0},{4,2},{6,4},{1,7},{3,1},{5,3},{7,5},{8,14},{10,8},{12,... | collective-permute-start | bytes 589832 | tf_op jit(solution)/shard_map/ppermute | solution.py:326
  116.2 20.6 %collective-permute-start.3 = (f32[32,1536]{1,0:T(8,128)S(1)}, f32[32,1536]{1,0:T(8,128)S(1)}, u32[]{:S(2)}, u32[]{:S(2)}) collective-permute-start(f32[32,1536]{1,0:T(8,128)S(1)} %get-tuple-element.25), channel_id=1, source_target_pairs={{0,6},{2,0},{4,2},{6,4},{1,7},{3,1},{5,3},{7,5},{8,14},{10,8},{12,... | collective-permute-start | bytes 589832 | tf_op jit(solution)/shard_map/ppermute | solution.py:327
  117.0 21.0 %collective-permute-start.6 = (f32[32,1536]{1,0:T(8,128)S(1)}, f32[32,1536]{1,0:T(8,128)S(1)}, u32[]{:S(2)}, u32[]{:S(2)}) collective-permute-start(f32[32,1536]{1,0:T(8,128)S(1)} %get-tuple-element.28), channel_id=1, source_target_pairs={{0,2},{2,4},{4,6},{6,0},{1,3},{3,5},{5,7},{7,1},{8,10},{10,12},{12... | collective-permute-start | bytes 589832 | tf_op jit(solution)/shard_map/ppermute | solution.py:327
  128.3 12.1 %collective-permute-start.2 = (f32[32,1536]{1,0:T(8,128)S(1)}, f32[32,1536]{1,0:T(8,128)S(1)}, u32[]{:S(2)}, u32[]{:S(2)}) collective-permute-start(f32[32,1536]{1,0:T(8,128)S(1)} %add.163), channel_id=1, source_target_pairs={{0,2},{2,4},{4,6},{6,0},{1,3},{3,5},{5,7},{7,1},{8,10},{10,12},{12... | collective-permute-start | bytes 589832 | tf_op jit(solution)/shard_map/ppermute | solution.py:329
  128.4 12.7 %collective-permute-start.5 = (f32[32,1536]{1,0:T(8,128)S(1)}, f32[32,1536]{1,0:T(8,128)S(1)}, u32[]{:S(2)}, u32[]{:S(2)}) collective-permute-start(f32[32,1536]{1,0:T(8,128)S(1)} %add.164), channel_id=1, source_target_pairs={{0,6},{2,0},{4,2},{6,4},{1,7},{3,1},{5,3},{7,5},{8,14},{10,8},{12,... | collective-permute-start | bytes 589832 | tf_op jit(solution)/shard_map/ppermute | solution.py:330
